TPU v7x, 128 devices: a whole 4x4x4 slice. The times are simulated.
128 devices in a mesh: seq: 16 (over y, z), head: 8 (over x, core).
Axes of the slice: x: 4, y: 4, z: 4, core: 2. Of those that a mesh axis runs over, the one named last changes fastest.
Arguments:
- pre_x: bfloat16 [16384, 5120], P('seq', 'head'), may hold values from -6 to 6
- pre_bc: bfloat16 [16384, 256], P('seq'), may hold values from -6 to 6
- gate_z: bfloat16 [16384, 5120], P('seq', 'head'), may hold values from -6 to 6
- dt_raw: float32 [80, 16384], P('head', 'seq'), may hold values from -3 to 3
- conv_x: float32 [4, 5120], P(None, 'head'), may hold values from -3 to 3
- conv_bc: float32 [4, 256], replicated, may hold values from -3 to 3
- head_params: float32 [3, 80], P(None, 'head'), may hold values from -12 to 2, as said below
- norm_gain: float32 [5120], P('head'), may hold values from 0.5 to 1.5
- w_out: bfloat16 [5120, 2560], P('head'), may hold values from -0.078125 to 0.078125
- t_conv_x: float32 [4, 5120], P(None, 'head'), may hold values from -3 to 3
- t_conv_bc: float32 [4, 256], replicated, may hold values from -3 to 3
- t_heads: float32 [3, 80], P(None, 'head'), may hold values from -3 to 3
- t_gain: float32 [5120], P('head'), may hold values from -1 to 1
- t_wout: bfloat16 [5120, 2560], P('head', 'seq'), may hold values from -0.078125 to 0.078125
Outputs:
- gn_conv_x: float32 [4, 5120], P(None, 'head')
- gn_conv_bc: float32 [4, 256], replicated
- gn_heads: float32 [3, 80], P(None, 'head')
- gn_gain: float32 [5120], P('head')
- gn_wout: float32 [5120, 2560], P('head', 'seq')
Inputs may be any that keep to these rules, and one draw needn't show every extreme that they name: `head_params`: row 0 is a step bias per head, row 1 a log decay rate per head, row 2 a skip gain per head.
All inputs are finite; a program needn't handle non-finite values.
Results may differ from a plain program's by a relative error of at most 0.00041.
Values may be sent and summed in bfloat16 or wider, within the bound.
A program may use at most 192 MiB of HBM per device.

v0:
```python
from functools import partial

import jax
import jax.numpy as jnp
from jax import lax
from jax.sharding import PartitionSpec as P

NH = 80
P_SIZE = 64
BLOCK = 256


def shifted(value, axis, steps):
    count = lax.axis_size(axis)
    leading, last = (max(0, -steps), min(count, count - steps))
    return lax.ppermute(value, axis, [(source, source + steps) for source in range(leading, last)])


def carried_in(value, axis, join, neutral, backward):
    count, mine = (lax.axis_size(axis), lax.axis_index(axis))
    pieces = jax.tree.map(lambda part: lax.all_gather(part, axis), value)
    if backward:
        pieces = jax.tree.map(lambda part: part[::-1], pieces)
        mine = count - 1 - mine
    so_far = jax.tree.map(
        lambda part, zero: jnp.full_like(part, 0) + jnp.asarray(zero, part.dtype), value, neutral
    )

    def step(position, so_far):
        longer = join(so_far, jax.tree.map(lambda part: part[position], pieces))
        return jax.tree.map(lambda new, old: jnp.where(position < mine, new, old), longer, so_far)

    return lax.fori_loop(0, count - 1, step, so_far)


def conv_silu(padded, weight):
    width = weight.shape[0]
    length = padded.shape[0] - width + 1
    total = jnp.zeros((length, padded.shape[1]), jnp.float32)
    for offset in range(width):
        total = total + weight[offset][None, :] * padded[offset : offset + length].astype(
            jnp.float32
        )
    return jax.nn.silu(total)


def block_step(state, pieces):
    x_block, b_block, c_block, step_block, decay_rate = pieces
    high = lax.Precision.HIGHEST
    length = b_block.shape[0]
    log_decay = -step_block * decay_rate[:, None]
    cumul = jnp.cumsum(log_decay, axis=1)
    lower_mask = jnp.arange(length)[:, None] >= jnp.arange(length)[None, :]
    diffs = cumul[:, :, None] - cumul[:, None, :]
    weights_in = jnp.where(lower_mask[None], jnp.exp(jnp.where(lower_mask[None], diffs, 0.0)), 0.0)
    inner = jnp.dot(c_block, b_block.T, precision=high)
    weights_in = inner[None] * weights_in * step_block[:, None, :]
    y_inner = jnp.einsum("hij,jhp->ihp", weights_in, x_block, precision=high)
    y_carry = jnp.exp(cumul).T[:, :, None] * jnp.einsum(
        "in,hpn->ihp", c_block, state, precision=high
    )
    to_end = jnp.exp(cumul[:, -1:] - cumul) * step_block
    scaled_x = to_end.T[:, :, None] * x_block
    new_state = jnp.exp(cumul[:, -1])[:, None, None] * state + jnp.einsum(
        "jhp,jn->hpn", scaled_x, b_block, precision=high
    )
    return (new_state, y_inner + y_carry)


def ssd_scan(xconv, b_mat, c_mat, step_size, decay_rate, start_state):
    length = xconv.shape[0]
    heads_here = step_size.shape[0]
    head_width = xconv.shape[1] // heads_here
    count = length // BLOCK
    x_blocks = xconv.reshape(count, BLOCK, heads_here, head_width)
    b_blocks = b_mat.reshape(count, BLOCK, b_mat.shape[1])
    c_blocks = c_mat.reshape(count, BLOCK, c_mat.shape[1])
    s_blocks = step_size.reshape(heads_here, count, BLOCK).transpose(1, 0, 2)

    def stepper(state, pieces):
        return block_step(state, (pieces[0], pieces[1], pieces[2], pieces[3], decay_rate))

    end_state, ys = lax.scan(
        jax.checkpoint(stepper), start_state, (x_blocks, b_blocks, c_blocks, s_blocks)
    )
    return (end_state, ys.reshape(length, heads_here * head_width))


def core_fn(padded_x, padded_bc, dt_raw, conv_x, conv_bc, head_params):
    xconv = conv_silu(padded_x, conv_x)
    bcconv = conv_silu(padded_bc, conv_bc)
    nstate = bcconv.shape[1] // 2
    step_size = jax.nn.softplus(dt_raw + head_params[0][:, None])
    decay_rate = jnp.exp(head_params[1])
    heads_here = step_size.shape[0]
    head_width = xconv.shape[1] // heads_here
    start_state = jnp.zeros((heads_here, head_width, nstate), jnp.float32)
    end_state, ys = ssd_scan(
        xconv, bcconv[:, :nstate], bcconv[:, nstate:], step_size, decay_rate, start_state
    )
    y_out = ys + jnp.repeat(head_params[2], head_width)[None, :] * xconv
    total_decay = jnp.exp(-jnp.sum(step_size * decay_rate[:, None], axis=1))
    return (y_out, total_decay, end_state)


def fix_fn(padded_bc, dt_raw, conv_bc, head_params, start_state):
    bcconv = conv_silu(padded_bc, conv_bc)
    nstate = bcconv.shape[1] // 2
    step_size = jax.nn.softplus(dt_raw + head_params[0][:, None])
    decay_rate = jnp.exp(head_params[1])
    cumul = jnp.cumsum(-step_size * decay_rate[:, None], axis=1)
    projected = jnp.einsum(
        "tn,hpn->thp", bcconv[:, nstate:], start_state, precision=lax.Precision.HIGHEST
    )
    lifted = jnp.exp(cumul).T[:, :, None] * projected
    return lifted.reshape(lifted.shape[0], lifted.shape[1] * lifted.shape[2])


def chain_linear(earlier, later):
    return (earlier[0] * later[0], later[0][:, None, None] * earlier[1] + later[1])


def on_device(
    pre_x,
    pre_bc,
    gate_z,
    dt_raw,
    conv_x,
    conv_bc,
    head_params,
    norm_gain,
    w_out,
    t_conv_x,
    t_conv_bc,
    t_heads,
    t_gain,
    t_wout,
):
    width = conv_x.shape[0] - 1
    tail_x, tail_bc = shifted((pre_x[-width:], pre_bc[-width:]), "seq", 1)
    padded_x = jnp.concatenate([tail_x, pre_x], axis=0)
    padded_bc = jnp.concatenate([tail_bc, pre_bc], axis=0)
    core_local = partial(core_fn, padded_x, padded_bc, dt_raw)
    fix_local = partial(fix_fn, padded_bc, dt_raw)
    primals = (conv_x, conv_bc, head_params)
    tangents = (t_conv_x, t_conv_bc, t_heads)
    (y_zero, decay, state), (d_y_zero, d_decay, d_state) = jax.jvp(core_local, primals, tangents)
    ones_here = jnp.ones(decay.shape, jnp.float32)
    zeros_state = jnp.zeros(state.shape, jnp.float32)
    start = carried_in((decay, state), "seq", chain_linear, (ones_here, zeros_state), False)[1]
    carried = d_state + d_decay[:, None, None] * start
    d_start = carried_in((decay, carried), "seq", chain_linear, (ones_here, zeros_state), False)[1]
    y_fix, d_y_fix = jax.jvp(
        fix_local, (conv_bc, head_params, start), (t_conv_bc, t_heads, d_start)
    )
    y_out = y_zero + y_fix
    d_y = d_y_zero + d_y_fix
    gate = jax.nn.silu(gate_z.astype(jnp.float32))
    gated = y_out * gate
    d_gated = d_y * gate
    channels = NH * P_SIZE * 1.0
    squares = lax.psum(jnp.sum(gated * gated, axis=1), "head")
    inv_rms = lax.rsqrt(squares / channels + 1e-05)
    crossed = lax.psum(jnp.sum(2.0 * gated * d_gated, axis=1), "head")
    d_inv = -0.5 * inv_rms**3 * crossed / channels
    normed = (gated * inv_rms[:, None] * norm_gain).astype(jnp.bfloat16)
    d_normed = (
        (d_gated * inv_rms[:, None] + gated * d_inv[:, None]) * norm_gain
        + gated * inv_rms[:, None] * t_gain
    ).astype(jnp.bfloat16)
    partial_out = jnp.dot(d_normed, w_out, preferred_element_type=jnp.float32) + jnp.dot(
        normed,
        lax.all_gather(t_wout, "seq", axis=1, tiled=True),
        preferred_element_type=jnp.float32,
    )
    probe_out = lax.psum(partial_out, "head").astype(jnp.bfloat16)
    gn_wout = lax.psum_scatter(
        jnp.dot(normed.T, probe_out, preferred_element_type=jnp.float32),
        "seq",
        scatter_dimension=1,
        tiled=True,
    )
    back_normed = jnp.dot(probe_out, w_out.T, preferred_element_type=jnp.float32)
    gain_part = jnp.sum(back_normed * gated * inv_rms[:, None], axis=0)
    weighted = back_normed * norm_gain
    mixed = lax.psum(jnp.sum(weighted * gated, axis=1), "head")
    back_y = (weighted * inv_rms[:, None] - gated * (inv_rms**3 * mixed / channels)[:, None]) * gate
    fix_value, fix_pull = jax.vjp(fix_local, conv_bc, head_params, start)
    back_bc_fix, back_heads_fix, back_start = fix_pull(back_y)
    adjoint_state = carried_in(
        (decay, back_start), "seq", chain_linear, (ones_here, zeros_state), True
    )[1]
    back_decay = jnp.sum(adjoint_state * start, axis=(1, 2))
    core_value, core_pull = jax.vjp(core_local, conv_x, conv_bc, head_params)
    back_cx, back_cbc, back_heads = core_pull((back_y, back_decay, adjoint_state))
    gn_conv_x, gn_heads, gn_gain = lax.psum(
        (back_cx, back_heads + back_heads_fix, gain_part), "seq"
    )
    gn_conv_bc = lax.psum(back_cbc + back_bc_fix, ("seq", "head"))
    return (gn_conv_x, gn_conv_bc, gn_heads, gn_gain, gn_wout)


def solution(mesh):
    in_specs = (
        P("seq", "head"),
        P("seq", None),
        P("seq", "head"),
        P("head", "seq"),
        P(None, "head"),
        P(),
        P(None, "head"),
        P("head"),
        P("head", None),
        P(None, "head"),
        P(),
        P(None, "head"),
        P("head"),
        P("head", "seq"),
    )
    out_specs = (P(None, "head"), P(), P(None, "head"), P("head"), P("head", "seq"))
    return jax.shard_map(
        on_device, mesh=mesh, in_specs=in_specs, out_specs=out_specs, check_vma=False
    )
```

profile of v0, /device:TPU:0, one launch (start us, length us, event | category | flops | bytes accessed | tf_op | source)
XLA Modules:
  0.0 1131.8 jit_solution(16198120730116998894)
XLA Ops:
  8.6 3.9 collective-permute-start.1
  14.1 3.8 collective-permute-start
  32.7 3.1 multiply_add_fusion.5
  40.3 5.3 multiply_add_fusion.3
  49.3 4.2 reshape.570
  53.5 3.8 copy.237
  57.2 4.2 reshape.573
  65.4 287.8 %while.97 = (s32[]{:T(128)}, f32[10,64,128]{2,1,0:T(8,128)}, f32[10,64,128]{2,1,0:T(8,128)}, f32[4,256,10,64]{1,0,3,2:T(4,128)}, f32[4,256,10,64]{1,0,3,2:T(4,12...) while((s32[]{:T(128)}, f32[10,64,128]{2,1,0:T(8,128)}, ...), condition=%wide.region_5.7_spmd.clone, body=%wide.region_0.6_spmd.clone.sunk | while | flops 3341637120 | bytes 40975856 | solution.py:83
  73.2 4.3 fusion.393
  79.1 15.2 %dynamic_update_slice.67 = f32[4,256,10,64]{1,0,3,2:T(4,128)} dynamic-update-slice(f32[4,256,10,64]{1,0,3,2:T(4,128)} %get-tuple-element.1723, f32[1,256,10,64]{1,0,3,2:T(1,128)} %copy.382, s32[]{:T(128)} %get-tuple-element.1720, s32[]{:T(128)} %constant.220.clone.1..sunk, s32[]{:T(128)} %constant.220.clone.1..sunk, s32[]{:T(128)} %constant.220.clone.1..sunk) | dynamic-update-slice | bytes 1310724 | tf_op jit(solution)/shard_map/jvp()/while/body/jit(dynamic_update_index_in_dim)/dynamic_update_slice | solution.py:83
  96.7 4.3 fusion.394
  103.7 5.2 fusion.396
  111.9 15.1 %dynamic_update_slice.68 = f32[4,256,10,64]{1,0,3,2:T(4,128)} dynamic-update-slice(f32[4,256,10,64]{1,0,3,2:T(4,128)} %get-tuple-element.1724, f32[1,256,10,64]{1,0,3,2:T(1,128)} %copy.383, s32[]{:T(128)} %get-tuple-element.1720, s32[]{:T(128)} %constant.220.clone.1..sunk, s32[]{:T(128)} %constant.220.clone.1..sunk, s32[]{:T(128)} %constant.220.clone.1..sunk) | dynamic-update-slice | bytes 1310724 | tf_op jit(solution)/shard_map/jvp()/while/body/jit(dynamic_update_index_in_dim)/dynamic_update_slice | solution.py:83
  142.0 4.3 fusion.393
  147.9 15.2 %dynamic_update_slice.67 = f32[4,256,10,64]{1,0,3,2:T(4,128)} dynamic-update-slice(f32[4,256,10,64]{1,0,3,2:T(4,128)} %get-tuple-element.1723, f32[1,256,10,64]{1,0,3,2:T(1,128)} %copy.382, s32[]{:T(128)} %get-tuple-element.1720, s32[]{:T(128)} %constant.220.clone.1..sunk, s32[]{:T(128)} %constant.220.clone.1..sunk, s32[]{:T(128)} %constant.220.clone.1..sunk) | dynamic-update-slice | bytes 1310724 | tf_op jit(solution)/shard_map/jvp()/while/body/jit(dynamic_update_index_in_dim)/dynamic_update_slice | solution.py:83
  165.5 4.3 fusion.394
  172.5 5.2 fusion.396
  181.7 15.1 %dynamic_update_slice.68 = f32[4,256,10,64]{1,0,3,2:T(4,128)} dynamic-update-slice(f32[4,256,10,64]{1,0,3,2:T(4,128)} %get-tuple-element.1724, f32[1,256,10,64]{1,0,3,2:T(1,128)} %copy.383, s32[]{:T(128)} %get-tuple-element.1720, s32[]{:T(128)} %constant.220.clone.1..sunk, s32[]{:T(128)} %constant.220.clone.1..sunk, s32[]{:T(128)} %constant.220.clone.1..sunk) | dynamic-update-slice | bytes 1310724 | tf_op jit(solution)/shard_map/jvp()/while/body/jit(dynamic_update_index_in_dim)/dynamic_update_slice | solution.py:83
  212.1 4.3 fusion.393
  217.9 15.2 %dynamic_update_slice.67 = f32[4,256,10,64]{1,0,3,2:T(4,128)} dynamic-update-slice(f32[4,256,10,64]{1,0,3,2:T(4,128)} %get-tuple-element.1723, f32[1,256,10,64]{1,0,3,2:T(1,128)} %copy.382, s32[]{:T(128)} %get-tuple-element.1720, s32[]{:T(128)} %constant.220.clone.1..sunk, s32[]{:T(128)} %constant.220.clone.1..sunk, s32[]{:T(128)} %constant.220.clone.1..sunk) | dynamic-update-slice | bytes 1310724 | tf_op jit(solution)/shard_map/jvp()/while/body/jit(dynamic_update_index_in_dim)/dynamic_update_slice | solution.py:83
  235.6 4.3 fusion.394
  242.6 5.2 fusion.396
  251.7 15.1 %dynamic_update_slice.68 = f32[4,256,10,64]{1,0,3,2:T(4,128)} dynamic-update-slice(f32[4,256,10,64]{1,0,3,2:T(4,128)} %get-tuple-element.1724, f32[1,256,10,64]{1,0,3,2:T(1,128)} %copy.383, s32[]{:T(128)} %get-tuple-element.1720, s32[]{:T(128)} %constant.220.clone.1..sunk, s32[]{:T(128)} %constant.220.clone.1..sunk, s32[]{:T(128)} %constant.220.clone.1..sunk) | dynamic-update-slice | bytes 1310724 | tf_op jit(solution)/shard_map/jvp()/while/body/jit(dynamic_update_index_in_dim)/dynamic_update_slice | solution.py:83
  282.2 4.3 fusion.393
  288.0 15.2 %dynamic_update_slice.67 = f32[4,256,10,64]{1,0,3,2:T(4,128)} dynamic-update-slice(f32[4,256,10,64]{1,0,3,2:T(4,128)} %get-tuple-element.1723, f32[1,256,10,64]{1,0,3,2:T(1,128)} %copy.382, s32[]{:T(128)} %get-tuple-element.1720, s32[]{:T(128)} %constant.220.clone.1..sunk, s32[]{:T(128)} %constant.220.clone.1..sunk, s32[]{:T(128)} %constant.220.clone.1..sunk) | dynamic-update-slice | bytes 1310724 | tf_op jit(solution)/shard_map/jvp()/while/body/jit(dynamic_update_index_in_dim)/dynamic_update_slice | solution.py:83
  305.7 4.3 fusion.394
  312.6 5.2 fusion.396
  321.8 15.1 %dynamic_update_slice.68 = f32[4,256,10,64]{1,0,3,2:T(4,128)} dynamic-update-slice(f32[4,256,10,64]{1,0,3,2:T(4,128)} %get-tuple-element.1724, f32[1,256,10,64]{1,0,3,2:T(1,128)} %copy.383, s32[]{:T(128)} %get-tuple-element.1720, s32[]{:T(128)} %constant.220.clone.1..sunk, s32[]{:T(128)} %constant.220.clone.1..sunk, s32[]{:T(128)} %constant.220.clone.1..sunk) | dynamic-update-slice | bytes 1310724 | tf_op jit(solution)/shard_map/jvp()/while/body/jit(dynamic_update_index_in_dim)/dynamic_update_slice | solution.py:83
  356.4 37.4 %all-reduce.22 = f32[160]{0:T(256)S(1)} all-reduce(f32[160]{0:T(256)S(1)} %get-tuple-element.1312), channel_id=2, replica_groups=mesh['seq'=16,'head'=8] {'seq'}, use_global_device_ids=true, to_apply=%add.22 | all-reduce | flops 160 | bytes 1280
  393.9 16.4 %all-gather.11.cloned.1.call-done = f32[160,64,128]{2,1,0:T(8,128)} async-done(((f32[10,64,128]{2,1,0:T(8,128)}), f32[160,64,128]{2,1,0:T(8,128)}) %all-gather.11.cloned.1.call-update) | async-done | bytes 5242896 | tf_op jit(solution)/shard_map/all_gather | solution.py:21
  410.3 29.1 %while.98 = (s32[]{:T(128)}, f32[10,64,128]{2,1,0:T(8,128)}, s32[]{:T(128)}, f32[16,10]{1,0:T(8,128)S(1)}, f32[16,10,64,128]{3,2,1,0:T(8,128)}, /*index=5*/s32[]{:T(128)}, s32[]{:T(128)}) while((s32[]{:T(128)}, f32[10,64,128]{2,1,0:T(8,128)}, s32[]{:T(128)}, f32[16,10]{1,0:T(8,128)S(1)}, f32[16,10,64,128]{3,2,1,0:T(8,128)}, ...), condition=%wide.region_12.14_spmd.clone, body=%wide.region_11.13_spmd.clone.sunk | while | flops 327684 | bytes 983265 | solution.py:33
  452.2 4.0 copy.324
  458.3 3.7 fusion.254
  462.0 4.6 broadcast_multiply_fusion.2
  466.6 30.8 %all-gather.13.cloned.1.call-done = f32[160,64,128]{2,1,0:T(8,128)} async-done(((f32[10,64,128]{2,1,0:T(8,128)}), f32[160,64,128]{2,1,0:T(8,128)}) %all-gather.13.cloned.1.call-update) | async-done | bytes 5242896 | tf_op jit(solution)/shard_map/all_gather | solution.py:21
  497.5 28.6 %while.99 = (s32[]{:T(128)}, f32[10,64,128]{2,1,0:T(8,128)}, s32[]{:T(128)}, f32[16,10]{1,0:T(8,128)S(1)}, f32[16,10,64,128]{3,2,1,0:T(8,128)}, /*index=5*/s32[]{:T(128)}, s32[]{:T(128)}) while((s32[]{:T(128)}, f32[10,64,128]{2,1,0:T(8,128)}, s32[]{:T(128)}, f32[16,10]{1,0:T(8,128)S(1)}, f32[16,10,64,128]{3,2,1,0:T(8,128)}, ...), condition=%wide.region_15.17_spmd.clone, body=%wide.region_14.16_spmd.clone.sunk | while | flops 327684 | bytes 983265 | solution.py:33
  526.1 5.4 multiply_add_fusion.2
  531.6 6.5 multiply_reduce_fusion.10
  538.1 15.4 %all-reduce.24 = (f32[1024]{0:T(1024)S(1)}, f32[1024]{0:T(1024)S(1)}) all-reduce(f32[1024]{0:T(1024)S(1)} %get-tuple-element.1117, f32[1024]{0:T(1024)S(1)} %get-tuple-element.1116), channel_id=1, replica_groups=mesh['seq'=16,'head'=8] {'head'}, use_global_device_ids=true, to_apply=%region_19.21 | all-reduce | flops 2048 | bytes 16384 | tf_op jit(solution)/shard_map/psum | solution.py:164
  553.5 10.0 fusion.225
  563.5 14.2 %convolution_add_fusion.8 = f32[1024,2560]{1,0:T(8,128)} fusion(f32[1024,2560]{1,0:T(8,128)} %fusion.225, bf16[640,2560]{0,1:T(8,128)(2,1)} %all-gather.9.cloned.1.call-done, f32[1024,640]{0,1:T(8,128)} %get-tuple-element.1258, f32[640]{0:T(1024)S(1)} %copy-done.66, f32[1024]{0:T(1024)S(1)} %get-tuple-element.1295), kind=kOutput, calls=%fused_computation.254 | convolution fusion | flops 3360030720 | bytes 26876416 | tf_op jit(solution)/shard_map/dot_general | solution.py:171
  577.7 110.6 %all-reduce.26 = bf16[1024,2560]{1,0:T(8,128)(2,1)} all-reduce(f32[1024,2560]{1,0:T(8,128)} %convolution_add_fusion.8), channel_id=1, replica_groups=mesh['seq'=16,'head'=8] {'head'}, use_global_device_ids=true, to_apply=%region_20.22 | all-reduce | flops 2621440 | bytes 15728640 | tf_op jit(solution)/shard_map/psum | solution.py:176
  688.3 9.1 multiply_reduce_fusion.5
  697.4 15.7 %psum.59 = f32[1024]{0:T(1024)S(1)} all-reduce(f32[1024]{0:T(1024)S(1)} %get-tuple-element.1111), channel_id=1, replica_groups=mesh['seq'=16,'head'=8] {'head'}, use_global_device_ids=true, to_apply=%region_22.24 | all-reduce | flops 1024 | bytes 8192 | tf_op jit(solution)/shard_map/psum | solution.py:186
  713.2 5.6 multiply_reduce_fusion.7
  718.8 2.9 fusion.220
  721.9 21.5 %while.101 = (s32[]{:T(128)}, f32[10,64,128]{2,1,0:T(8,128)}, f32[4,10,64,128]{3,2,1,0:T(8,128)}, f32[4,10,256]{2,1,0:T(8,128)S(1)}, f32[10,1]{0,1:T(1,128)S(1)}...) while((s32[]{:T(128)}, f32[10,64,128]{2,1,0:T(8,128)}, ...), condition=%wide.region_30.33_spmd.clone, body=%wide.region_27.32_spmd.clone.sunk | while | flops 252487712 | bytes 2350028 | solution.py:83
  748.2 12.5 %reduce-window.120 = f32[10,8,128]{2,1,0:T(8,128)S(1)} reduce-window(f32[10,8,128]{2,1,0:T(8,128)S(1)} %slice.333, f32[]{:T(128)} %constant.221.clone.1), window={size=1x1x128 pad=0_0x0_0x0_127}, to_apply=%region_67.70 | reduce-window | flops 1300480 | bytes 81924 | tf_op jit(solution)/shard_map/reduce-window.16
  761.8 6.3 fusion.232
  768.1 9.6 fusion.214
  778.4 5.7 rev.7
  784.1 16.9 %while.100 = (s32[]{:T(128)}, f32[10,64,128]{2,1,0:T(8,128)S(1)}, s32[]{:T(128)}, f32[16,10]{1,0:T(8,128)S(1)}, f32[16,10,64,128]{3,2,1,0:T(8,128)}, /*index=5*/s32[]{:T(128)}, s32[]{:T(128)}) while((s32[]{:T(128)}, f32[10,64,128]{2,1,0:T(8,128)S(1)}, s32[]{:T(128)}, f32[16,10]{1,0:T(8,128)S(1)}, ...), condition=%wide.region_26.29_spmd.clone, body=%wide.region_25.28_spmd.clone.sunk | while | flops 327684 | bytes 983265 | solution.py:33
  805.5 167.7 %while.102 = (s32[]{:T(128)}, f32[10]{0:T(128)S(1)}, f32[10,64,128]{2,1,0:T(8,128)S(1)}, f32[4,256,10,64]{1,0,3,2:T(4,128)}, f32[4,256,128]{2,1,0:T(8,128)}, /*i...) while((s32[]{:T(128)}, f32[10]{0:T(128)S(1)}, ...), condition=%wide.region_45.48_spmd.clone, body=%wide.region_31.47_spmd.clone.sunk | while | flops 2582600704 | bytes 25211380 | solution.py:83
  815.8 4.2 fusion.424
  831.4 15.1 %dynamic_update_slice.73 = f32[4,256,10,64]{1,0,3,2:T(4,128)} dynamic-update-slice(f32[4,256,10,64]{1,0,3,2:T(4,128)} %get-tuple-element.1870, f32[1,256,10,64]{1,0,3,2:T(1,128)S(1)} %copy.396, s32[]{:T(128)S(6)} %sub.449, s32[]{:T(128)} %constant.220.clone.1..sunk.5, s32[]{:T(128)} %constant.220.clone.1..sunk.5, s32[]{:T(128)} %constant.220.clone.1..sunk.5) | dynamic-update-slice | bytes 1310724 | tf_op jit(solution)/shard_map/transpose(jvp())/while/body/jit(dynamic_update_index_in_dim)/dynamic_update_slice | solution.py:83
  857.6 4.2 fusion.424
  873.3 15.1 %dynamic_update_slice.73 = f32[4,256,10,64]{1,0,3,2:T(4,128)} dynamic-update-slice(f32[4,256,10,64]{1,0,3,2:T(4,128)} %get-tuple-element.1870, f32[1,256,10,64]{1,0,3,2:T(1,128)S(1)} %copy.396, s32[]{:T(128)S(6)} %sub.449, s32[]{:T(128)} %constant.220.clone.1..sunk.5, s32[]{:T(128)} %constant.220.clone.1..sunk.5, s32[]{:T(128)} %constant.220.clone.1..sunk.5) | dynamic-update-slice | bytes 1310724 | tf_op jit(solution)/shard_map/transpose(jvp())/while/body/jit(dynamic_update_index_in_dim)/dynamic_update_slice | solution.py:83
  899.4 4.2 fusion.424
  915.1 15.1 %dynamic_update_slice.73 = f32[4,256,10,64]{1,0,3,2:T(4,128)} dynamic-update-slice(f32[4,256,10,64]{1,0,3,2:T(4,128)} %get-tuple-element.1870, f32[1,256,10,64]{1,0,3,2:T(1,128)S(1)} %copy.396, s32[]{:T(128)S(6)} %sub.449, s32[]{:T(128)} %constant.220.clone.1..sunk.5, s32[]{:T(128)} %constant.220.clone.1..sunk.5, s32[]{:T(128)} %constant.220.clone.1..sunk.5) | dynamic-update-slice | bytes 1310724 | tf_op jit(solution)/shard_map/transpose(jvp())/while/body/jit(dynamic_update_index_in_dim)/dynamic_update_slice | solution.py:83
  941.2 4.2 fusion.424
  956.9 15.1 %dynamic_update_slice.73 = f32[4,256,10,64]{1,0,3,2:T(4,128)} dynamic-update-slice(f32[4,256,10,64]{1,0,3,2:T(4,128)} %get-tuple-element.1870, f32[1,256,10,64]{1,0,3,2:T(1,128)S(1)} %copy.396, s32[]{:T(128)S(6)} %sub.449, s32[]{:T(128)} %constant.220.clone.1..sunk.5, s32[]{:T(128)} %constant.220.clone.1..sunk.5, s32[]{:T(128)} %constant.220.clone.1..sunk.5) | dynamic-update-slice | bytes 1310724 | tf_op jit(solution)/shard_map/transpose(jvp())/while/body/jit(dynamic_update_index_in_dim)/dynamic_update_slice | solution.py:83
  977.5 8.1 fusion.210
  987.6 62.9 %psum.61 = f32[4,256]{1,0:T(4,128)} all-reduce(f32[4,256]{1,0:T(4,128)S(1)} %add_add_fusion), channel_id=1, replica_groups=mesh['seq'=16,'head'=8] {'seq','head'}, use_global_device_ids=true, to_apply=%region_59.62 | all-reduce | flops 1024 | bytes 8192 | tf_op jit(solution)/shard_map/psum | solution.py:199
  1052.8 72.1 %all-reduce.23 = (f32[4,640]{1,0:T(4,128)}, f32[3,10]{1,0:T(4,128)}, f32[640]{0:T(1024)}) all-reduce(f32[4,640]{1,0:T(4,128)S(1)} %pad_add_fusion, f32[3,10]{1,0:T(4,128)S(1)} %add_add_fusion.1, f32[640]{0:T(1024)S(1)} %copy-done.85), channel_id=1, replica_groups=mesh['seq'=16,'head'=8] {'seq'}, use_global_device_ids=true, to_apply=%region_50.53 | all-reduce | flops 3230 | bytes 25840 | tf_op jit(solution)/shard_map/psum | solution.py:196
  (992 shorter events, 351.8 us)
Async XLA Ops:
  7.2 546.4 %copy-start = (bf16[640,2560]{1,0:T(8,128)(2,1)S(1)}, bf16[640,2560]{1,0:T(8,128)(2,1)}, u32[]{:S(2)}) copy-start(bf16[640,2560]{1,0:T(8,128)(2,1)} %param.37) | copy-start | bytes 9830404
  7.2 403.2 %all-gather.11.cloned.1.call-start = ((), (), s32[]{:S(2)}) async-start(), calls=%async_computation.3 | async-start | bytes 5570560 | tf_op jit(solution)/shard_map/all_gather | solution.py:21
  8.6 24.0 %collective-permute-start.1 = (bf16[3,256]{1,0:T(4,128)(2,1)}, bf16[3,256]{1,0:T(4,128)(2,1)S(1)}, u32[]{:S(2)}, u32[]{:S(2)}) collective-permute-start(bf16[3,256]{1,0:T(4,128)(2,1)} %slice.261), channel_id=1, source_target_pairs={{0,8},{8,16},{16,24},{24,32},{32,40},{40,48},{48,56},{56,64},{64,7... | collective-permute-start | bytes 4616 | tf_op jit(solution)/shard_map/ppermute | solution.py:16
  14.1 26.2 %collective-permute-start = (bf16[3,640]{0,1:T(8,128)(2,1)}, bf16[3,640]{0,1:T(8,128)(2,1)S(1)}, u32[]{:S(2)}, u32[]{:S(2)}) collective-permute-start(bf16[3,640]{0,1:T(8,128)(2,1)} %copy.233), channel_id=1, source_target_pairs={{0,8},{8,16},{16,24},{24,32},{32,40},{40,48},{48,56},{56,64},{64,7... | collective-permute-start | bytes 11528 | tf_op jit(solution)/shard_map/ppermute | solution.py:16
  19.3 11.1 copy-start.81
  109.6 17.4 %copy-start.51 = (f32[10,256]{1,0:T(8,128)S(1)}, f32[10,256]{1,0:T(8,128)}, u32[]{:S(2)}) copy-start(f32[10,256]{1,0:T(8,128)} %get-tuple-element.1636) | copy-start | bytes 30724 | tf_op jit(solution)/shard_map/jvp()/while
  109.6 17.4 %copy-start.59 = (f32[10]{0:T(128)S(1)}, f32[10]{0:T(128)}, u32[]{:S(2)}) copy-start(f32[10]{0:T(128)} %copy-done.58) | copy-start | bytes 124 | tf_op jit(solution)/shard_map/jvp()/while
  109.6 17.5 %copy-start.43 = (f32[256,10]{0,1:T(8,128)S(1)}, f32[256,10]{0,1:T(8,128)}, u32[]{:S(2)}) copy-start(f32[256,10]{0,1:T(8,128)} %get-tuple-element.1638) | copy-start | bytes 30724 | tf_op jit(solution)/shard_map/jvp()/while
  110.4 18.8 %copy-start.65 = (f32[10]{0:T(128)S(1)}, f32[10]{0:T(128)}, u32[]{:S(2)}) copy-start(f32[10]{0:T(128)} %copy-done.64) | copy-start | bytes 124 | tf_op jit(solution)/shard_map/jvp()/while
  179.4 17.4 %copy-start.51 = (f32[10,256]{1,0:T(8,128)S(1)}, f32[10,256]{1,0:T(8,128)}, u32[]{:S(2)}) copy-start(f32[10,256]{1,0:T(8,128)} %get-tuple-element.1636) | copy-start | bytes 30724 | tf_op jit(solution)/shard_map/jvp()/while
  179.4 17.4 %copy-start.59 = (f32[10]{0:T(128)S(1)}, f32[10]{0:T(128)}, u32[]{:S(2)}) copy-start(f32[10]{0:T(128)} %copy-done.58) | copy-start | bytes 124 | tf_op jit(solution)/shard_map/jvp()/while
  179.4 17.5 %copy-start.43 = (f32[256,10]{0,1:T(8,128)S(1)}, f32[256,10]{0,1:T(8,128)}, u32[]{:S(2)}) copy-start(f32[256,10]{0,1:T(8,128)} %get-tuple-element.1638) | copy-start | bytes 30724 | tf_op jit(solution)/shard_map/jvp()/while
  180.2 18.8 %copy-start.65 = (f32[10]{0:T(128)S(1)}, f32[10]{0:T(128)}, u32[]{:S(2)}) copy-start(f32[10]{0:T(128)} %copy-done.64) | copy-start | bytes 124 | tf_op jit(solution)/shard_map/jvp()/while
  196.9 7.4 copy-start.35
  196.9 7.4 copy-start.61
  196.9 7.4 copy-start.72
  249.5 17.4 %copy-start.51 = (f32[10,256]{1,0:T(8,128)S(1)}, f32[10,256]{1,0:T(8,128)}, u32[]{:S(2)}) copy-start(f32[10,256]{1,0:T(8,128)} %get-tuple-element.1636) | copy-start | bytes 30724 | tf_op jit(solution)/shard_map/jvp()/while
  249.5 17.4 %copy-start.59 = (f32[10]{0:T(128)S(1)}, f32[10]{0:T(128)}, u32[]{:S(2)}) copy-start(f32[10]{0:T(128)} %copy-done.58) | copy-start | bytes 124 | tf_op jit(solution)/shard_map/jvp()/while
  249.5 17.5 %copy-start.43 = (f32[256,10]{0,1:T(8,128)S(1)}, f32[256,10]{0,1:T(8,128)}, u32[]{:S(2)}) copy-start(f32[256,10]{0,1:T(8,128)} %get-tuple-element.1638) | copy-start | bytes 30724 | tf_op jit(solution)/shard_map/jvp()/while
  250.2 18.8 %copy-start.65 = (f32[10]{0:T(128)S(1)}, f32[10]{0:T(128)}, u32[]{:S(2)}) copy-start(f32[10]{0:T(128)} %copy-done.64) | copy-start | bytes 124 | tf_op jit(solution)/shard_map/jvp()/while
  267.0 7.4 copy-start.35
  267.0 7.4 copy-start.61
  319.5 17.4 %copy-start.51 = (f32[10,256]{1,0:T(8,128)S(1)}, f32[10,256]{1,0:T(8,128)}, u32[]{:S(2)}) copy-start(f32[10,256]{1,0:T(8,128)} %get-tuple-element.1636) | copy-start | bytes 30724 | tf_op jit(solution)/shard_map/jvp()/while
  319.5 17.4 %copy-start.59 = (f32[10]{0:T(128)S(1)}, f32[10]{0:T(128)}, u32[]{:S(2)}) copy-start(f32[10]{0:T(128)} %copy-done.58) | copy-start | bytes 124 | tf_op jit(solution)/shard_map/jvp()/while
  319.5 17.5 %copy-start.43 = (f32[256,10]{0,1:T(8,128)S(1)}, f32[256,10]{0,1:T(8,128)}, u32[]{:S(2)}) copy-start(f32[256,10]{0,1:T(8,128)} %get-tuple-element.1638) | copy-start | bytes 30724 | tf_op jit(solution)/shard_map/jvp()/while
  320.3 18.8 %copy-start.65 = (f32[10]{0:T(128)S(1)}, f32[10]{0:T(128)}, u32[]{:S(2)}) copy-start(f32[10]{0:T(128)} %copy-done.64) | copy-start | bytes 124 | tf_op jit(solution)/shard_map/jvp()/while
  337.0 7.4 copy-start.35
  337.0 7.4 copy-start.61
  353.2 57.1 %copy-start.62 = (f32[10]{0:T(128)}, f32[10]{0:T(128)S(1)}, u32[]{:S(2)}) copy-start(f32[10]{0:T(128)S(1)} %get-tuple-element.1928) | copy-start | bytes 124
  353.2 144.2 %all-gather.13.cloned.1.call-start = ((), (), s32[]{:S(2)}) async-start(), calls=%async_computation.4 | async-start | bytes 5570560 | tf_op jit(solution)/shard_map/all_gather | solution.py:21
  356.3 85.0 %copy-start.83 = (f32[10]{0:T(128)}, f32[10]{0:T(128)S(1)}, u32[]{:S(2)}) copy-start(f32[10]{0:T(128)S(1)} %get-tuple-element.1133) | copy-start | bytes 124
  410.3 31.8 %copy-start.57 = (f32[10,1024]{1,0:T(8,128)S(1)}, f32[10,1024]{1,0:T(8,128)}, u32[]{:S(2)}) copy-start(f32[10,1024]{1,0:T(8,128)} %get-tuple-element.1293) | copy-start | bytes 122884
  410.3 35.1 %copy-start.55 = (f32[10,1024]{1,0:T(8,128)S(1)}, f32[10,1024]{1,0:T(8,128)}, u32[]{:S(2)}) copy-start(f32[10,1024]{1,0:T(8,128)} %get-tuple-element.1259) | copy-start | bytes 122884
  441.3 10.7 copy-start.87
  441.3 122.2 %all-gather.9.cloned.1.call-start = ((), (), s32[]{:S(2)}) async-start(), calls=%async_computation.1 | async-start | bytes 3481600 | tf_op jit(solution)/shard_map/all_gather | solution.py:173
  442.1 336.3 %all-gather.15.cloned.1.call-start = ((), (), s32[]{:S(2)}) async-start(), calls=%async_computation.5 | async-start | bytes 5570560 | tf_op jit(solution)/shard_map/all_gather | solution.py:21
  449.6 81.9 %copy-start.67 = (f32[640]{0:T(1024)}, f32[640]{0:T(1024)S(1)}, u32[]{:S(2)}) copy-start(f32[640]{0:T(1024)S(1)} %mul.1235) | copy-start | bytes 7684
  531.5 22.0 %copy-start.66 = (f32[640]{0:T(1024)S(1)}, f32[640]{0:T(1024)}, u32[]{:S(2)}) copy-start(f32[640]{0:T(1024)} %param.36) | copy-start | bytes 7684
  531.5 22.0 %copy-start.88 = (f32[640]{0:T(1024)S(1)}, f32[640]{0:T(1024)}, u32[]{:S(2)}) copy-start(f32[640]{0:T(1024)} %param.41) | copy-start | bytes 7684
  718.8 43.0 %copy-start.2 = (f32[1024,640]{0,1:T(8,128)}, f32[1024,640]{0,1:T(8,128)S(1)}, u32[]{:S(2)}) copy-start(f32[1024,640]{0,1:T(8,128)S(1)} %get-tuple-element.1254) | copy-start | bytes 7864324
  721.8 403.1 %reduce-scatter.2.cloned.1.call-start = ((), (), s32[]{:S(2)}) async-start(), calls=%async_computation.2 | async-start | bytes 6963200 | tf_op jit(solution)/shard_map/reduce_scatter | solution.py:177
  805.5 171.2 %copy-start.68 = (f32[640]{0:T(1024)S(1)}, f32[640]{0:T(1024)}, u32[]{:S(2)}) copy-start(f32[640]{0:T(1024)} %copy-done.67) | copy-start | bytes 7684
  830.8 16.8 %copy-start.37 = (f32[4,10,256]{2,1,0:T(8,128)S(1)}, f32[4,10,256]{2,1,0:T(8,128)}, u32[]{:S(2)}) copy-start(f32[4,10,256]{2,1,0:T(8,128)} %copy-done.36) | copy-start | bytes 122884 | tf_op jit(solution)/shard_map/transpose(jvp())/while
  872.6 16.7 %copy-start.37 = (f32[4,10,256]{2,1,0:T(8,128)S(1)}, f32[4,10,256]{2,1,0:T(8,128)}, u32[]{:S(2)}) copy-start(f32[4,10,256]{2,1,0:T(8,128)} %copy-done.36) | copy-start | bytes 122884 | tf_op jit(solution)/shard_map/transpose(jvp())/while
  914.4 16.7 %copy-start.37 = (f32[4,10,256]{2,1,0:T(8,128)S(1)}, f32[4,10,256]{2,1,0:T(8,128)}, u32[]{:S(2)}) copy-start(f32[4,10,256]{2,1,0:T(8,128)} %copy-done.36) | copy-start | bytes 122884 | tf_op jit(solution)/shard_map/transpose(jvp())/while
  956.2 16.8 %copy-start.37 = (f32[4,10,256]{2,1,0:T(8,128)S(1)}, f32[4,10,256]{2,1,0:T(8,128)}, u32[]{:S(2)}) copy-start(f32[4,10,256]{2,1,0:T(8,128)} %copy-done.36) | copy-start | bytes 122884 | tf_op jit(solution)/shard_map/transpose(jvp())/while
  977.5 8.3 copy-start.26
  977.5 8.3 copy-start.28
  977.5 8.3 copy-start.30
  977.5 8.3 copy-start.40
  977.5 8.3 copy-start.41
  977.5 8.3 copy-start.42
  977.5 8.3 copy-start.70
  977.5 8.3 copy-start.77
  977.5 8.3 copy-start.78
  977.5 8.3 copy-start.79
  977.5 8.3 copy-start.80
  985.8 139.0 %copy-start.1 = (bf16[640,2560]{1,0:T(8,128)(2,1)S(1)}, bf16[640,2560]{1,0:T(8,128)(2,1)}, u32[]{:S(2)}) copy-start(bf16[640,2560]{1,0:T(8,128)(2,1)} %param.37) | copy-start | bytes 9830404
  986.8 65.0 %copy-start.84 = (f32[10]{0:T(128)S(1)}, f32[10]{0:T(128)}, u32[]{:S(2)}) copy-start(f32[10]{0:T(128)} %copy-done.83) | copy-start | bytes 124
  986.8 65.0 %copy-start.86 = (f32[3,10]{1,0:T(4,128)S(1)}, f32[3,10]{1,0:T(4,128)}, u32[]{:S(2)}) copy-start(f32[3,10]{1,0:T(4,128)} %param.35) | copy-start | bytes 364
  986.8 65.0 %copy-start.53 = (f32[10,1024]{1,0:T(8,128)S(1)}, f32[10,1024]{1,0:T(8,128)}, u32[]{:S(2)}) copy-start(f32[10,1024]{1,0:T(8,128)} %param.32) | copy-start | bytes 122884
  986.8 65.0 %copy-start.56 = (f32[2,8,8,128]{3,1,2,0:T(8,128)S(1)}, f32[2,8,8,128]{3,1,2,0:T(8,128)}, u32[]{:S(2)}) copy-start(f32[2,8,8,128]{3,1,2,0:T(8,128)} %copy.333) | copy-start | bytes 196612
  986.8 65.0 %copy-start.82 = (f32[10]{0:T(128)S(1)}, f32[10]{0:T(128)}, u32[]{:S(2)}) copy-start(f32[10]{0:T(128)} %copy-done.81) | copy-start | bytes 124
  986.8 66.0 %copy-start.85 = (f32[640]{0:T(1024)S(1)}, f32[640]{0:T(1024)}, u32[]{:S(2)}) copy-start(f32[640]{0:T(1024)} %get-tuple-element.1110) | copy-start | bytes 7684
  (125 other events, 649.0 us)
Sparse Core Ops, SparseCore 0:
  353.4 56.9 all-gather.10
  441.5 55.9 all-gather.12
  499.7 48.1 all-gather.8
  721.9 53.5 all-gather.14
  779.3 81.6 reduce-scatter.1
where the time goes:
time: 1150 us; the launch traced here: 1130 us
  blocking collectives  314 us (27%)
  local copies, waits for them, and re-layouts  304 us (26%)
  matrix products  252 us (22%)
  other arithmetic  177 us (15%)
  waiting for transfers between devices  48 us (4%)
  between operations  15.8 us (1%)
  loops' own time  13 us (1%)
    dynamic_update_slice x24, local copies, waits for them, and re-layouts, ssd_scan(): lax.scan(jax.checkpoint(stepper), start_state, (x_blocks, b_blocks, c_blo...  196 us
    psum x1, blocking collectives, on_device(): probe_out = lax.psum(partial_out, 'head').astype(jnp.bfloat16)  111 us
    dot_general x20, matrix products, block_step(): y_inner = jnp.einsum('hij,jhp->ihp', weights_in, x_block, precision=high)  81.5 us
    select_n x45, other arithmetic, step(): jnp.where(position < mine, new, old)  73.8 us
    psum x1, blocking collectives, on_device(): lax.psum((back_cx, back_heads + back_heads_fix, gain_part), 'seq')  72.1 us
    psum x1, blocking collectives, on_device(): gn_conv_bc = lax.psum(back_cbc + back_bc_fix, ('seq', 'head'))  62.9 us
    dot_general x24, matrix products, block_step(): jnp.einsum('jhp,jn->hpn', scaled_x, b_block, precision=high)  50.5 us
    all_gather x3, waiting for transfers between devices, carried_in(): pieces = jax.tree.map(lambda part: lax.all_gather(part, axis), value)  47.3 us
  transfers between devices with their start and end apart: 7, of which 2 were waited for; matrix products, arithmetic and copies ran while one was open for 32% of the time, Pallas kernels for 0%

commit v1 on v0

v1 whole, which is shorter than its diff:
```python
import jax
import jax.numpy as jnp
from jax import lax
from jax.experimental import pallas as pl
from jax.experimental.pallas import tpu as pltpu
from jax.sharding import PartitionSpec as P

QB = 128
HW = 64
F32 = jnp.float32
BF16 = jnp.bfloat16
MESH = pl.DeviceIdType.MESH
S_, DS_, C_, DC_, CS_, SG_, K_, DK_ = (16 * i for i in range(8))
LIMIT = 50 * 1024 * 1024


def split(a):
    high = a.astype(BF16)
    return high, (a - high.astype(F32)).astype(BF16)


def nn(a, b):
    return jnp.dot(a, b, preferred_element_type=F32)


def nt(a, b):
    return lax.dot_general(a, b, (((1,), (1,)), ((), ())), preferred_element_type=F32)


def nn3(a, b):
    (ah, al), (bh, bl) = split(a), split(b)
    return nn(ah, bh) + nn(ah, bl) + nn(al, bh)


def nt3(a, b):
    (ah, al), (bh, bl) = split(a), split(b)
    return nt(ah, bh) + nt(ah, bl) + nt(al, bh)


def lane_mask():
    return lax.broadcasted_iota(jnp.int32, (1, 128), 1) < HW


def bcast(cols, at):
    return jnp.broadcast_to(cols[:, at : at + 1], (cols.shape[0], 128))


def expand(cols, base, pair):
    return jnp.where(
        lane_mask(), bcast(cols, base + 2 * pair), bcast(cols, base + 2 * pair + 1)
    )


def expand_all(cols, base, heads):
    return jnp.concatenate([expand(cols, base, p) for p in range(heads // 2)], axis=1)


def load_window(window, halo, block, first):
    @pl.when(first)
    def _():
        window[0:8] = halo[...]

    @pl.when(jnp.logical_not(first))
    def _():
        window[0:8] = window[QB : QB + 8]

    window[8 : QB + 8] = block[...].astype(F32)


def conv_pair(window, weight, t_weight):
    z = jnp.zeros((QB, window.shape[1]), F32)
    dz = jnp.zeros((QB, window.shape[1]), F32)
    for k in range(4):
        rows = window[5 + k : 5 + k + QB, :]
        z = z + weight[k : k + 1, :] * rows
        dz = dz + t_weight[k : k + 1, :] * rows
    sig = jax.nn.sigmoid(z)
    slope = sig * (1.0 + z * (1.0 - sig))
    return z * sig, slope * dz, slope


def first_kernel(
    pre_x, halo_x, pre_bc, halo_bc, dt, cx, tcx, cbc, tcbc, hpc,
    x_o, dx_o, gx_o, bc_o, dbc_o, gbc_o, row_o, col_o, st_o, dst_o, log_o, msg_o,
    wx, wbc, feat, state, d_state, logs,
):
    step = pl.program_id(0)
    heads = dt.shape[0]
    nst = cbc.shape[1] // 2

    @pl.when(step == 0)
    def _():
        state[...] = jnp.zeros_like(state)
        d_state[...] = jnp.zeros_like(d_state)
        logs[...] = jnp.zeros_like(logs)
        feat[...] = jnp.zeros_like(feat)

    load_window(wx, halo_x, pre_x, step == 0)
    load_window(wbc, halo_bc, pre_bc, step == 0)
    z = dt[...] + hpc[:, 0:1]
    rate = jnp.exp(hpc[:, 1:2])
    t_bias, t_lrate = hpc[:, 3:4], hpc[:, 4:5]
    size = jnp.maximum(z, 0.0) + jnp.log1p(jnp.exp(-jnp.abs(z)))
    sig = jax.nn.sigmoid(z)
    log_decay = -size * rate
    at_i = lax.broadcasted_iota(jnp.int32, (QB, QB), 1)
    at_j = lax.broadcasted_iota(jnp.int32, (QB, QB), 0)
    upper = jnp.where(at_j <= at_i, 1.0, 0.0).astype(F32)
    cumul = jnp.dot(log_decay, upper, precision=lax.Precision.HIGHEST, preferred_element_type=F32)
    sig_sum = jnp.dot(sig, upper, precision=lax.Precision.HIGHEST, preferred_element_type=F32)
    d_size = sig * t_bias
    d_cumul = cumul * t_lrate - rate * t_bias * sig_sum
    to_end = jnp.exp(cumul[:, QB - 1 : QB] - cumul)
    feat[S_ : S_ + heads] = size
    feat[DS_ : DS_ + heads] = d_size
    feat[C_ : C_ + heads] = cumul
    feat[DC_ : DC_ + heads] = d_cumul
    feat[CS_ : CS_ + heads] = sig_sum
    feat[SG_ : SG_ + heads] = sig
    feat[K_ : K_ + heads] = to_end * size
    feat[DK_ : DK_ + heads] = to_end * (
        d_size + size * (d_cumul[:, QB - 1 : QB] - d_cumul)
    )
    rows = feat[...]
    cols = rows.T
    row_o[...] = rows
    col_o[...] = cols

    bc, dbc, gbc = conv_pair(wbc, cbc, tcbc)
    bc_o[...] = bc
    dbc_o[...] = dbc
    gbc_o[...] = gbc
    x, dx, gx = conv_pair(wx, cx, tcx)
    x_o[...] = x
    dx_o[...] = dx
    gx_o[...] = gx

    last = cols[QB - 1 : QB, :]
    own = expand_all(last, C_, heads)
    d_own = expand_all(last, DC_, heads)
    sig_own = expand_all(last, CS_, heads)
    log_o[0, 0:1, :] = logs[0:1, :]
    log_o[0, 1:2, :] = logs[1:2, :]
    log_o[0, 2:3, :] = own
    log_o[0, 3:4, :] = d_own
    log_o[0, 4:5, :] = sig_own
    log_o[0, 5:8, :] = jnp.zeros((3, own.shape[1]), F32)
    logs[0:1, :] = logs[0:1, :] + own
    logs[1:2, :] = logs[1:2, :] + d_own

    st_o[0] = state[...]
    dst_o[0] = d_state[...]
    bt = bc[:, :nst].T
    dbt = dbc[:, :nst].T
    both = jnp.concatenate([bt, dbt], axis=1)
    both_h, both_l = split(both)
    for p in range(heads // 2):
        at = slice(128 * p, 128 * p + 128)
        k_x, dk_x = expand(cols, K_, p), expand(cols, DK_, p)
        ux = k_x * x[:, at]
        dux = k_x * dx[:, at] + dk_x * x[:, at]
        z_h, z_l = split(jnp.concatenate([dux, ux], axis=0))
        d_add = nn(both_h, z_h) + nn(both_h, z_l) + nn(both_l, z_h)
        b_h, b_l, u_h, u_l = both_h[:, :QB], both_l[:, :QB], z_h[QB:], z_l[QB:]
        add = nn(b_h, u_h) + nn(b_h, u_l) + nn(b_l, u_h)
        decay = jnp.exp(own[:, at])
        before = state[:, at]
        d_state[:, at] = decay * (d_state[:, at] + d_own[:, at] * before) + d_add
        state[:, at] = decay * before + add

    @pl.when(step == pl.num_programs(0) - 1)
    def _():
        parts = msg_o.shape[0]
        width = state.shape[1]
        msg_o[:, 0:8, :] = state[...].reshape(parts, 8, width)
        msg_o[:, 8:16, :] = d_state[...].reshape(parts, 8, width)
        msg_o[:, 16:24, :] = jnp.broadcast_to(logs[...][None], (parts, 8, width))


def first_call(pre_x, halo_x, pre_bc, halo_bc, dt, cx, tcx, cbc, tcbc, hpc, parts):
    length, width = pre_x.shape
    wide = pre_bc.shape[1]
    nst = wide // 2
    heads = dt.shape[0]
    count = length // QB
    whole = lambda a: pl.BlockSpec(a.shape, lambda i: (0,) * a.ndim)
    rows = lambda w: pl.BlockSpec((QB, w), lambda i: (i, 0))
    cube = lambda r: pl.BlockSpec((1, r, width), lambda i: (i, 0, 0))
    out = lambda *s: jax.ShapeDtypeStruct(s, F32)
    return pl.pallas_call(
        first_kernel,
        grid=(count,),
        in_specs=[
            rows(width), whole(halo_x), rows(wide), whole(halo_bc),
            pl.BlockSpec((heads, QB), lambda i: (0, i)),
            whole(cx), whole(tcx), whole(cbc), whole(tcbc), whole(hpc),
        ],
        out_specs=[rows(width)] * 3 + [rows(wide)] * 3 + [
            pl.BlockSpec((128, QB), lambda i: (0, i)),
            rows(128), cube(nst), cube(nst), cube(8),
            pl.BlockSpec((parts, 24, width), lambda i: (0, 0, 0)),
        ],
        out_shape=[out(length, width)] * 3 + [out(length, wide)] * 3 + [
            out(128, length), out(length, 128),
            out(count, nst, width), out(count, nst, width), out(count, 8, width),
            out(parts, 24, width),
        ],
        scratch_shapes=[
            pltpu.VMEM((QB + 8, width), F32), pltpu.VMEM((QB + 8, wide), F32),
            pltpu.VMEM((128, QB), F32), pltpu.VMEM((nst, width), F32),
            pltpu.VMEM((nst, width), F32), pltpu.VMEM((8, width), F32),
        ],
        compiler_params=pltpu.CompilerParams(vmem_limit_bytes=LIMIT),
        name="conv_and_states",
    )(pre_x, halo_x, pre_bc, halo_bc, dt, cx, tcx, cbc, tcbc, hpc)


def scan_kernel(count, forward, msg, result, landed, answer, send1, recv1, send2, recv2):
    me = lax.axis_index("seq")
    barrier = pltpu.get_barrier_semaphore()
    for k in range(1, count):
        pl.semaphore_signal(
            barrier, inc=1, device_id={"seq": lax.rem(me + k, count)}, device_id_type=MESH
        )
    pl.semaphore_wait(barrier, count - 1)
    first = []
    for k in range(1, count):
        to = lax.rem(me + k, count)
        copy = pltpu.make_async_remote_copy(
            src_ref=msg.at[to],
            dst_ref=landed.at[me],
            send_sem=send1.at[k],
            recv_sem=recv1.at[k],
            device_id={"seq": to},
            device_id_type=MESH,
        )
        copy.start()
        first.append(copy)
    landed[me] = msg[me]
    for copy in first:
        copy.wait()
    width = msg.shape[2]
    state = jnp.zeros((8, width), F32)
    d_state = jnp.zeros((8, width), F32)
    for i in range(count) if forward else range(count - 1, -1, -1):
        if forward:
            answer[i, 0:8] = state
            answer[i, 8:16] = d_state
            decay = jnp.exp(landed[i, 16:17])
            d_state = decay * (d_state + landed[i, 17:18] * state) + landed[i, 8:16]
        else:
            answer[i] = state
            decay = jnp.exp(landed[i, 8:9])
        state = decay * state + landed[i, 0:8]
    second = []
    for k in range(1, count):
        to = lax.rem(me + k, count)
        copy = pltpu.make_async_remote_copy(
            src_ref=answer.at[to],
            dst_ref=result.at[me],
            send_sem=send2.at[k],
            recv_sem=recv2.at[k],
            device_id={"seq": to},
            device_id_type=MESH,
        )
        copy.start()
        second.append(copy)
    result[me] = answer[me]
    for copy in second:
        copy.wait()


def scan_call(msg, forward, collective_id):
    parts, rows, width = msg.shape
    back = 16 if forward else 8
    vmem = pl.BlockSpec(memory_space=pltpu.VMEM)

    def kernel(*refs):
        scan_kernel(parts, forward, *refs)

    return pl.pallas_call(
        kernel,
        in_specs=[vmem],
        out_specs=vmem,
        out_shape=jax.ShapeDtypeStruct((parts, back, width), F32),
        scratch_shapes=[
            pltpu.VMEM((parts, rows, width), F32),
            pltpu.VMEM((parts, back, width), F32),
            pltpu.SemaphoreType.DMA((parts,)),
            pltpu.SemaphoreType.DMA((parts,)),
            pltpu.SemaphoreType.DMA((parts,)),
            pltpu.SemaphoreType.DMA((parts,)),
        ],
        compiler_params=pltpu.CompilerParams(
            collective_id=collective_id, has_side_effects=True, vmem_limit_bytes=LIMIT
        ),
        name="state_scan_forward" if forward else "state_scan_backward",
    )(msg)


def second_kernel(
    x, dx, bc, dbc, rowv, colv, st, dst, log, start, gate_z, dexp,
    gated_o, dgated_o, s0_o, sums_o,
):
    nst = bc.shape[1] // 2
    heads = x.shape[1] // HW
    b_mat, c_mat = bc[:, :nst], bc[:, nst:]
    db_mat, dc_mat = dbc[:, :nst], dbc[:, nst:]
    at_j = lax.broadcasted_iota(jnp.int32, (QB, QB), 1)
    at_i = lax.broadcasted_iota(jnp.int32, (QB, QB), 0)
    keep = at_i >= at_j
    inner = jnp.where(keep, nt3(c_mat, b_mat), 0.0)
    d_inner = jnp.where(
        keep,
        nt3(
            jnp.concatenate([dc_mat, c_mat], axis=1),
            jnp.concatenate([b_mat, db_mat], axis=1),
        ),
        0.0,
    )
    cols = colv[...]
    rows = rowv[...]
    mask = lane_mask()
    squares = jnp.zeros((QB, 128), F32)
    crossed = jnp.zeros((QB, 128), F32)
    for p in range(heads // 2):
        at = slice(128 * p, 128 * p + 128)
        reach = jnp.exp(log[0, 0:1, at])
        s_in = start[:, 0:8, at].reshape(nst, 128)
        ds_in = start[:, 8:16, at].reshape(nst, 128)
        s0 = st[0, :, at] + reach * s_in
        ds0 = dst[0, :, at] + reach * (ds_in + log[0, 1:2, at] * s_in)
        s0_o[0, :, at] = s0
        xp, dxp = x[:, at], dx[:, at]
        size, d_size = expand(cols, S_, p), expand(cols, DS_, p)
        u = size * xp
        du = size * dxp + d_size * xp
        z_h, z_l = split(jnp.concatenate([u, s0], axis=0))
        dz_h, dz_l = split(jnp.concatenate([du, ds0], axis=0))
        mats, d_mats = [], []
        for h in (2 * p, 2 * p + 1):
            c_col = bcast(cols, C_ + h)
            dc_col = bcast(cols, DC_ + h)
            c_row = rows[C_ + h : C_ + h + 1, :]
            dc_row = rows[DC_ + h : DC_ + h + 1, :]
            level = jnp.exp(jnp.minimum(c_col - c_row, 0.0))
            m = inner * level
            dm = d_inner * level + m * (dc_col - dc_row)
            lift = jnp.exp(c_col)
            e = lift * c_mat
            de = lift * dc_mat + dc_col * e
            mats.append(jnp.concatenate([m, e], axis=1))
            d_mats.append(jnp.concatenate([dm, de], axis=1))
        a_h, a_l = split(jnp.concatenate(mats, axis=0))
        da_h, da_l = split(jnp.concatenate(d_mats, axis=0))
        big = nn(a_h, jnp.concatenate([z_h, dz_h], axis=1))
        big = big + nn(a_h, jnp.concatenate([z_l, dz_l], axis=1))
        big = big + nn(a_l, jnp.concatenate([z_h, dz_h], axis=1))
        small = nn(da_h, jnp.concatenate([z_h, z_l], axis=1))
        low = nn(da_l, z_h)
        y2 = big[:, :128]
        dy2 = big[:, 128:] + small[:, :128] + small[:, 128:] + low
        skip, d_skip = dexp[0:1, at], dexp[1:2, at]
        y = jnp.where(mask, y2[:QB], y2[QB:]) + skip * xp
        dy = jnp.where(mask, dy2[:QB], dy2[QB:]) + skip * dxp + d_skip * xp
        gz = gate_z[:, at].astype(F32)
        gate = gz * jax.nn.sigmoid(gz)
        gated = y * gate
        dgated = dy * gate
        gated_o[:, at] = gated
        dgated_o[:, at] = dgated
        squares = squares + gated * gated
        crossed = crossed + 2.0 * gated * dgated
    sums_o[0:1, :] = jnp.sum(squares.T, axis=0, keepdims=True)
    sums_o[1:2, :] = jnp.sum(crossed.T, axis=0, keepdims=True)


def second_call(x, dx, bc, dbc, rowv, colv, st, dst, logs, start, gate_z, dexp):
    length, width = x.shape
    wide = bc.shape[1]
    nst = wide // 2
    count = length // QB
    whole = lambda a: pl.BlockSpec(a.shape, lambda i: (0,) * a.ndim)
    rows = lambda w: pl.BlockSpec((QB, w), lambda i: (i, 0))
    cube = lambda r: pl.BlockSpec((1, r, width), lambda i: (i, 0, 0))
    out = lambda *s: jax.ShapeDtypeStruct(s, F32)
    return pl.pallas_call(
        second_kernel,
        grid=(count,),
        in_specs=[
            rows(width), rows(width), rows(wide), rows(wide),
            pl.BlockSpec((128, QB), lambda i: (0, i)),
            rows(128), cube(nst), cube(nst), cube(8), whole(start), rows(width), whole(dexp),
        ],
        out_specs=[rows(width), rows(width), cube(nst), pl.BlockSpec((2, QB), lambda i: (0, i))],
        out_shape=[out(length, width), out(length, width), out(count, nst, width), out(2, length)],
        compiler_params=pltpu.CompilerParams(vmem_limit_bytes=LIMIT),
        name="outputs_and_tangents",
    )(x, dx, bc, dbc, rowv, colv, st, dst, logs, start, gate_z, dexp)


def third_kernel(by, bc, colv, log, lam_o, msg_o, state, total):
    step = pl.program_id(0)
    nst = bc.shape[1] // 2
    heads = by.shape[1] // HW

    @pl.when(step == 0)
    def _():
        state[...] = jnp.zeros_like(state)
        total[...] = jnp.zeros_like(total)

    lam_o[0] = state[...]
    cols = colv[...]
    ct_h, ct_l = split(bc[:, nst:].T)
    for p in range(heads // 2):
        at = slice(128 * p, 128 * p + 128)
        lifted = jnp.exp(expand(cols, C_, p)) * by[:, at]
        l_h, l_l = split(lifted)
        add = nn(ct_h, l_h) + nn(ct_h, l_l) + nn(ct_l, l_h)
        state[:, at] = jnp.exp(log[0, 2:3, at]) * state[:, at] + add
    total[0:1, :] = total[0:1, :] + log[0, 2:3, :]

    @pl.when(step == pl.num_programs(0) - 1)
    def _():
        parts = msg_o.shape[0]
        width = state.shape[1]
        msg_o[:, 0:8, :] = state[...].reshape(parts, 8, width)
        msg_o[:, 8:16, :] = jnp.broadcast_to(total[...][None], (parts, 8, width))


def third_call(by, bc, colv, logs, parts):
    length, width = by.shape
    wide = bc.shape[1]
    nst = wide // 2
    count = length // QB
    rows = lambda w: pl.BlockSpec((QB, w), lambda i: (count - 1 - i, 0))
    cube = lambda r: pl.BlockSpec((1, r, width), lambda i: (count - 1 - i, 0, 0))
    out = lambda *s: jax.ShapeDtypeStruct(s, F32)
    return pl.pallas_call(
        third_kernel,
        grid=(count,),
        in_specs=[rows(width), rows(wide), rows(128), cube(8)],
        out_specs=[cube(nst), pl.BlockSpec((parts, 16, width), lambda i: (0, 0, 0))],
        out_shape=[out(count, nst, width), out(parts, 16, width)],
        scratch_shapes=[pltpu.VMEM((nst, width), F32), pltpu.VMEM((8, width), F32)],
        compiler_params=pltpu.CompilerParams(vmem_limit_bytes=LIMIT),
        name="adjoint_states",
    )(by, bc, colv, logs)


def fold(a):
    return jnp.sum(a.reshape(a.shape[0] // 8, 8, a.shape[1]), axis=0)


def fourth_kernel(
    by, x, gx, pre_x, halo_x, bc, gbc, pre_bc, halo_bc, rowv, colv, s0_b, lam_b, log, last_log,
    s_end, dexp,
    gcx_o, gcbc_o, lane_o, head_o,
    wx, wbc,
):
    step = pl.program_id(0)
    nst = bc.shape[1] // 2
    heads = x.shape[1] // HW

    @pl.when(step == 0)
    def _():
        gcx_o[...] = jnp.zeros_like(gcx_o)
        gcbc_o[...] = jnp.zeros_like(gcbc_o)
        lane_o[...] = jnp.zeros_like(lane_o)
        head_o[...] = jnp.zeros_like(head_o)

    load_window(wx, halo_x, pre_x, step == 0)
    load_window(wbc, halo_bc, pre_bc, step == 0)
    b_mat, c_mat = bc[:, :nst], bc[:, nst:]
    at_i = lax.broadcasted_iota(jnp.int32, (QB, QB), 1)
    at_j = lax.broadcasted_iota(jnp.int32, (QB, QB), 0)
    keep = at_i >= at_j
    inner_t = jnp.where(keep, nt3(b_mat, c_mat), 0.0)
    cols = colv[...]
    rows = rowv[...]
    mask = lane_mask()
    back_inner_t = jnp.zeros((QB, QB), F32)
    back_b = jnp.zeros((QB, nst), F32)
    back_c = jnp.zeros((QB, nst), F32)
    for p in range(heads // 2):
        at = slice(128 * p, 128 * p + 128)
        own, sig_own = log[0, 2:3, at], log[0, 4:5, at]
        reach = jnp.exp(last_log[0, 0:1, at] + last_log[0, 2:3, at] - log[0, 0:1, at] - own)
        s1 = lam_b[0, :, at] + reach * s_end[:, :, at].reshape(nst, 128)
        s0 = s0_b[0, :, at]
        byp, xp = by[:, at], x[:, at]
        size = expand(cols, S_, p)
        u = size * xp
        rhs_h, rhs_l = split(jnp.concatenate([byp, s1], axis=0))
        u_h, u_l = split(
            jnp.concatenate([jnp.where(mask, u, 0.0), jnp.where(mask, 0.0, u)], axis=0)
        )
        y_h, y_l = split(
            jnp.concatenate([jnp.where(mask, byp, 0.0), jnp.where(mask, 0.0, byp)], axis=0)
        )
        s0_h, s0_l = split(s0)
        mt_tt = nt(u_h, rhs_h) + nt(u_h, rhs_l) + nt(u_l, rhs_h)
        v_all = nt(y_h, s0_h) + nt(y_h, s0_l) + nt(y_l, s0_h)
        mats = []
        for s in range(2):
            h = 2 * p + s
            c_col, cs_col = bcast(cols, C_ + h), bcast(cols, CS_ + h)
            c_row = rows[C_ + h : C_ + h + 1, :]
            cs_row = rows[CS_ + h : CS_ + h + 1, :]
            c_end, cs_end = c_row[:, QB - 1 : QB], cs_row[:, QB - 1 : QB]
            back_mt = mt_tt[s * QB : s * QB + QB, :QB]
            tt = mt_tt[s * QB : s * QB + QB, QB:]
            v = v_all[s * QB : s * QB + QB]
            diff = jnp.minimum(c_row - c_col, 0.0)
            level = jnp.exp(diff)
            back_inner_t = back_inner_t + level * back_mt
            m_t = inner_t * level
            prod = m_t * back_mt
            lifted = jnp.exp(c_col) * v
            back_c = back_c + lifted
            lc = lifted * c_mat
            left = c_end - c_col
            to_end = jnp.exp(left)
            tb = to_end * tt
            back_b = back_b + tb
            tbb = tb * b_mat
            head_o[h, 0] = head_o[h, 0] + fold(prod * diff + lc * c_col + tbb * left)
            head_o[h, 1] = head_o[h, 1] + fold(
                prod * (cs_row - cs_col) + lc * cs_col + tbb * (cs_end - cs_col)
            )
            mats.append(jnp.concatenate([m_t, to_end * b_mat], axis=1))
        a_h, a_l = split(jnp.concatenate(mats, axis=0))
        wide = nn(a_h, jnp.concatenate([rhs_h, rhs_l], axis=1))
        back_u2 = wide[:, :128] + wide[:, 128:] + nn(a_l, rhs_h)
        back_u = jnp.where(mask, back_u2[:QB], back_u2[QB:])
        back_x = back_u * size + dexp[0:1, at] * byp
        carried = jnp.sum(s1 * s0, axis=0, keepdims=True) * jnp.exp(own)
        through = jnp.sum(expand(cols, SG_, p) * (back_u * xp), axis=0, keepdims=True)
        lane_o[0:1, at] = lane_o[0:1, at] + through
        lane_o[1:2, at] = lane_o[1:2, at] + carried * own
        lane_o[2:3, at] = lane_o[2:3, at] + carried * sig_own
        lane_o[3:4, at] = lane_o[3:4, at] + jnp.sum(byp * xp, axis=0, keepdims=True)
        back_z = back_x * gx[:, at]
        for k in range(4):
            gcx_o[k : k + 1, at] = gcx_o[k : k + 1, at] + jnp.sum(
                back_z * wx[5 + k : 5 + k + QB, at], axis=0, keepdims=True
            )
    back_inner_t = jnp.where(keep, back_inner_t, 0.0)
    back_b = back_b + nn3(back_inner_t, c_mat)
    back_c = back_c + nn3(back_inner_t.T, b_mat)
    back_zbc = jnp.concatenate([back_b, back_c], axis=1) * gbc[...]
    for k in range(4):
        gcbc_o[k : k + 1, :] = gcbc_o[k : k + 1, :] + jnp.sum(
            back_zbc * wbc[5 + k : 5 + k + QB, :], axis=0, keepdims=True
        )


def fourth_call(
    by, x, gx, pre_x, halo_x, bc, gbc, pre_bc, halo_bc, rowv, colv, s0, lam, logs, s_end, dexp
):
    length, width = by.shape
    wide = bc.shape[1]
    nst = wide // 2
    heads = width // HW
    count = length // QB
    whole = lambda a: pl.BlockSpec(a.shape, lambda i: (0,) * a.ndim)
    rows = lambda w: pl.BlockSpec((QB, w), lambda i: (i, 0))
    cube = lambda r: pl.BlockSpec((1, r, width), lambda i: (i, 0, 0))
    out = lambda *s: jax.ShapeDtypeStruct(s, F32)
    fixed = lambda *s: pl.BlockSpec(s, lambda i: (0,) * len(s))
    return pl.pallas_call(
        fourth_kernel,
        grid=(count,),
        in_specs=[
            rows(width), rows(width), rows(width), rows(width), whole(halo_x),
            rows(wide), rows(wide), rows(wide), whole(halo_bc),
            pl.BlockSpec((128, QB), lambda i: (0, i)), rows(128),
            cube(nst), cube(nst), cube(8),
            pl.BlockSpec((1, 8, width), lambda i: (count - 1, 0, 0)),
            whole(s_end), whole(dexp),
        ],
        out_specs=[fixed(8, width), fixed(8, wide), fixed(8, width), fixed(heads, 2, 8, 128)],
        out_shape=[out(8, width), out(8, wide), out(8, width), out(heads, 2, 8, 128)],
        scratch_shapes=[pltpu.VMEM((QB + 8, width), F32), pltpu.VMEM((QB + 8, wide), F32)],
        compiler_params=pltpu.CompilerParams(vmem_limit_bytes=LIMIT),
        name="adjoint_gradients",
    )(by, x, gx, pre_x, halo_x, bc, gbc, pre_bc, halo_bc, rowv, colv, s0, lam, logs, logs, s_end, dexp)


def on_device(
    pre_x, pre_bc, gate_z, dt_raw, conv_x, conv_bc, head_params, norm_gain, w_out,
    t_conv_x, t_conv_bc, t_heads, t_gain, t_wout,
):
    count = lax.axis_size("seq")
    width = pre_x.shape[1]
    heads = dt_raw.shape[0]
    channels = width * lax.axis_size("head") * 1.0
    tails = jnp.concatenate([pre_x[-8:], pre_bc[-8:]], axis=1)
    tails = lax.ppermute(tails, "seq", [(i, i + 1) for i in range(count - 1)]).astype(F32)
    halo_x, halo_bc = tails[:, :width], tails[:, width:]
    t_wout_all = lax.all_gather(t_wout, "seq", axis=1, tiled=True)
    hpc = jnp.concatenate([head_params, t_heads], axis=0).T
    dexp = jnp.repeat(jnp.stack([head_params[2], t_heads[2]]), HW, axis=1)
    x, dx, gx, bc, dbc, gbc, rowv, colv, st, dst, logs, msg = first_call(
        pre_x, halo_x, pre_bc, halo_bc, dt_raw, conv_x, t_conv_x, conv_bc, t_conv_bc, hpc, count
    )
    start = scan_call(msg, True, 1)
    gated, d_gated, s0, sums = second_call(
        x, dx, bc, dbc, rowv, colv, st, dst, logs, start, gate_z, dexp
    )
    sums = lax.psum(sums, "head")
    inv_rms = lax.rsqrt(sums[0] / channels + 1e-05)
    d_inv = -0.5 * inv_rms**3 * sums[1] / channels
    normed = (gated * inv_rms[:, None] * norm_gain).astype(BF16)
    d_normed = (
        (d_gated * inv_rms[:, None] + gated * d_inv[:, None]) * norm_gain
        + gated * inv_rms[:, None] * t_gain
    ).astype(BF16)
    partial_out = nn(d_normed, w_out) + nn(normed, t_wout_all)
    probe_part = lax.psum_scatter(partial_out, "head", scatter_dimension=0, tiled=True)
    probe_out = lax.all_gather(probe_part.astype(BF16), "head", axis=0, tiled=True)
    gn_wout = lax.psum_scatter(nn(normed.T, probe_out), "seq", scatter_dimension=1, tiled=True)
    back_normed = nt(probe_out, w_out)
    gain_part = jnp.sum(back_normed * gated * inv_rms[:, None], axis=0)
    weighted = back_normed * norm_gain
    mixed = lax.psum(jnp.sum(weighted * gated, axis=1), "head")
    gate = jax.nn.silu(gate_z.astype(F32))
    back_y = (weighted * inv_rms[:, None] - gated * (inv_rms**3 * mixed / channels)[:, None]) * gate
    lam, msg_back = third_call(back_y, bc, colv, logs, count)
    s_end = scan_call(msg_back, False, 2)
    gcx, gcbc, lanes, head_sums = fourth_call(
        back_y, x, gx, pre_x, halo_x, bc, gbc, pre_bc, halo_bc, rowv, colv, s0, lam, logs, s_end, dexp
    )
    per_head = jnp.sum(lanes[:4].reshape(4, heads, HW), axis=2)
    through_c = jnp.sum(head_sums, axis=(2, 3))
    log_rate = per_head[1] + through_c[:, 0]
    rate = jnp.exp(head_params[1])
    bias = per_head[0] - rate * (per_head[2] + through_c[:, 1])
    gn_heads = jnp.stack([bias, log_rate, per_head[3]])
    gn_conv_x, gn_heads, gn_gain = lax.psum((gcx[:4], gn_heads, gain_part), "seq")
    gn_conv_bc = lax.psum(gcbc[:4], ("seq", "head"))
    return (gn_conv_x, gn_conv_bc, gn_heads, gn_gain, gn_wout)


def solution(mesh):
    in_specs = (
        P("seq", "head"), P("seq", None), P("seq", "head"), P("head", "seq"), P(None, "head"),
        P(), P(None, "head"), P("head"), P("head", None), P(None, "head"), P(), P(None, "head"),
        P("head"), P("head", "seq"),
    )
    out_specs = (P(None, "head"), P(), P(None, "head"), P("head"), P("head", "seq"))
    return jax.shard_map(
        on_device, mesh=mesh, in_specs=in_specs, out_specs=out_specs, check_vma=False
    )
```

time: 1150 us -> 471 us (0.41); the launches traced: 1130 us -> 470 us
  local copies, waits for them, and re-layouts: 304 us -> 13.5 us
  matrix products: 252 us -> 43.7 us
  other arithmetic: 177 us -> 8.27 us
  blocking collectives: 314 us -> 161 us
  Pallas kernels: 0 us -> 127 us
  waiting for transfers between devices: 48 us -> 98.5 us
  loops' own time: 13 us -> 0 us
    dot_general x101 -> x4, matrix products: 252 us -> 43.7 us  [the longest x3 34.5 us: nn(): return jnp.dot(a, b, preferred_element_type=F32)]
    dynamic_update_slice x24 -> x0, local copies, waits for them, and re-layouts: 196 us -> none  [ssd_scan(): lax.scan(jax.checkpoint(stepper), start_state, (x_blocks, b_blocks, c_blo...]
    pallas_call x0 -> x6, Pallas kernels: none -> 127 us  [the longest x2 65.3 us: scan_call(): pl.pallas_call(kernel, in_specs=[vmem], out_specs=vmem, out_shape=jax.Sha...]
    psum x4 -> x3, blocking collectives: 261 us -> 147 us  [the longest x1 72.3 us: on_device(): lax.psum((gcx[:4], gn_heads, gain_part), 'seq')]
    select_n x45 -> x0, other arithmetic: 73.8 us -> none  [step(): jnp.where(position < mine, new, old)]
    reduce_scatter x1 -> x2, waiting for transfers between devices: 0.01 us -> 61.8 us  [the longest x1 61.8 us: on_device(): lax.psum_scatter(partial_out, 'head', scatter_dimension=0, tiled=True)]
    another operation x68 -> x2, other arithmetic: 40.1 us -> 0.02 us  [the longest x1 0.01 us: on_device(): gn_heads = jnp.stack([bias, log_rate, per_head[3]])]
    unnamed x1 -> x0, blocking collectives: 37.4 us -> none
  transfers between devices with their start and end apart: 7 -> 5, of which waited for: 2 -> 2; matrix products, arithmetic and copies ran while one was open for 32% -> 7% of each run, Pallas kernels for 0% -> 27%
where the time goes in v1:
time: 471 us; the launch traced here: 470 us
  blocking collectives  161 us (34%)
  Pallas kernels  127 us (27%)
  waiting for transfers between devices  98.5 us (21%)
  matrix products  43.7 us (9%)
  between operations  14 us (3%)
  local copies, waits for them, and re-layouts  13.5 us (3%)
  other arithmetic  8.27 us (2%)
    psum x1, blocking collectives, on_device(): lax.psum((gcx[:4], gn_heads, gain_part), 'seq')  72.3 us
    pallas_call x2, Pallas kernels, scan_call(): pl.pallas_call(kernel, in_specs=[vmem], out_specs=vmem, out_shape=jax.Sha...  65.3 us
    psum x1, blocking collectives, on_device(): gn_conv_bc = lax.psum(gcbc[:4], ('seq', 'head'))  62.2 us
    reduce_scatter x1, waiting for transfers between devices, on_device(): lax.psum_scatter(partial_out, 'head', scatter_dimension=0, tiled=True)  61.8 us
    all_gather x1, waiting for transfers between devices, on_device(): lax.all_gather(probe_part.astype(BF16), 'head', axis=0, tiled=True)  36 us
    dot_general x3, matrix products, nn(): return jnp.dot(a, b, preferred_element_type=F32)  34.5 us
    pallas_call x1, Pallas kernels, fourth_call(): pl.pallas_call(fourth_kernel, grid=(count,), in_specs=[rows(width), rows(...  21 us
    pallas_call x1, Pallas kernels, second_call(): pl.pallas_call(second_kernel, grid=(count,), in_specs=[rows(width), rows(...  16.8 us
  transfers between devices with their start and end apart: 5, of which 2 were waited for; matrix products, arithmetic and copies ran while one was open for 7% of the time, Pallas kernels for 27%

profile of v1, /device:TPU:0, one launch (start us, length us, event | category | flops | bytes accessed | tf_op | source)
XLA Modules:
  0.0 470.2 jit_solution(4330423866194401821)
XLA Ops:
  7.2 0.0 copy-start
  7.2 0.0 all-gather.3.cloned.1.call-start
  7.2 0.7 all-gather.3.cloned.1.call-update
  7.9 0.0 reduce-scatter.3.cloned.1.call-start
  8.0 0.9 slice.54
  8.9 0.7 slice.55
  9.6 3.9 collective-permute-start
  13.5 0.8 copy.25
  14.2 0.7 slice.58
  14.9 0.8 copy.26
  15.7 0.7 slice.59
  16.4 0.1 maximum_bitcast_fusion.hpc
  16.5 0.1 broadcast_in_dim.2
  16.5 0.1 reshape.45.dexp
  16.6 0.0 collective-permute-done
  16.6 0.0 copy-start.5
  16.6 1.0 copy-done.5
  17.7 0.8 copy-done.10
  18.5 0.7 copy-done.13
  19.2 0.7 copy-done.14
  19.9 0.7 copy-done.16
  20.6 0.7 copy-done.17
  21.3 16.0 %conv_and_states.1 = (f32[1024,640]{1,0:T(8,128)}, f32[1024,640]{1,0:T(8,128)}, f32[1024,640]{1,0:T(8,128)}, f32[1024,256]{1,0:T(8,128)S(1)}, f32[1024,256]{1,0:...) custom-call(bf16[1024,640]{1,0:T(8,128)(2,1)} %pre_x.3, ...), custom_call_target="tpu_custom_call" | custom-call | tf_op jit(solution)/shard_map/conv_and_states/pallas_call | solution.py:190
  37.3 0.0 copy-start.7
  37.3 38.8 %state_scan_forward.1.start = f32[16,16,640]{2,1,0:T(8,128)S(1)} custom-call(f32[16,24,640]{2,1,0:T(8,128)S(1)} %get-tuple-element.36.refs_0_), custom_call_target="tpu_custom_call" | custom-call | tf_op jit(solution)/shard_map/state_scan_forward/pallas_call | solution.py:281
  76.1 0.0 copy-start.9
  76.1 1.2 copy-done.9
  77.3 16.8 %outputs_and_tangents.1 = (f32[1024,640]{1,0:T(8,128)}, f32[1024,640]{1,0:T(8,128)}, f32[8,128,640]{2,1,0:T(8,128)}, f32[2,1024]{1,0:T(2,128)S(1)}) custom-call(f32[1024,640]{1,0:T(8,128)} %get-tuple-element.27.x, f32[1024,640]{1,0:T(8,128)} %get-tuple-element.28.dx, f32[1024,256]{1,0:T(8,128)S(1)} %get-tuple-element.29.bc, f32[1024,256]{1,0:T(8,128)S(1)} %copy-done.9, ...), custom_call_target="tpu_custom_call" | custom-call | tf_op jit(solution)/shard_map/outputs_and_tangents/pallas_call | solution.py:387
  94.1 0.0 copy-done.11
  94.1 0.0 copy-done.1
  94.2 12.7 %psum.42 = f32[2,1024]{1,0:T(2,128)S(1)} all-reduce(f32[2,1024]{1,0:T(2,128)S(1)} %get-tuple-element.38), channel_id=1, replica_groups=mesh['seq'=16,'head'=8] {'head'}, use_global_device_ids=true, to_apply=%region_0.0 | all-reduce | flops 2048 | bytes 16384 | tf_op jit(solution)/shard_map/psum | solution.py:611
  106.9 10.1 %fusion.4 = f32[1024,2560]{1,0:T(8,128)} fusion(bf16[640,2560]{1,0:T(8,128)(2,1)S(1)} %copy-done, f32[1024,640]{1,0:T(8,128)} %get-tuple-element.39, f32[1024,640]{1,0:T(8,128)} %get-tuple-element.37, f32[640]{0:T(1024)S(1)} %copy-done.20, f32[640]{0:T(1024)S(1)} %copy-done.19, f32[1024]{0:T(1024)S(1)} %multiply_multiply_fusion.2, f32[1024]{0:T(1024)S(1)} %bitcast.18), kind=kOutput, calls=%fused_computation.11 | convolution fusion | flops 3360686080 | bytes 19018752 | tf_op jit(solution)/shard_map/dot_general | solution.py:23
  117.0 14.0 %convolution_add_fusion = f32[1024,2560]{1,0:T(8,128)} fusion(f32[1024,2560]{1,0:T(8,128)} %fusion.4, bf16[640,2560]{0,1:T(8,128)(2,1)} %all-gather.3.cloned.1.call-done, f32[1024,640]{1,0:T(8,128)} %get-tuple-element.39, f32[640]{0:T(1024)S(1)} %copy-done.19, f32[1024]{0:T(1024)S(1)} %bitcast.19), kind=kOutput, calls=%fused_computation | convolution fusion | flops 3360030720 | bytes 26876416 | tf_op jit(solution)/shard_map/dot_general | solution.py:23
  131.0 0.0 reduce-scatter.3.cloned.1.call-update
  131.0 0.0 all-gather.5.cloned.1.call-start
  131.1 61.8 %reduce-scatter.3.cloned.1.call-done = f32[128,2560]{1,0:T(8,128)} async-done(((f32[1024,2560]{1,0:T(8,128)}), f32[128,2560]{1,0:T(8,128)}) %reduce-scatter.3.cloned.1.call-update) | async-done | bytes 1310736 | tf_op jit(solution)/shard_map/reduce_scatter | solution.py:620
  192.8 2.2 convert_element_type.18
  195.1 0.0 all-gather.5.cloned.1.call-update
  195.1 0.2 reduce-scatter.5.cloned.1.call-start
  195.3 36.0 %all-gather.5.cloned.1.call-done = bf16[1024,2560]{1,0:T(8,128)(2,1)} async-done(((bf16[128,2560]{1,0:T(8,128)(2,1)}), bf16[1024,2560]{1,0:T(8,128)(2,1)}) %all-gather.5.cloned.1.call-update) | async-done | bytes 5242896 | tf_op jit(solution)/shard_map/all_gather | solution.py:621
  231.4 10.4 %fusion.13 = f32[640,2560]{0,1:T(8,128)} fusion(bf16[1024,2560]{1,0:T(8,128)(2,1)} %all-gather.5.cloned.1.call-done, f32[1024,640]{1,0:T(8,128)} %get-tuple-element.39, f32[640]{0:T(1024)S(1)} %copy-done.19, f32[1024]{0:T(1024)S(1)} %bitcast.20), kind=kOutput, calls=%fused_computation.32 | convolution fusion | flops 3357409280 | bytes 14424576 | tf_op jit(solution)/shard_map/dot_general | solution.py:23
  241.8 0.0 reduce-scatter.5.cloned.1.call-update
  241.8 9.2 %multiply_reduce_fusion = (f32[640]{0:T(1024)S(1)}, f32[1024]{0:T(1024)S(1)}, f32[1024,640]{1,0:T(8,128)}) fusion(f32[1024,640]{1,0:T(8,128)} %get-tuple-element.39, f32[1024]{0:T(1024)S(1)} %bitcast.21, f32[640]{0:T(1024)S(1)} %copy-done.19, bf16[1024,2560]{1,0:T(8,128)(2,1)} %all-gather.5.cloned.1.call-done, bf16[640,2560]{1,0:T(8,128)(2,1)S(1)} %copy-done), kind=kOutput, calls=%fused_computation.7 | convolution fusion | flops 3359373824 | bytes 13775872 | tf_op jit(solution)/shard_map/dot_general | solution.py:27
  251.0 13.9 %psum.43 = f32[1024]{0:T(1024)S(1)} all-reduce(f32[1024]{0:T(1024)S(1)} %get-tuple-element.50), channel_id=1, replica_groups=mesh['seq'=16,'head'=8] {'head'}, use_global_device_ids=true, to_apply=%region_3.0 | all-reduce | flops 1024 | bytes 8192 | tf_op jit(solution)/shard_map/psum | solution.py:626
  264.9 5.0 %fusion.3.by = f32[1024,640]{1,0:T(8,128)} fusion(bf16[1024,640]{1,0:T(8,128)(2,1)} %gate_z.1, f32[1024,640]{1,0:T(8,128)} %get-tuple-element.39, f32[1024,640]{1,0:T(8,128)} %get-tuple-element.61, f32[1024]{0:T(1024)S(1)} %multiply_multiply_fusion.1, f32[640]{0:T(1024)S(1)} %copy-done.19, f32[1024]{0:T(1024)S(1)} %bitcast.23), kind=kLoop, calls=%fused_computation.6 | loop fusion | flops 6553600 | bytes 9185792 | tf_op jit(solution)/shard_map/mul | solution.py:628
  269.9 0.0 copy-done.2
  269.9 0.0 copy-start.12
  269.9 7.9 %adjoint_states.1 = (f32[8,128,640]{2,1,0:T(8,128)}, f32[16,16,640]{2,1,0:T(8,128)S(1)}) custom-call(f32[1024,640]{1,0:T(8,128)} %fusion.3.by, f32[1024,256]{1,0:T(8,128)S(1)} %copy-done.2, f32[1024,128]{1,0:T(8,128)S(1)} %copy-done.4, f32[8,8,640]{2,1,0:T(8,128)S(1)} %get-tuple-element.35.log.last_log), custom_call_target="tpu_custom_call" | custom-call | tf_op jit(solution)/shard_map/adjoint_states/pallas_call | solution.py:439
  277.8 26.5 %state_scan_backward.1.s_end = f32[16,8,640]{2,1,0:T(8,128)S(1)} custom-call(f32[16,16,640]{2,1,0:T(8,128)S(1)} %get-tuple-element.44.refs_0_), custom_call_target="tpu_custom_call" | custom-call | tf_op jit(solution)/shard_map/state_scan_backward/pallas_call | solution.py:281
  304.4 0.0 copy-done.6
  304.4 0.0 copy-done.8
  304.4 0.0 copy-done.12
  304.4 21.0 %adjoint_gradients.1 = (f32[8,640]{1,0:T(8,128)S(1)}, f32[8,256]{1,0:T(8,128)S(1)}, f32[8,640]{1,0:T(8,128)S(1)}, f32[10,2,8,128]{3,2,1,0:T(8,128)S(1)}) custom-call(f32[1024,640]{1,0:T(8,128)} %fusion.3.by, f32[1024,640]{1,0:T(8,128)} %get-tuple-element.27.x, f32[1024,640]{1,0:T(8,128)} %get-tuple-element.40.gx, bf16[1024,640]{1,0:T(8,128)(2,1)} %pre_x.3, ...), custom_call_target="tpu_custom_call" | custom-call | tf_op jit(solution)/shard_map/adjoint_gradients/pallas_call | solution.py:571
  325.4 0.6 copy-done.15
  326.0 0.6 copy-done.18
  326.6 0.1 reshape.46
  326.7 0.1 reduce_sum.37
  326.7 0.1 reduce_sum.38
  326.9 0.7 slice.62
  327.6 0.7 slice.63
  328.3 62.2 %psum.45 = f32[4,256]{1,0:T(4,128)} all-reduce(f32[4,256]{1,0:T(4,128)S(1)} %slice.63), channel_id=1, replica_groups=mesh['seq'=16,'head'=8] {'seq','head'}, use_global_device_ids=true, to_apply=%region_5.0 | all-reduce | flops 1024 | bytes 8192 | tf_op jit(solution)/shard_map/psum | solution.py:641
  390.5 0.2 slice_reduce_fusion.1
  390.7 0.7 fusion.12
  391.4 72.3 %all-reduce = (f32[4,640]{1,0:T(4,128)}, f32[3,10]{1,0:T(4,128)}, f32[640]{0:T(1024)}) all-reduce(f32[4,640]{1,0:T(4,128)S(1)} %slice.62, f32[3,10]{1,0:T(4,128)S(1)} %pad_maximum_fusion.1, f32[640]{0:T(1024)S(1)} %get-tuple-element.49), channel_id=1, replica_groups=mesh['seq'=16,'head'=8] {'seq'}, use_global_device_ids=true, to_apply=%region_4.0 | all-reduce | flops 3230 | bytes 25840 | tf_op jit(solution)/shard_map/psum | solution.py:640
  (33 shorter events, 0.1 us)
Async XLA Ops:
  7.2 99.7 %copy-start = (bf16[640,2560]{1,0:T(8,128)(2,1)S(1)}, bf16[640,2560]{1,0:T(8,128)(2,1)}, u32[]{:S(2)}) copy-start(bf16[640,2560]{1,0:T(8,128)(2,1)} %param.22) | copy-start | bytes 9830404
  7.2 109.8 %all-gather.3.cloned.1.call-start = ((), (), s32[]{:S(2)}) async-start(), calls=%async_computation.2 | async-start | bytes 3481600 | tf_op jit(solution)/shard_map/all_gather | solution.py:601
  7.9 184.9 %reduce-scatter.3.cloned.1.call-start = ((), (), s32[]{:S(2)}) async-start(), calls=%async_computation.3 | async-start | bytes 11796480 | tf_op jit(solution)/shard_map/reduce_scatter | solution.py:620
  9.6 7.1 %collective-permute-start = (bf16[8,896]{1,0:T(8,128)(2,1)S(1)}, bf16[8,896]{1,0:T(8,128)(2,1)S(1)}, u32[]{:S(2)}, u32[]{:S(2)}) collective-permute-start(bf16[8,896]{1,0:T(8,128)(2,1)S(1)} %pad_maximum_fusion), channel_id=1, source_target_pairs={{0,8},{8,16},{16,24},{24,32},{32,40},{40,48},{48,56},{56,64},{64,7... | collective-permute-start | bytes 43016 | tf_op jit(solution)/shard_map/ppermute | solution.py:599
  16.6 77.5 %copy-start.11 = (f32[2,640]{1,0:T(2,128)}, f32[2,640]{1,0:T(2,128)S(1)}, u32[]{:S(2)}) copy-start(f32[2,640]{1,0:T(2,128)S(1)} %reshape.45.dexp) | copy-start | bytes 15364
  16.6 1.0 copy-start.5
  17.7 0.8 copy-start.10
  18.5 0.7 copy-start.13
  19.2 0.7 copy-start.14
  19.9 0.7 copy-start.16
  20.6 0.7 copy-start.17
  37.3 56.8 %copy-start.1 = (f32[1024,256]{1,0:T(8,128)}, f32[1024,256]{1,0:T(8,128)S(1)}, u32[]{:S(2)}) copy-start(f32[1024,256]{1,0:T(8,128)S(1)} %get-tuple-element.29.bc) | copy-start | bytes 3145732
  37.3 56.9 %copy-start.3 = (f32[1024,128]{1,0:T(8,128)}, f32[1024,128]{1,0:T(8,128)S(1)}, u32[]{:S(2)}) copy-start(f32[1024,128]{1,0:T(8,128)S(1)} %get-tuple-element.32.colv) | copy-start | bytes 1572868
  37.3 56.9 %copy-start.7 = (f32[128,1024]{1,0:T(8,128)}, f32[128,1024]{1,0:T(8,128)S(1)}, u32[]{:S(2)}) copy-start(f32[128,1024]{1,0:T(8,128)S(1)} %get-tuple-element.31.rowv) | copy-start | bytes 1572868
  76.1 1.2 copy-start.9
  77.3 29.6 %copy-start.19 = (f32[640]{0:T(1024)S(1)}, f32[640]{0:T(1024)}, u32[]{:S(2)}) copy-start(f32[640]{0:T(1024)} %param.21) | copy-start | bytes 7684
  77.3 29.6 %copy-start.20 = (f32[640]{0:T(1024)S(1)}, f32[640]{0:T(1024)}, u32[]{:S(2)}) copy-start(f32[640]{0:T(1024)} %param.26) | copy-start | bytes 7684
  131.0 100.3 %all-gather.5.cloned.1.call-start = ((), (), s32[]{:S(2)}) async-start(), calls=%async_computation.4 | async-start | bytes 5898240 | tf_op jit(solution)/shard_map/all_gather | solution.py:621
  195.1 268.6 %reduce-scatter.5.cloned.1.call-start = ((), (), s32[]{:S(2)}) async-start(), calls=%async_computation.5 | async-start | bytes 6963200 | tf_op jit(solution)/shard_map/reduce_scatter | solution.py:622
  264.9 5.0 %copy-start.2 = (f32[1024,256]{1,0:T(8,128)S(1)}, f32[1024,256]{1,0:T(8,128)}, u32[]{:S(2)}) copy-start(f32[1024,256]{1,0:T(8,128)} %copy-done.1) | copy-start | bytes 3145732
  264.9 5.0 %copy-start.4 = (f32[1024,128]{1,0:T(8,128)S(1)}, f32[1024,128]{1,0:T(8,128)}, u32[]{:S(2)}) copy-start(f32[1024,128]{1,0:T(8,128)} %copy-done.3) | copy-start | bytes 1572868
  269.9 34.5 %copy-start.6 = (bf16[1024,256]{1,0:T(8,128)(2,1)S(1)}, bf16[1024,256]{1,0:T(8,128)(2,1)}, u32[]{:S(2)}) copy-start(bf16[1024,256]{1,0:T(8,128)(2,1)} %pre_bc.3) | copy-start | bytes 1572868
  269.9 34.5 %copy-start.8 = (f32[128,1024]{1,0:T(8,128)S(1)}, f32[128,1024]{1,0:T(8,128)}, u32[]{:S(2)}) copy-start(f32[128,1024]{1,0:T(8,128)} %copy-done.7) | copy-start | bytes 1572868
  269.9 34.5 %copy-start.12 = (f32[2,640]{1,0:T(2,128)S(1)}, f32[2,640]{1,0:T(2,128)}, u32[]{:S(2)}) copy-start(f32[2,640]{1,0:T(2,128)} %copy-done.11) | copy-start | bytes 15364
  325.4 0.6 copy-start.15
  326.0 0.6 copy-start.18
Sparse Core Ops, SparseCore 0:
  10.2 67.2 all-gather.2
  131.1 61.6 reduce-scatter.2
  195.2 36.1 all-gather.4
  241.9 92.7 reduce-scatter.4

commit v2 on v1

--- a/solution.py
+++ b/solution.py
@@ -81,7 +81,7 @@
 
 def first_kernel(
     pre_x, halo_x, pre_bc, halo_bc, dt, cx, tcx, cbc, tcbc, hpc,
-    x_o, dx_o, gx_o, bc_o, dbc_o, gbc_o, row_o, col_o, st_o, dst_o, log_o, msg_o,
+    x_o, dx_o, gx_o, bc_o, dbc_o, gbc_o, row_o, col_o, st_o, dst_o, log_o, msg_o, tile_o,
     wx, wbc, feat, state, d_state, logs,
 ):
     step = pl.program_id(0)
@@ -94,6 +94,7 @@
         d_state[...] = jnp.zeros_like(d_state)
         logs[...] = jnp.zeros_like(logs)
         feat[...] = jnp.zeros_like(feat)
+        tile_o[...] = jnp.zeros_like(tile_o)
 
     load_window(wx, halo_x, pre_x, step == 0)
     load_window(wbc, halo_bc, pre_bc, step == 0)
@@ -136,6 +137,7 @@
     gx_o[...] = gx
 
     last = cols[QB - 1 : QB, :]
+    tile_o[0:1, :] = tile_o[0:1, :] + last
     own = expand_all(last, C_, heads)
     d_own = expand_all(last, DC_, heads)
     sig_own = expand_all(last, CS_, heads)
@@ -174,7 +176,6 @@
         width = state.shape[1]
         msg_o[:, 0:8, :] = state[...].reshape(parts, 8, width)
         msg_o[:, 8:16, :] = d_state[...].reshape(parts, 8, width)
-        msg_o[:, 16:24, :] = jnp.broadcast_to(logs[...][None], (parts, 8, width))
 
 
 def first_call(pre_x, halo_x, pre_bc, halo_bc, dt, cx, tcx, cbc, tcbc, hpc, parts):
@@ -198,12 +199,13 @@
         out_specs=[rows(width)] * 3 + [rows(wide)] * 3 + [
             pl.BlockSpec((128, QB), lambda i: (0, i)),
             rows(128), cube(nst), cube(nst), cube(8),
-            pl.BlockSpec((parts, 24, width), lambda i: (0, 0, 0)),
+            pl.BlockSpec((parts, 16, width), lambda i: (0, 0, 0)),
+            pl.BlockSpec((8, 128), lambda i: (0, 0)),
         ],
         out_shape=[out(length, width)] * 3 + [out(length, wide)] * 3 + [
             out(128, length), out(length, 128),
             out(count, nst, width), out(count, nst, width), out(count, 8, width),
-            out(parts, 24, width),
+            out(parts, 16, width), out(8, 128),
         ],
         scratch_shapes=[
             pltpu.VMEM((QB + 8, width), F32), pltpu.VMEM((QB + 8, wide), F32),
@@ -215,87 +217,432 @@
     )(pre_x, halo_x, pre_bc, halo_bc, dt, cx, tcx, cbc, tcbc, hpc)
 
 
-def scan_kernel(count, forward, msg, result, landed, answer, send1, recv1, send2, recv2):
+def greet(peers):
+    barrier = pltpu.get_barrier_semaphore()
+    for peer in peers:
+        pl.semaphore_signal(barrier, inc=1, device_id=peer, device_id_type=MESH)
+    pl.semaphore_wait(barrier, len(peers))
+
+
+def others(axis, count):
+    me = lax.axis_index(axis)
+    return [lax.rem(me + k, count) for k in range(1, count)]
+
+
+def send(src, dst, send_sem, recv_sem, device):
+    copy = pltpu.make_async_remote_copy(
+        src_ref=src, dst_ref=dst, send_sem=send_sem, recv_sem=recv_sem,
+        device_id=device, device_id_type=MESH,
+    )
+    copy.start()
+    return copy
+
+
+def scan_forward_kernel(
+    msg, tile, result, decay_o, landed, tiles, answer, send0, recv0, send1, recv1, send2, recv2
+):
+    count = msg.shape[0]
+    width = msg.shape[2]
+    heads = width // HW
     me = lax.axis_index("seq")
-    barrier = pltpu.get_barrier_semaphore()
-    for k in range(1, count):
-        pl.semaphore_signal(
-            barrier, inc=1, device_id={"seq": lax.rem(me + k, count)}, device_id_type=MESH
-        )
-    pl.semaphore_wait(barrier, count - 1)
-    first = []
-    for k in range(1, count):
-        to = lax.rem(me + k, count)
-        copy = pltpu.make_async_remote_copy(
-            src_ref=msg.at[to],
-            dst_ref=landed.at[me],
-            send_sem=send1.at[k],
-            recv_sem=recv1.at[k],
-            device_id={"seq": to},
-            device_id_type=MESH,
-        )
-        copy.start()
-        first.append(copy)
+    peers = others("seq", count)
+    greet([{"seq": to} for to in peers])
+    copies = []
+    for k, to in enumerate(peers):
+        at = {"seq": to}
+        copies.append(send(tile, tiles.at[me], send0.at[k], recv0.at[k], at))
+        copies.append(send(msg.at[to], landed.at[me], send1.at[k], recv1.at[k], at))
     landed[me] = msg[me]
-    for copy in first:
+    tiles[me] = tile[...]
+    for copy in copies:
         copy.wait()
-    width = msg.shape[2]
     state = jnp.zeros((8, width), F32)
     d_state = jnp.zeros((8, width), F32)
-    for i in range(count) if forward else range(count - 1, -1, -1):
-        if forward:
-            answer[i, 0:8] = state
-            answer[i, 8:16] = d_state
-            decay = jnp.exp(landed[i, 16:17])
-            d_state = decay * (d_state + landed[i, 17:18] * state) + landed[i, 8:16]
-        else:
-            answer[i] = state
-            decay = jnp.exp(landed[i, 8:9])
+    for i in range(count):
+        answer[i, 0:8] = state
+        answer[i, 8:16] = d_state
+        features = tiles[i, 0:1, :]
+        decay = jnp.exp(expand_all(features, C_, heads))
+        decay_o[i : i + 1, :] = decay
+        d_state = decay * (d_state + expand_all(features, DC_, heads) * state)
+        d_state = d_state + landed[i, 8:16]
         state = decay * state + landed[i, 0:8]
-    second = []
-    for k in range(1, count):
-        to = lax.rem(me + k, count)
-        copy = pltpu.make_async_remote_copy(
-            src_ref=answer.at[to],
-            dst_ref=result.at[me],
-            send_sem=send2.at[k],
-            recv_sem=recv2.at[k],
-            device_id={"seq": to},
-            device_id_type=MESH,
+    copies = []
+    for k, to in enumerate(peers):
+        copies.append(
+            send(answer.at[to], result.at[me], send2.at[k], recv2.at[k], {"seq": to})
         )
-        copy.start()
-        second.append(copy)
     result[me] = answer[me]
-    for copy in second:
+    for copy in copies:
         copy.wait()
 
 
-def scan_call(msg, forward, collective_id):
+def scan_backward_kernel(msg, decays, result, landed, answer, send1, recv1, send2, recv2):
+    count = msg.shape[0]
+    width = msg.shape[2]
+    me = lax.axis_index("seq")
+    peers = others("seq", count)
+    greet([{"seq": to} for to in peers])
+    copies = []
+    for k, to in enumerate(peers):
+        copies.append(send(msg.at[to], landed.at[me], send1.at[k], recv1.at[k], {"seq": to}))
+    landed[me] = msg[me]
+    for copy in copies:
+        copy.wait()
+    state = jnp.zeros((8, width), F32)
+    for i in range(count - 1, -1, -1):
+        answer[i] = state
+        state = decays[i : i + 1, :] * state + landed[i]
+    copies = []
+    for k, to in enumerate(peers):
+        copies.append(
+            send(answer.at[to], result.at[me], send2.at[k], recv2.at[k], {"seq": to})
+        )
+    result[me] = answer[me]
+    for copy in copies:
+        copy.wait()
+
+
+VMEM = pl.BlockSpec(memory_space=pltpu.VMEM)
+
+
+def scan_forward(msg, tile):
     parts, rows, width = msg.shape
-    back = 16 if forward else 8
-    vmem = pl.BlockSpec(memory_space=pltpu.VMEM)
-
-    def kernel(*refs):
-        scan_kernel(parts, forward, *refs)
-
+    sems = [pltpu.SemaphoreType.DMA((parts,))] * 6
     return pl.pallas_call(
-        kernel,
-        in_specs=[vmem],
-        out_specs=vmem,
-        out_shape=jax.ShapeDtypeStruct((parts, back, width), F32),
+        scan_forward_kernel,
+        in_specs=[VMEM] * 2,
+        out_specs=[VMEM] * 2,
+        out_shape=[
+            jax.ShapeDtypeStruct((parts, rows, width), F32),
+            jax.ShapeDtypeStruct((parts, width), F32),
+        ],
         scratch_shapes=[
             pltpu.VMEM((parts, rows, width), F32),
-            pltpu.VMEM((parts, back, width), F32),
-            pltpu.SemaphoreType.DMA((parts,)),
-            pltpu.SemaphoreType.DMA((parts,)),
-            pltpu.SemaphoreType.DMA((parts,)),
-            pltpu.SemaphoreType.DMA((parts,)),
+            pltpu.VMEM((parts, 8, 128), F32),
+            pltpu.VMEM((parts, rows, width), F32),
+        ]
+        + sems,
+        compiler_params=pltpu.CompilerParams(
+            collective_id=1, has_side_effects=True, vmem_limit_bytes=LIMIT
+        ),
+        name="state_scan_forward",
+    )(msg, tile)
+
+
+def scan_backward(msg, decays):
+    parts, rows, width = msg.shape
+    sems = [pltpu.SemaphoreType.DMA((parts,))] * 4
+    return pl.pallas_call(
+        scan_backward_kernel,
+        in_specs=[VMEM] * 2,
+        out_specs=VMEM,
+        out_shape=jax.ShapeDtypeStruct((parts, rows, width), F32),
+        scratch_shapes=[pltpu.VMEM((parts, rows, width), F32)] * 2 + sems,
+        compiler_params=pltpu.CompilerParams(
+            collective_id=2, has_side_effects=True, vmem_limit_bytes=LIMIT
+        ),
+        name="state_scan_backward",
+    )(msg, decays)
+
+
+def middle_kernel(
+    gated, dgated, sums, gate_z, w, tw, gain, tgain,
+    by_o, gnw_o, gain_o,
+    got, scal, both, part, sib, far_src, far_dst, out_src, out_dst, probe, back, mix, mix_got,
+    sums_s, sums_r, sib_s, sib_r, far_s, far_r, out_s, out_r, ag_s, ag_r, mix_s, mix_r,
+):
+    length, width = gated.shape
+    cols = w.shape[1]
+    half = cols // 2
+    groups = width // 128
+    channels = width * 8.0
+    head = lax.axis_index("head")
+    mine = head // 2
+    core = lax.rem(head, 2)
+    right, left, far = (lax.rem(mine + k, 4) for k in (1, 3, 2))
+    device = lambda chip, c: {"head": chip * 2 + c}
+    to_right, to_left, to_sib = device(right, core), device(left, core), device(mine, 1 - core)
+    peers = others("head", 8)
+    greet([{"head": to} for to in peers])
+    copies = []
+    for k, to in enumerate(peers):
+        copies.append(send(sums, got.at[head], sums_s.at[k], sums_r.at[k], {"head": to}))
+    got[head] = sums[...]
+    gain_o[...] = jnp.zeros_like(gain_o)
+    for copy in copies:
+        copy.wait()
+    total = got[0]
+    for i in range(1, 8):
+        total = total + got[i]
+    inv = lax.rsqrt(total[0:1] / channels + 1e-05)
+    scal[0:1] = inv
+    scal[1:2] = -0.5 * inv * inv * inv * total[1:2] / channels
+
+    def column(row, start):
+        at = pl.ds(pl.multiple_of(start, 128), 128)
+        return jnp.broadcast_to(scal[row : row + 1, at], (128, 128)).T
+
+    def compute(index, chip):
+        slot = index % 2
+        for c in range(2):
+            start = pl.multiple_of(chip * 256 + c * 128, 128)
+            rows = pl.ds(start, 128)
+            inv_c, d_inv_c = column(0, start), column(1, start)
+            for g in range(groups):
+                at = slice(128 * g, 128 * g + 128)
+                gt, dgt = gated[rows, at], dgated[rows, at]
+                ga = gain[:, at]
+                scaled = gt * inv_c
+                normed = scaled * ga
+                d_normed = (dgt * inv_c + gt * d_inv_c) * ga + scaled * tgain[:, at]
+                both[rows, at] = d_normed.astype(BF16)
+                both[rows, width + 128 * g : width + 128 * g + 128] = normed.astype(BF16)
+        rows = pl.ds(pl.multiple_of(chip * 256, 256), 256)
+
+        def tile(i, carry):
+            at = pl.ds(pl.multiple_of(i * 512, 512), 512)
+            res = nn(both[rows, 0:width], w[:, at]) + nn(both[rows, width:], tw[:, at])
+            part[slot, 0, :, at] = res[:128]
+            part[slot, 1, :, at] = res[128:]
+            return carry
+
+        lax.fori_loop(0, cols // 512, tile, 0)
+        return send(
+            part.at[slot, 1 - core], sib.at[index], sib_s.at[index], sib_r.at[index], to_sib
+        )
+
+    def pair(index, h):
+        at = slice(half * h, half * h + half)
+        return part[index % 2, core, :, at] + sib[index, :, at]
+
+    first = compute(0, far)
+    second = compute(1, right)
+    first.wait()
+    far_src[0] = pair(0, 0).astype(BF16)
+    far_src[1] = pair(0, 1).astype(BF16)
+    far_l = send(far_src.at[0], far_dst.at[0], far_s.at[0], far_r.at[0], to_right)
+    far_rt = send(far_src.at[1], far_dst.at[1], far_s.at[1], far_r.at[1], to_left)
+    third = compute(2, left)
+    second.wait()
+    out_src[0, 1] = pair(1, 1).astype(BF16)
+    out_rr = send(out_src.at[0, 1], out_dst.at[0, 1], out_s.at[0], out_r.at[0], to_right)
+    far_l.wait()
+    out_src[0, 0] = (pair(1, 0) + far_dst[0].astype(F32)).astype(BF16)
+    out_rl = send(out_src.at[0, 0], out_dst.at[0, 0], out_s.at[1], out_r.at[1], to_right)
+    fourth = compute(3, mine)
+    third.wait()
+    out_src[1, 0] = pair(2, 0).astype(BF16)
+    out_ll = send(out_src.at[1, 0], out_dst.at[1, 0], out_s.at[2], out_r.at[2], to_left)
+    far_rt.wait()
+    out_src[1, 1] = (pair(2, 1) + far_dst[1].astype(F32)).astype(BF16)
+    out_lr = send(out_src.at[1, 1], out_dst.at[1, 1], out_s.at[3], out_r.at[3], to_left)
+    fourth.wait()
+    for copy in (out_rr, out_rl, out_ll, out_lr):
+        copy.wait()
+
+    def chunk(chip, c):
+        return pl.ds(pl.multiple_of(chip * 256 + c * 128, 128), 128)
+
+    own = chunk(mine, core)
+    for h in range(2):
+        res = pair(3, h) + out_dst[0, h].astype(F32) + out_dst[1, h].astype(F32)
+        probe[own, half * h : half * h + half] = res.astype(BF16)
+
+    def pass_on(slot, chip, h, device):
+        if h is None:
+            ref = probe.at[chunk(chip, core), :]
+        else:
+            ref = probe.at[chunk(chip, core), half * h : half * h + half]
+        return send(ref, ref, ag_s.at[slot], ag_r.at[slot], device)
+
+    go_right = pass_on(0, mine, None, to_right)
+    go_left = pass_on(1, mine, None, to_left)
+    sib_own = pass_on(2, mine, None, to_sib)
+
+    def back_product(chip):
+        rows = pl.ds(pl.multiple_of(chip * 256, 256), 256)
+        for lo, hi in ((0, 256), (256, 512), (512, 640)):
+            back[rows, lo:hi] = nt(probe[rows, :], w[lo:hi, :])
+
+        def tile(i, carry):
+            at = pl.ds(pl.multiple_of(i * 512, 512), 512)
+            gnw_o[:, at] = carry + lax.dot_general(
+                both[rows, width:],
+                probe[rows, at],
+                (((0,), (0,)), ((), ())),
+                preferred_element_type=F32,
+            )
+            return carry
+
+        def tile_add(i, carry):
+            at = pl.ds(pl.multiple_of(i * 512, 512), 512)
+            gnw_o[:, at] = gnw_o[:, at] + lax.dot_general(
+                both[rows, width:],
+                probe[rows, at],
+                (((0,), (0,)), ((), ())),
+                preferred_element_type=F32,
+            )
+            return carry
+
+        lax.fori_loop(0, cols // 512, tile if chip is mine else tile_add, 0.0 if chip is mine else 0)
+        for c in range(2):
+            start = pl.multiple_of(chip * 256 + c * 128, 128)
+            rows = pl.ds(start, 128)
+            inv_c = column(0, start)
+            mixed = jnp.zeros((128, 128), F32)
+            for g in range(groups):
+                at = slice(128 * g, 128 * g + 128)
+                prod = back[rows, at] * gated[rows, at]
+                gain_o[:, at] = gain_o[:, at] + fold(prod * inv_c)
+                mixed = mixed + prod * gain[:, at]
+            mix[pl.ds(chip * 2 + c, 1), :] = jnp.sum(mixed.T, axis=0, keepdims=True)
+
+    sib_own.wait()
+    back_product(mine)
+    go_right.wait()
+    fwd_l = pass_on(3, left, 0, to_right)
+    sib_left = pass_on(4, left, None, to_sib)
+    go_left.wait()
+    fwd_r = pass_on(5, right, 1, to_left)
+    sib_right = pass_on(6, right, None, to_sib)
+    sib_left.wait()
+    back_product(left)
+    fwd_l.wait()
+    sib_far_l = pass_on(7, far, 0, to_sib)
+    fwd_r.wait()
+    sib_far_r = pass_on(8, far, 1, to_sib)
+    sib_right.wait()
+    back_product(right)
+    sib_far_l.wait()
+    sib_far_r.wait()
+    back_product(far)
+    copies = []
+    for k, to in enumerate(peers):
+        copies.append(send(mix, mix_got.at[head], mix_s.at[k], mix_r.at[k], {"head": to}))
+    mix_got[head] = mix[...]
+    for copy in copies:
+        copy.wait()
+    total = mix_got[0]
+    for i in range(1, 8):
+        total = total + mix_got[i]
+    mix[...] = total / channels
+
+    def finish(i, carry):
+        start = pl.multiple_of(i * 128, 128)
+        rows = pl.ds(start, 128)
+        inv_c = column(0, start)
+        mixed_c = jnp.broadcast_to(mix[pl.ds(i, 1), :], (128, 128)).T * (inv_c * inv_c * inv_c)
+        for g in range(groups):
+            at = slice(128 * g, 128 * g + 128)
+            gz = gate_z[rows, at].astype(F32)
+            gate = gz * jax.nn.sigmoid(gz)
+            by_o[rows, at] = (
+                back[rows, at] * gain[:, at] * inv_c - gated[rows, at] * mixed_c
+            ) * gate
+        return carry
+
+    lax.fori_loop(0, length // 128, finish, 0)
+
+
+def middle_call(gated, dgated, sums, gate_z, w, tw, gain, tgain):
+    length, width = gated.shape
+    cols = w.shape[1]
+    half = cols // 2
+    out = lambda *s: jax.ShapeDtypeStruct(s, F32)
+    dma = pltpu.SemaphoreType.DMA
+    return pl.pallas_call(
+        middle_kernel,
+        in_specs=[VMEM] * 8,
+        out_specs=[VMEM] * 3,
+        out_shape=[out(length, width), out(width, cols), out(8, width)],
+        scratch_shapes=[
+            pltpu.VMEM((8, 2, length), F32),
+            pltpu.VMEM((8, length), F32),
+            pltpu.VMEM((length, 2 * width), BF16),
+            pltpu.VMEM((2, 2, 128, cols), F32),
+            pltpu.VMEM((4, 128, cols), F32),
+            pltpu.VMEM((2, 128, half), BF16),
+            pltpu.VMEM((2, 128, half), BF16),
+            pltpu.VMEM((2, 2, 128, half), BF16),
+            pltpu.VMEM((2, 2, 128, half), BF16),
+            pltpu.VMEM((length, cols), BF16),
+            pltpu.VMEM((length, width), F32),
+            pltpu.VMEM((8, 128), F32),
+            pltpu.VMEM((8, 8, 128), F32),
+            dma((8,)), dma((8,)), dma((4,)), dma((4,)), dma((2,)), dma((2,)),
+            dma((4,)), dma((4,)), dma((9,)), dma((9,)), dma((8,)), dma((8,)),
         ],
         compiler_params=pltpu.CompilerParams(
-            collective_id=collective_id, has_side_effects=True, vmem_limit_bytes=LIMIT
+            collective_id=3, has_side_effects=True, vmem_limit_bytes=60 * 1024 * 1024
         ),
-        name="state_scan_forward" if forward else "state_scan_backward",
-    )(msg)
+        name="probe_and_back",
+    )(gated, dgated, sums, gate_z, w, tw, gain, tgain)
+
+
+def final_kernel(
+    pack, hp, gcx_o, gcbc_o, heads_o, gain_o, landed, part, landed2, send1, recv1, send2, recv2
+):
+    count, n_head = landed.shape[0], landed2.shape[0]
+    width = pack.shape[1]
+    heads = hp.shape[1]
+    me, head = lax.axis_index("seq"), lax.axis_index("head")
+    seq_peers, head_peers = others("seq", count), others("head", n_head)
+    greet([{"seq": to} for to in seq_peers] + [{"head": to} for to in head_peers])
+    copies = []
+    for k, to in enumerate(seq_peers):
+        copies.append(send(pack, landed.at[me], send1.at[k], recv1.at[k], {"seq": to}))
+    landed[me] = pack[...]
+    for copy in copies:
+        copy.wait()
+    total = landed[0]
+    for i in range(1, count):
+        total = total + landed[i]
+    part[...] = total[8:16, 0:256]
+    copies = []
+    for k, to in enumerate(head_peers):
+        copies.append(send(part, landed2.at[head], send2.at[k], recv2.at[k], {"head": to}))
+    landed2[head] = part[...]
+    gcx_o[...] = total[0:4]
+    gain_o[...] = total[8:9]
+    at = lax.broadcasted_iota(jnp.int32, (width, 128), 0)
+    to = lax.broadcasted_iota(jnp.int32, (width, 128), 1) * HW
+    pick = jnp.where((at >= to) & (at < to + HW), 1.0, 0.0).astype(F32)
+    sums = jnp.dot(
+        total, pick, precision=lax.Precision.HIGHEST, preferred_element_type=F32
+    )[:, :heads]
+    heads_o[0:1] = sums[4:5] - jnp.exp(hp[1:2]) * sums[6:7]
+    heads_o[1:2] = sums[5:6]
+    heads_o[2:3] = sums[7:8]
+    for copy in copies:
+        copy.wait()
+    total2 = landed2[0]
+    for i in range(1, n_head):
+        total2 = total2 + landed2[i]
+    gcbc_o[...] = total2[1:5]
+
+
+def final_call(pack, head_params, count, n_head):
+    width = pack.shape[1]
+    heads = head_params.shape[1]
+    out = lambda *s: jax.ShapeDtypeStruct(s, F32)
+    dma = pltpu.SemaphoreType.DMA
+    return pl.pallas_call(
+        final_kernel,
+        in_specs=[VMEM] * 2,
+        out_specs=[VMEM] * 4,
+        out_shape=[out(4, width), out(4, 256), out(3, heads), out(1, width)],
+        scratch_shapes=[
+            pltpu.VMEM((count, 16, width), F32),
+            pltpu.VMEM((8, 256), F32),
+            pltpu.VMEM((n_head, 8, 256), F32),
+            dma((count,)), dma((count,)), dma((n_head,)), dma((n_head,)),
+        ],
+        compiler_params=pltpu.CompilerParams(
+            collective_id=4, has_side_effects=True, vmem_limit_bytes=LIMIT
+        ),
+        name="final_sums",
+    )(pack, head_params)
 
 
 def second_kernel(
@@ -399,7 +746,7 @@
     )(x, dx, bc, dbc, rowv, colv, st, dst, logs, start, gate_z, dexp)
 
 
-def third_kernel(by, bc, colv, log, lam_o, msg_o, state, total):
+def third_kernel(by, bc, colv, log, lam_o, msg_o, state):
     step = pl.program_id(0)
     nst = bc.shape[1] // 2
     heads = by.shape[1] // HW
@@ -407,7 +754,6 @@
     @pl.when(step == 0)
     def _():
         state[...] = jnp.zeros_like(state)
-        total[...] = jnp.zeros_like(total)
 
     lam_o[0] = state[...]
     cols = colv[...]
@@ -418,14 +764,12 @@
         l_h, l_l = split(lifted)
         add = nn(ct_h, l_h) + nn(ct_h, l_l) + nn(ct_l, l_h)
         state[:, at] = jnp.exp(log[0, 2:3, at]) * state[:, at] + add
-    total[0:1, :] = total[0:1, :] + log[0, 2:3, :]
 
     @pl.when(step == pl.num_programs(0) - 1)
     def _():
         parts = msg_o.shape[0]
         width = state.shape[1]
-        msg_o[:, 0:8, :] = state[...].reshape(parts, 8, width)
-        msg_o[:, 8:16, :] = jnp.broadcast_to(total[...][None], (parts, 8, width))
+        msg_o[...] = state[...].reshape(parts, 8, width)
 
 
 def third_call(by, bc, colv, logs, parts):
@@ -440,9 +784,9 @@
         third_kernel,
         grid=(count,),
         in_specs=[rows(width), rows(wide), rows(128), cube(8)],
-        out_specs=[cube(nst), pl.BlockSpec((parts, 16, width), lambda i: (0, 0, 0))],
-        out_shape=[out(count, nst, width), out(parts, 16, width)],
-        scratch_shapes=[pltpu.VMEM((nst, width), F32), pltpu.VMEM((8, width), F32)],
+        out_specs=[cube(nst), pl.BlockSpec((parts, 8, width), lambda i: (0, 0, 0))],
+        out_shape=[out(count, nst, width), out(parts, 8, width)],
+        scratch_shapes=[pltpu.VMEM((nst, width), F32)],
         compiler_params=pltpu.CompilerParams(vmem_limit_bytes=LIMIT),
         name="adjoint_states",
     )(by, bc, colv, logs)
@@ -454,9 +798,9 @@
 
 def fourth_kernel(
     by, x, gx, pre_x, halo_x, bc, gbc, pre_bc, halo_bc, rowv, colv, s0_b, lam_b, log, last_log,
-    s_end, dexp,
-    gcx_o, gcbc_o, lane_o, head_o,
-    wx, wbc,
+    s_end, dexp, gain,
+    pack_o,
+    wx, wbc, head_o,
 ):
     step = pl.program_id(0)
     nst = bc.shape[1] // 2
@@ -464,9 +808,8 @@
 
     @pl.when(step == 0)
     def _():
-        gcx_o[...] = jnp.zeros_like(gcx_o)
-        gcbc_o[...] = jnp.zeros_like(gcbc_o)
-        lane_o[...] = jnp.zeros_like(lane_o)
+        pack_o[...] = jnp.zeros_like(pack_o)
+        pack_o[8:9, :] = jnp.sum(gain[...], axis=0, keepdims=True)
         head_o[...] = jnp.zeros_like(head_o)
 
     load_window(wx, halo_x, pre_x, step == 0)
@@ -536,13 +879,13 @@
         back_x = back_u * size + dexp[0:1, at] * byp
         carried = jnp.sum(s1 * s0, axis=0, keepdims=True) * jnp.exp(own)
         through = jnp.sum(expand(cols, SG_, p) * (back_u * xp), axis=0, keepdims=True)
-        lane_o[0:1, at] = lane_o[0:1, at] + through
-        lane_o[1:2, at] = lane_o[1:2, at] + carried * own
-        lane_o[2:3, at] = lane_o[2:3, at] + carried * sig_own
-        lane_o[3:4, at] = lane_o[3:4, at] + jnp.sum(byp * xp, axis=0, keepdims=True)
+        pack_o[4:5, at] = pack_o[4:5, at] + through
+        pack_o[5:6, at] = pack_o[5:6, at] + carried * own
+        pack_o[6:7, at] = pack_o[6:7, at] + carried * sig_own
+        pack_o[7:8, at] = pack_o[7:8, at] + jnp.sum(byp * xp, axis=0, keepdims=True)
         back_z = back_x * gx[:, at]
         for k in range(4):
-            gcx_o[k : k + 1, at] = gcx_o[k : k + 1, at] + jnp.sum(
+            pack_o[k : k + 1, at] = pack_o[k : k + 1, at] + jnp.sum(
                 back_z * wx[5 + k : 5 + k + QB, at], axis=0, keepdims=True
             )
     back_inner_t = jnp.where(keep, back_inner_t, 0.0)
@@ -550,13 +893,25 @@
     back_c = back_c + nn3(back_inner_t.T, b_mat)
     back_zbc = jnp.concatenate([back_b, back_c], axis=1) * gbc[...]
     for k in range(4):
-        gcbc_o[k : k + 1, :] = gcbc_o[k : k + 1, :] + jnp.sum(
+        pack_o[9 + k : 10 + k, 0 : 2 * nst] = pack_o[9 + k : 10 + k, 0 : 2 * nst] + jnp.sum(
             back_zbc * wbc[5 + k : 5 + k + QB, :], axis=0, keepdims=True
         )
 
+    @pl.when(step == pl.num_programs(0) - 1)
+    def _():
+        for p in range(heads // 2):
+            at = slice(128 * p, 128 * p + 128)
+            for kind in range(2):
+                even, odd = head_o[2 * p, kind], head_o[2 * p + 1, kind]
+                even = even + pltpu.roll(even, HW, 1)
+                odd = odd + pltpu.roll(odd, HW, 1)
+                both = jnp.sum(jnp.where(mask, even, odd), axis=0, keepdims=True)
+                pack_o[5 + kind : 6 + kind, at] = pack_o[5 + kind : 6 + kind, at] + both
+
 
 def fourth_call(
-    by, x, gx, pre_x, halo_x, bc, gbc, pre_bc, halo_bc, rowv, colv, s0, lam, logs, s_end, dexp
+    by, x, gx, pre_x, halo_x, bc, gbc, pre_bc, halo_bc, rowv, colv, s0, lam, logs, s_end, dexp,
+    gain,
 ):
     length, width = by.shape
     wide = bc.shape[1]
@@ -577,14 +932,17 @@
             pl.BlockSpec((128, QB), lambda i: (0, i)), rows(128),
             cube(nst), cube(nst), cube(8),
             pl.BlockSpec((1, 8, width), lambda i: (count - 1, 0, 0)),
-            whole(s_end), whole(dexp),
+            whole(s_end), whole(dexp), whole(gain),
         ],
-        out_specs=[fixed(8, width), fixed(8, wide), fixed(8, width), fixed(heads, 2, 8, 128)],
-        out_shape=[out(8, width), out(8, wide), out(8, width), out(heads, 2, 8, 128)],
-        scratch_shapes=[pltpu.VMEM((QB + 8, width), F32), pltpu.VMEM((QB + 8, wide), F32)],
+        out_specs=fixed(16, width),
+        out_shape=out(16, width),
+        scratch_shapes=[
+            pltpu.VMEM((QB + 8, width), F32), pltpu.VMEM((QB + 8, wide), F32),
+            pltpu.VMEM((heads, 2, 8, 128), F32),
+        ],
         compiler_params=pltpu.CompilerParams(vmem_limit_bytes=LIMIT),
         name="adjoint_gradients",
-    )(by, x, gx, pre_x, halo_x, bc, gbc, pre_bc, halo_bc, rowv, colv, s0, lam, logs, logs, s_end, dexp)
+    )(by, x, gx, pre_x, halo_x, bc, gbc, pre_bc, halo_bc, rowv, colv, s0, lam, logs, logs, s_end, dexp, gain)
 
 
 def on_device(
@@ -601,45 +959,27 @@
     t_wout_all = lax.all_gather(t_wout, "seq", axis=1, tiled=True)
     hpc = jnp.concatenate([head_params, t_heads], axis=0).T
     dexp = jnp.repeat(jnp.stack([head_params[2], t_heads[2]]), HW, axis=1)
-    x, dx, gx, bc, dbc, gbc, rowv, colv, st, dst, logs, msg = first_call(
+    x, dx, gx, bc, dbc, gbc, rowv, colv, st, dst, logs, msg, tile = first_call(
         pre_x, halo_x, pre_bc, halo_bc, dt_raw, conv_x, t_conv_x, conv_bc, t_conv_bc, hpc, count
     )
-    start = scan_call(msg, True, 1)
+    start, decays = scan_forward(msg, tile)
     gated, d_gated, s0, sums = second_call(
         x, dx, bc, dbc, rowv, colv, st, dst, logs, start, gate_z, dexp
     )
-    sums = lax.psum(sums, "head")
-    inv_rms = lax.rsqrt(sums[0] / channels + 1e-05)
-    d_inv = -0.5 * inv_rms**3 * sums[1] / channels
-    normed = (gated * inv_rms[:, None] * norm_gain).astype(BF16)
-    d_normed = (
-        (d_gated * inv_rms[:, None] + gated * d_inv[:, None]) * norm_gain
-        + gated * inv_rms[:, None] * t_gain
-    ).astype(BF16)
-    partial_out = nn(d_normed, w_out) + nn(normed, t_wout_all)
-    probe_part = lax.psum_scatter(partial_out, "head", scatter_dimension=0, tiled=True)
-    probe_out = lax.all_gather(probe_part.astype(BF16), "head", axis=0, tiled=True)
-    gn_wout = lax.psum_scatter(nn(normed.T, probe_out), "seq", scatter_dimension=1, tiled=True)
-    back_normed = nt(probe_out, w_out)
-    gain_part = jnp.sum(back_normed * gated * inv_rms[:, None], axis=0)
-    weighted = back_normed * norm_gain
-    mixed = lax.psum(jnp.sum(weighted * gated, axis=1), "head")
-    gate = jax.nn.silu(gate_z.astype(F32))
-    back_y = (weighted * inv_rms[:, None] - gated * (inv_rms**3 * mixed / channels)[:, None]) * gate
+    back_y, gnw, gain_part = middle_call(
+        gated, d_gated, sums, gate_z, w_out, t_wout_all, norm_gain[None], t_gain[None]
+    )
+    gn_wout = lax.psum_scatter(gnw, "seq", scatter_dimension=1, tiled=True)
     lam, msg_back = third_call(back_y, bc, colv, logs, count)
-    s_end = scan_call(msg_back, False, 2)
-    gcx, gcbc, lanes, head_sums = fourth_call(
-        back_y, x, gx, pre_x, halo_x, bc, gbc, pre_bc, halo_bc, rowv, colv, s0, lam, logs, s_end, dexp
-    )
-    per_head = jnp.sum(lanes[:4].reshape(4, heads, HW), axis=2)
-    through_c = jnp.sum(head_sums, axis=(2, 3))
-    log_rate = per_head[1] + through_c[:, 0]
-    rate = jnp.exp(head_params[1])
-    bias = per_head[0] - rate * (per_head[2] + through_c[:, 1])
-    gn_heads = jnp.stack([bias, log_rate, per_head[3]])
-    gn_conv_x, gn_heads, gn_gain = lax.psum((gcx[:4], gn_heads, gain_part), "seq")
-    gn_conv_bc = lax.psum(gcbc[:4], ("seq", "head"))
-    return (gn_conv_x, gn_conv_bc, gn_heads, gn_gain, gn_wout)
+    s_end = scan_backward(msg_back, decays)
+    pack = fourth_call(
+        back_y, x, gx, pre_x, halo_x, bc, gbc, pre_bc, halo_bc, rowv, colv, s0, lam, logs, s_end, dexp,
+        gain_part,
+    )
+    gn_conv_x, gn_conv_bc, gn_heads, gn_gain = final_call(
+        pack, head_params, count, lax.axis_size("head")
+    )
+    return (gn_conv_x, gn_conv_bc, gn_heads, gn_gain[0], gn_wout)
 
 
 def solution(mesh):

time: 471 us -> 293 us (0.62)
  blocking collectives: 161 us -> 0 us
  Pallas kernels: 127 us -> 222 us
  waiting for transfers between devices: 98.5 us -> 22.4 us
  matrix products: 43.7 us -> 0 us
  local copies, waits for them, and re-layouts: 13.5 us -> 29 us
  other arithmetic: 8.27 us -> 0.7 us
    psum x4 -> x0, blocking collectives: 161 us -> none  [the longest x1 72.3 us: on_device(): lax.psum((gcx[:4], gn_heads, gain_part), 'seq')]
    pallas_call x2 -> x4, Pallas kernels: 65.3 us -> 161 us  [the longest x1 85.2 us: middle_call(): pl.pallas_call(middle_kernel, in_specs=[VMEM] * 8, out_specs=[VMEM] * 3,...]
    reduce_scatter x2 -> x0, waiting for transfers between devices: 61.8 us -> none  [the longest x1 61.8 us: on_device(): lax.psum_scatter(partial_out, 'head', scatter_dimension=0, tiled=True)]
    dot_general x4 -> x0, matrix products: 43.7 us -> none  [the longest x3 34.5 us: nn(): return jnp.dot(a, b, preferred_element_type=F32)]
    all_gather x1 -> x0, waiting for transfers between devices: 36 us -> none  [on_device(): lax.all_gather(probe_part.astype(BF16), 'head', axis=0, tiled=True)]
    unnamed x4 -> x3, waiting for transfers between devices: 0.73 us -> 22.4 us
    unnamed x44 -> x28, local copies, waits for them, and re-layouts: 8.65 us -> 18 us
    all_gather x0 -> x1, local copies, waits for them, and re-layouts: none -> 5.6 us  [on_device(): t_wout_all = lax.all_gather(t_wout, 'seq', axis=1, tiled=True)]
  transfers between devices with their start and end apart: 5 -> 3, of which waited for: 2 -> 1; matrix products, arithmetic and copies ran while one was open for 7% -> 3% of each run, Pallas kernels for 27% -> 47%
where the time goes in v2:
time: 293 us; the launch traced here: 292 us
  Pallas kernels  222 us (76%)
  local copies, waits for them, and re-layouts  29 us (10%)
  waiting for transfers between devices  22.4 us (8%)
  between operations  14.2 us (5%)
  starting transfers between devices  3.97 us (1%)
    pallas_call x1, Pallas kernels, middle_call(): pl.pallas_call(middle_kernel, in_specs=[VMEM] * 8, out_specs=[VMEM] * 3,...  85.2 us
    pallas_call x1, Pallas kernels, scan_forward(): pl.pallas_call(scan_forward_kernel, in_specs=[VMEM] * 2, out_specs=[VMEM]...  35.8 us
    unnamed x3, waiting for transfers between devices  22.4 us
    pallas_call x1, Pallas kernels, scan_backward(): pl.pallas_call(scan_backward_kernel, in_specs=[VMEM] * 2, out_specs=VMEM,...  22.1 us
    pallas_call x1, Pallas kernels, fourth_call(): pl.pallas_call(fourth_kernel, grid=(count,), in_specs=[rows(width), rows(...  21 us
    unnamed x28, local copies, waits for them, and re-layouts  18 us
    pallas_call x1, Pallas kernels, final_call(): pl.pallas_call(final_kernel, in_specs=[VMEM] * 2, out_specs=[VMEM] * 4, o...  17.8 us
    pallas_call x1, Pallas kernels, second_call(): pl.pallas_call(second_kernel, grid=(count,), in_specs=[rows(width), rows(...  16.4 us
  transfers between devices with their start and end apart: 3, of which 1 were waited for; matrix products, arithmetic and copies ran while one was open for 3% of the time, Pallas kernels for 47%

profile of v2, /device:TPU:0, one launch (start us, length us, event | category | flops | bytes accessed | tf_op | source)
XLA Modules:
  0.0 292.2 jit_solution(3876187309827745402)
XLA Ops:
  7.2 0.0 all-gather.2.cloned.1.call-start
  7.2 0.7 all-gather.2.cloned.1.call-update
  7.9 0.0 reduce-scatter.4.cloned.1.call-start
  7.9 0.7 slice.18
  8.7 0.7 slice.19
  9.3 3.9 %collective-permute-start = (bf16[8,896]{1,0:T(8,128)(2,1)S(1)}, bf16[8,896]{1,0:T(8,128)(2,1)S(1)}, u32[]{:S(2)}, u32[]{:S(2)}) collective-permute-start(bf16[8,896]{1,0:T(8,128)(2,1)S(1)} %pad_maximum_fusion), channel_id=1, source_target_pairs={{0,8},{8,16},{16,24},{24,32},{32,40},{40,48},{48,56},{56,64},{64,7... | collective-permute-start | bytes 43016 | tf_op jit(solution)/shard_map/ppermute | solution.py:957
  13.2 0.8 copy.27
  14.0 0.7 slice.22
  14.7 0.8 copy.28
  15.5 0.7 slice.23
  16.2 0.1 maximum_bitcast_fusion.hpc
  16.2 0.1 broadcast_in_dim.9
  16.3 0.1 reshape.13.dexp
  16.4 1.3 broadcast_in_dim.10.gain
  17.7 1.3 broadcast_in_dim.11.tgain
  18.9 0.0 collective-permute-done
  18.9 0.0 copy-start
  19.0 1.0 copy-done
  20.0 0.0 copy-start.3
  20.0 0.8 copy-done.3
  20.8 0.0 copy-start.5
  20.8 0.7 copy-done.5
  21.5 0.0 copy-start.6
  21.5 0.7 copy-done.6
  22.2 0.0 copy-start.9
  22.2 0.7 copy-done.9
  22.9 0.0 copy-start.10
  22.9 0.7 copy-done.10
  23.6 16.0 %conv_and_states.1 = (f32[1024,640]{1,0:T(8,128)}, f32[1024,640]{1,0:T(8,128)}, f32[1024,640]{1,0:T(8,128)}, f32[1024,256]{1,0:T(8,128)S(1)}, f32[1024,256]{1,0:...) custom-call(bf16[1024,640]{1,0:T(8,128)(2,1)} %pre_x.3, ...), custom_call_target="tpu_custom_call" | custom-call | tf_op jit(solution)/shard_map/conv_and_states/pallas_call | solution.py:191
  39.6 35.8 %state_scan_forward.1 = (f32[16,16,640]{2,1,0:T(8,128)S(1)}, f32[16,640]{1,0:T(8,128)S(1)}) custom-call(f32[16,16,640]{2,1,0:T(8,128)S(1)} %get-tuple-element.42.msg, f32[8,128]{1,0:T(8,128)S(1)} %get-tuple-element.43.tile), custom_call_target="tpu_custom_call" | custom-call | tf_op jit(solution)/shard_map/state_scan_forward/pallas_call | solution.py:312
  75.4 0.0 copy-start.2
  75.4 1.2 copy-done.2
  76.6 16.4 %outputs_and_tangents.1 = (f32[1024,640]{1,0:T(8,128)}, f32[1024,640]{1,0:T(8,128)}, f32[8,128,640]{2,1,0:T(8,128)}, f32[2,1024]{1,0:T(2,128)S(1)}) custom-call(f32[1024,640]{1,0:T(8,128)} %get-tuple-element.33.x, f32[1024,640]{1,0:T(8,128)} %get-tuple-element.34.dx, f32[1024,256]{1,0:T(8,128)S(1)} %get-tuple-element.35.bc, f32[1024,256]{1,0:T(8,128)S(1)} %copy-done.2, ...), custom_call_target="tpu_custom_call" | custom-call | tf_op jit(solution)/shard_map/outputs_and_tangents/pallas_call | solution.py:734
  93.0 0.0 copy-start.8
  93.0 0.6 copy-done.8
  93.6 0.0 all-gather.2.cloned.1.call-done
  93.6 5.6 %copy.29.tw = bf16[640,2560]{1,0:T(8,128)(2,1)} copy(bf16[640,2560]{0,1:T(8,128)(2,1)} %all-gather.2.cloned.1.call-done) | data formatting | bytes 6553600 | tf_op jit(solution)/shard_map/all_gather | solution.py:959
  99.2 85.2 %probe_and_back.1 = (f32[1024,640]{1,0:T(8,128)}, f32[640,2560]{1,0:T(8,128)}, f32[8,640]{1,0:T(8,128)}) custom-call(f32[1024,640]{1,0:T(8,128)} %get-tuple-element.45.gated, f32[1024,640]{1,0:T(8,128)} %get-tuple-element.46.dgated, f32[2,1024]{1,0:T(2,128)} %copy-done.8, bf16[1024,640]{1,0:T(8,128)(2,1)} %gate_z.3, bf16[640,2560]{1,0:T(8,128)(2,1)} %w.1, ...), custom_call_target="tpu_custom_call" | custom-call | tf_op jit(solution)/shard_map/probe_and_back/pallas_call | solution.py:554
  184.3 8.2 %copy.31 = f32[640,2560]{0,1:T(8,128)} copy(f32[640,2560]{1,0:T(8,128)} %get-tuple-element.60) | data formatting | bytes 13107200
  192.5 0.0 reduce-scatter.4.cloned.1.call-update
  192.5 0.0 copy-start.1
  192.5 0.0 copy-start.4
  192.6 7.8 %adjoint_states.1 = (f32[8,128,640]{2,1,0:T(8,128)}, f32[16,8,640]{2,1,0:T(8,128)S(1)}) custom-call(f32[1024,640]{1,0:T(8,128)} %get-tuple-element.48.by, f32[1024,256]{1,0:T(8,128)S(1)} %get-tuple-element.35.bc, f32[1024,128]{1,0:T(8,128)S(1)} %get-tuple-element.38.colv, f32[8,8,640]{2,1,0:T(8,128)S(1)} %get-tuple-element.41.log.last_log), custom_call_target="tpu_custom_call" | custom-call | tf_op jit(solution)/shard_map/adjoint_states/pallas_call | solution.py:783
  200.4 22.1 %state_scan_backward.1.s_end = f32[16,8,640]{2,1,0:T(8,128)S(1)} custom-call(f32[16,8,640]{2,1,0:T(8,128)S(1)} %get-tuple-element.53.msg, f32[16,640]{1,0:T(8,128)S(1)} %get-tuple-element.54.decays), custom_call_target="tpu_custom_call" | custom-call | tf_op jit(solution)/shard_map/state_scan_backward/pallas_call | solution.py:336
  222.5 0.0 copy-done.1
  222.5 0.0 copy-done.4
  222.5 0.0 copy-start.7
  222.5 21.0 %adjoint_gradients.1.pack = f32[16,640]{1,0:T(8,128)S(1)} custom-call(f32[1024,640]{1,0:T(8,128)} %get-tuple-element.48.by, f32[1024,640]{1,0:T(8,128)} %get-tuple-element.33.x, f32[1024,640]{1,0:T(8,128)} %get-tuple-element.49.gx, bf16[1024,640]{1,0:T(8,128)(2,1)} %pre_x.3, f32[8,640]{1,0:T(8,128)S(1)} %slice.24.halo_x, ...), custom_call_target="tpu_custom_call" | custom-call | tf_op jit(solution)/shard_map/adjoint_gradients/pallas_call | solution.py:926
  243.5 0.0 copy-done.7
  243.5 17.8 %final_sums.1 = (f32[4,640]{1,0:T(4,128)S(1)}, f32[4,256]{1,0:T(4,128)S(1)}, f32[3,10]{1,0:T(4,128)S(1)}, f32[1,640]{1,0:T(1,128)S(1)}) custom-call(f32[16,640]{1,0:T(8,128)S(1)} %adjoint_gradients.1.pack, f32[3,10]{1,0:T(4,128)S(1)} %copy-done.7), custom_call_target="tpu_custom_call" | custom-call | tf_op jit(solution)/shard_map/final_sums/pallas_call | solution.py:630
  261.3 0.6 reduce
  261.9 21.7 %reduce-scatter.4.cloned.1.call-done = f32[160,640]{1,0:T(8,128)} async-done(((f32[2560,640]{1,0:T(8,128)}), f32[160,640]{1,0:T(8,128)}) %reduce-scatter.4.cloned.1.call-update) | async-done | bytes 409616
  283.6 0.6 copy.36
  284.2 0.6 copy.37
  284.8 0.6 copy.38
  (4 shorter events, 0.0 us)
Async XLA Ops:
  7.2 86.4 %all-gather.2.cloned.1.call-start = ((), (), s32[]{:S(2)}) async-start(), calls=%async_computation.1 | async-start | bytes 3481600 | tf_op jit(solution)/shard_map/all_gather | solution.py:959
  7.9 275.7 %reduce-scatter.4.cloned.1.call-start = ((), (), s32[]{:S(2)}) async-start(), calls=%async_computation.2 | async-start | bytes 6963200
  9.3 9.6 %collective-permute-start = (bf16[8,896]{1,0:T(8,128)(2,1)S(1)}, bf16[8,896]{1,0:T(8,128)(2,1)S(1)}, u32[]{:S(2)}, u32[]{:S(2)}) collective-permute-start(bf16[8,896]{1,0:T(8,128)(2,1)S(1)} %pad_maximum_fusion), channel_id=1, source_target_pairs={{0,8},{8,16},{16,24},{24,32},{32,40},{40,48},{48,56},{56,64},{64,7... | collective-permute-start | bytes 43016 | tf_op jit(solution)/shard_map/ppermute | solution.py:957
  18.9 1.0 copy-start
  20.0 0.8 copy-start.3
  20.8 0.7 copy-start.5
  21.5 0.7 copy-start.6
  22.2 0.7 copy-start.9
  22.9 0.7 copy-start.10
  75.4 1.2 copy-start.2
  93.0 0.6 copy-start.8
  192.5 29.9 %copy-start.1 = (bf16[1024,256]{1,0:T(8,128)(2,1)S(1)}, bf16[1024,256]{1,0:T(8,128)(2,1)}, u32[]{:S(2)}) copy-start(bf16[1024,256]{1,0:T(8,128)(2,1)} %pre_bc.3) | copy-start | bytes 1572868
  192.5 29.9 %copy-start.4 = (f32[8,640]{1,0:T(8,128)S(1)}, f32[8,640]{1,0:T(8,128)}, u32[]{:S(2)}) copy-start(f32[8,640]{1,0:T(8,128)} %get-tuple-element.55.gain) | copy-start | bytes 61444
  222.5 21.0 %copy-start.7 = (f32[3,10]{1,0:T(4,128)S(1)}, f32[3,10]{1,0:T(4,128)}, u32[]{:S(2)}) copy-start(f32[3,10]{1,0:T(4,128)} %hp.1) | copy-start | bytes 364
Sparse Core Ops, SparseCore 0:
  10.2 66.0 all-gather.1
  192.7 90.9 reduce-scatter.3

commit v3 on v2

v3 whole, which is shorter than its diff:
```python
import jax
import jax.numpy as jnp
from jax import lax
from jax.experimental import pallas as pl
from jax.experimental.pallas import tpu as pltpu
from jax.sharding import PartitionSpec as P

QB = 128
HW = 64
F32 = jnp.float32
BF16 = jnp.bfloat16
MESH = pl.DeviceIdType.MESH
S_, DS_, C_, DC_, CS_, SG_, K_, DK_ = (16 * i for i in range(8))
LIMIT = 50 * 1024 * 1024


def split(a):
    high = a.astype(BF16)
    return high, (a - high.astype(F32)).astype(BF16)


def nn(a, b):
    return jnp.dot(a, b, preferred_element_type=F32)


def nt(a, b):
    return lax.dot_general(a, b, (((1,), (1,)), ((), ())), preferred_element_type=F32)


def nn3(a, b):
    (ah, al), (bh, bl) = split(a), split(b)
    return nn(ah, bh) + nn(ah, bl) + nn(al, bh)


def nt3(a, b):
    (ah, al), (bh, bl) = split(a), split(b)
    return nt(ah, bh) + nt(ah, bl) + nt(al, bh)


def lane_mask():
    return lax.broadcasted_iota(jnp.int32, (1, 128), 1) < HW


def bcast(cols, at):
    return jnp.broadcast_to(cols[:, at : at + 1], (cols.shape[0], 128))


def expand(cols, base, pair):
    return jnp.where(
        lane_mask(), bcast(cols, base + 2 * pair), bcast(cols, base + 2 * pair + 1)
    )


def expand_all(cols, base, heads):
    return jnp.concatenate([expand(cols, base, p) for p in range(heads // 2)], axis=1)


def load_window(window, halo, block, first):
    @pl.when(first)
    def _():
        window[0:8] = halo[...]

    @pl.when(jnp.logical_not(first))
    def _():
        window[0:8] = window[QB : QB + 8]

    window[8 : QB + 8] = block[...].astype(F32)


def conv_pair(window, weight, t_weight):
    z = jnp.zeros((QB, window.shape[1]), F32)
    dz = jnp.zeros((QB, window.shape[1]), F32)
    for k in range(4):
        rows = window[5 + k : 5 + k + QB, :]
        z = z + weight[k : k + 1, :] * rows
        dz = dz + t_weight[k : k + 1, :] * rows
    sig = jax.nn.sigmoid(z)
    slope = sig * (1.0 + z * (1.0 - sig))
    return z * sig, slope * dz, slope


def first_kernel(
    pre_x, halo_x, pre_bc, halo_bc, dt, cx, tcx, cbc, tcbc, hpc,
    x_o, dx_o, gx_o, bc_o, dbc_o, gbc_o, row_o, col_o, st_o, dst_o, log_o, msg_o, tile_o,
    wx, wbc, feat, state, d_state, logs,
):
    step = pl.program_id(0)
    heads = dt.shape[0]
    nst = cbc.shape[1] // 2

    @pl.when(step == 0)
    def _():
        state[...] = jnp.zeros_like(state)
        d_state[...] = jnp.zeros_like(d_state)
        logs[...] = jnp.zeros_like(logs)
        feat[...] = jnp.zeros_like(feat)
        tile_o[...] = jnp.zeros_like(tile_o)

    load_window(wx, halo_x, pre_x, step == 0)
    load_window(wbc, halo_bc, pre_bc, step == 0)
    z = dt[...] + hpc[:, 0:1]
    rate = jnp.exp(hpc[:, 1:2])
    t_bias, t_lrate = hpc[:, 3:4], hpc[:, 4:5]
    size = jnp.maximum(z, 0.0) + jnp.log1p(jnp.exp(-jnp.abs(z)))
    sig = jax.nn.sigmoid(z)
    log_decay = -size * rate
    at_i = lax.broadcasted_iota(jnp.int32, (QB, QB), 1)
    at_j = lax.broadcasted_iota(jnp.int32, (QB, QB), 0)
    upper = jnp.where(at_j <= at_i, 1.0, 0.0).astype(F32)
    cumul = jnp.dot(log_decay, upper, precision=lax.Precision.HIGHEST, preferred_element_type=F32)
    sig_sum = jnp.dot(sig, upper, precision=lax.Precision.HIGHEST, preferred_element_type=F32)
    d_size = sig * t_bias
    d_cumul = cumul * t_lrate - rate * t_bias * sig_sum
    to_end = jnp.exp(cumul[:, QB - 1 : QB] - cumul)
    feat[S_ : S_ + heads] = size
    feat[DS_ : DS_ + heads] = d_size
    feat[C_ : C_ + heads] = cumul
    feat[DC_ : DC_ + heads] = d_cumul
    feat[CS_ : CS_ + heads] = sig_sum
    feat[SG_ : SG_ + heads] = sig
    feat[K_ : K_ + heads] = to_end * size
    feat[DK_ : DK_ + heads] = to_end * (
        d_size + size * (d_cumul[:, QB - 1 : QB] - d_cumul)
    )
    rows = feat[...]
    cols = rows.T
    row_o[...] = rows
    col_o[...] = cols

    bc, dbc, gbc = conv_pair(wbc, cbc, tcbc)
    bc_o[...] = bc
    dbc_o[...] = dbc
    gbc_o[...] = gbc
    x, dx, gx = conv_pair(wx, cx, tcx)
    x_o[...] = x
    dx_o[...] = dx
    gx_o[...] = gx

    last = cols[QB - 1 : QB, :]
    tile_o[0:1, :] = tile_o[0:1, :] + last
    own = expand_all(last, C_, heads)
    d_own = expand_all(last, DC_, heads)
    sig_own = expand_all(last, CS_, heads)
    log_o[0, 0:1, :] = logs[0:1, :]
    log_o[0, 1:2, :] = logs[1:2, :]
    log_o[0, 2:3, :] = own
    log_o[0, 3:4, :] = d_own
    log_o[0, 4:5, :] = sig_own
    log_o[0, 5:8, :] = jnp.zeros((3, own.shape[1]), F32)
    logs[0:1, :] = logs[0:1, :] + own
    logs[1:2, :] = logs[1:2, :] + d_own

    st_o[0] = state[...]
    dst_o[0] = d_state[...]
    bt = bc[:, :nst].T
    dbt = dbc[:, :nst].T
    both = jnp.concatenate([bt, dbt], axis=1)
    both_h, both_l = split(both)
    for p in range(heads // 2):
        at = slice(128 * p, 128 * p + 128)
        k_x, dk_x = expand(cols, K_, p), expand(cols, DK_, p)
        ux = k_x * x[:, at]
        dux = k_x * dx[:, at] + dk_x * x[:, at]
        z_h, z_l = split(jnp.concatenate([dux, ux], axis=0))
        d_add = nn(both_h, z_h) + nn(both_h, z_l) + nn(both_l, z_h)
        b_h, b_l, u_h, u_l = both_h[:, :QB], both_l[:, :QB], z_h[QB:], z_l[QB:]
        add = nn(b_h, u_h) + nn(b_h, u_l) + nn(b_l, u_h)
        decay = jnp.exp(own[:, at])
        before = state[:, at]
        d_state[:, at] = decay * (d_state[:, at] + d_own[:, at] * before) + d_add
        state[:, at] = decay * before + add

    @pl.when(step == pl.num_programs(0) - 1)
    def _():
        parts = msg_o.shape[0]
        width = state.shape[1]
        msg_o[:, 0:8, :] = state[...].reshape(parts, 8, width)
        msg_o[:, 8:16, :] = d_state[...].reshape(parts, 8, width)


def first_call(pre_x, halo_x, pre_bc, halo_bc, dt, cx, tcx, cbc, tcbc, hpc, parts):
    length, width = pre_x.shape
    wide = pre_bc.shape[1]
    nst = wide // 2
    heads = dt.shape[0]
    count = length // QB
    whole = lambda a: pl.BlockSpec(a.shape, lambda i: (0,) * a.ndim)
    rows = lambda w: pl.BlockSpec((QB, w), lambda i: (i, 0))
    cube = lambda r: pl.BlockSpec((1, r, width), lambda i: (i, 0, 0))
    out = lambda *s: jax.ShapeDtypeStruct(s, F32)
    return pl.pallas_call(
        first_kernel,
        grid=(count,),
        in_specs=[
            rows(width), whole(halo_x), rows(wide), whole(halo_bc),
            pl.BlockSpec((heads, QB), lambda i: (0, i)),
            whole(cx), whole(tcx), whole(cbc), whole(tcbc), whole(hpc),
        ],
        out_specs=[rows(width)] * 3 + [rows(wide)] * 3 + [
            pl.BlockSpec((128, QB), lambda i: (0, i)),
            rows(128), cube(nst), cube(nst), cube(8),
            pl.BlockSpec((parts, 16, width), lambda i: (0, 0, 0)),
            pl.BlockSpec((8, 128), lambda i: (0, 0)),
        ],
        out_shape=[out(length, width)] * 3 + [out(length, wide)] * 3 + [
            out(128, length), out(length, 128),
            out(count, nst, width), out(count, nst, width), out(count, 8, width),
            out(parts, 16, width), out(8, 128),
        ],
        scratch_shapes=[
            pltpu.VMEM((QB + 8, width), F32), pltpu.VMEM((QB + 8, wide), F32),
            pltpu.VMEM((128, QB), F32), pltpu.VMEM((nst, width), F32),
            pltpu.VMEM((nst, width), F32), pltpu.VMEM((8, width), F32),
        ],
        compiler_params=pltpu.CompilerParams(vmem_limit_bytes=LIMIT),
        name="conv_and_states",
    )(pre_x, halo_x, pre_bc, halo_bc, dt, cx, tcx, cbc, tcbc, hpc)


def greet(peers):
    barrier = pltpu.get_barrier_semaphore()
    for peer in peers:
        pl.semaphore_signal(barrier, inc=1, device_id=peer, device_id_type=MESH)
    pl.semaphore_wait(barrier, len(peers))


def others(axis, count):
    me = lax.axis_index(axis)
    return [lax.rem(me + k, count) for k in range(1, count)]


def link(src, dst, send_sem, recv_sem, device):
    return pltpu.make_async_remote_copy(
        src_ref=src, dst_ref=dst, send_sem=send_sem, recv_sem=recv_sem,
        device_id=device, device_id_type=MESH,
    )


def send(*what):
    copy = link(*what)
    copy.start()
    return copy


def scan_forward_kernel(
    msg, tile, result, decay_o, landed, tiles, answer, send0, recv0, send1, recv1, send2, recv2
):
    count = msg.shape[0]
    width = msg.shape[2]
    heads = width // HW
    me = lax.axis_index("seq")
    peers = others("seq", count)
    greet([{"seq": to} for to in peers])
    copies = []
    for k, to in enumerate(peers):
        at = {"seq": to}
        copies.append(send(tile, tiles.at[me], send0.at[k], recv0.at[k], at))
        copies.append(send(msg.at[to], landed.at[me], send1.at[k], recv1.at[k], at))
    landed[me] = msg[me]
    tiles[me] = tile[...]
    for copy in copies:
        copy.wait()
    state = jnp.zeros((8, width), F32)
    d_state = jnp.zeros((8, width), F32)
    for i in range(count):
        answer[i, 0:8] = state
        answer[i, 8:16] = d_state
        features = tiles[i, 0:1, :]
        decay = jnp.exp(expand_all(features, C_, heads))
        decay_o[i : i + 1, :] = decay
        d_state = decay * (d_state + expand_all(features, DC_, heads) * state)
        d_state = d_state + landed[i, 8:16]
        state = decay * state + landed[i, 0:8]
    copies = []
    for k, to in enumerate(peers):
        copies.append(
            send(answer.at[to], result.at[me], send2.at[k], recv2.at[k], {"seq": to})
        )
    result[me] = answer[me]
    for copy in copies:
        copy.wait()


VMEM = pl.BlockSpec(memory_space=pltpu.VMEM)


def scan_forward(msg, tile):
    parts, rows, width = msg.shape
    sems = [pltpu.SemaphoreType.DMA((parts,))] * 6
    return pl.pallas_call(
        scan_forward_kernel,
        in_specs=[VMEM] * 2,
        out_specs=[VMEM] * 2,
        out_shape=[
            jax.ShapeDtypeStruct((parts, rows, width), F32),
            jax.ShapeDtypeStruct((parts, width), F32),
        ],
        scratch_shapes=[
            pltpu.VMEM((parts, rows, width), F32),
            pltpu.VMEM((parts, 8, 128), F32),
            pltpu.VMEM((parts, rows, width), F32),
        ]
        + sems,
        compiler_params=pltpu.CompilerParams(
            collective_id=1, has_side_effects=True, vmem_limit_bytes=LIMIT
        ),
        name="state_scan_forward",
    )(msg, tile)


def middle_kernel(
    gated, dgated, sums, gate_z, w, tw, gain, tgain,
    by_o, gain_o, sum_z_o, sum_y_o,
    got, scal, both, part, sib, far_src, far_dst, out_src, out_dst, probe, back, gnw, got_z, got_y,
    mix, mix_got,
    sums_s, sums_r, sib_s, sib_r, far_s, far_r, out_s, out_r, ag_s, ag_r, mix_s, mix_r,
    az_s, az_r, ay_s, ay_r,
):
    length, width = gated.shape
    blocks, _, blk = probe.shape
    groups = width // 128
    channels = width * 8.0
    head = lax.axis_index("head")
    me = lax.axis_index("seq")
    my_y, my_z = me // 4, lax.rem(me, 4)
    mine = head // 2
    core = lax.rem(head, 2)
    right, left, far = (lax.rem(mine + k, 4) for k in (1, 3, 2))
    device = lambda chip, c: {"head": chip * 2 + c}
    to_right, to_left, to_sib = device(right, core), device(left, core), device(mine, 1 - core)
    y_peers = [{"seq": lax.rem(my_y + k, 4) * 4 + my_z} for k in range(1, 4)]
    z_peers = [{"seq": my_y * 4 + lax.rem(my_z + k, 4)} for k in range(1, 4)]
    peers = others("head", 8)
    greet([{"head": to} for to in peers] + y_peers + z_peers)
    copies = []
    for k, to in enumerate(peers):
        copies.append(send(sums, got.at[head], sums_s.at[k], sums_r.at[k], {"head": to}))
    got[head] = sums[...]
    gain_o[...] = jnp.zeros_like(gain_o)
    for copy in copies:
        copy.wait()
    total = got[0]
    for i in range(1, 8):
        total = total + got[i]
    inv = lax.rsqrt(total[0:1] / channels + 1e-05)
    scal[0:1] = inv
    scal[1:2] = -0.5 * inv * inv * inv * total[1:2] / channels

    def column(row, start):
        at = pl.ds(pl.multiple_of(start, 128), 128)
        return jnp.broadcast_to(scal[row : row + 1, at], (128, 128)).T

    def norm(i, carry):
        start = pl.multiple_of(i * 128, 128)
        rows = pl.ds(start, 128)
        inv_c, d_inv_c = column(0, start), column(1, start)
        for g in range(groups):
            at = slice(128 * g, 128 * g + 128)
            gt, dgt = gated[rows, at], dgated[rows, at]
            ga = gain[:, at]
            scaled = gt * inv_c
            normed = scaled * ga
            d_normed = (dgt * inv_c + gt * d_inv_c) * ga + scaled * tgain[:, at]
            both[rows, at] = d_normed.astype(BF16)
            both[rows, width + 128 * g : width + 128 * g + 128] = normed.astype(BF16)
        return carry

    lax.fori_loop(0, length // 128, norm, 0)

    def columns(i):
        return pl.ds(pl.multiple_of(lax.rem(my_y + 1 + i, 4) * blk, 128), blk)

    def compute(i):
        slot, at = i % 2, columns(i)

        res = nn(both[:, 0:width], w[:, at]) + nt(both[:, width:], tw[at, :])
        part[slot] = res.reshape(4, 2, 128, blk)
        return send(part.at[slot, :, 1 - core], sib.at[i], sib_s.at[i], sib_r.at[i], to_sib)

    def pairs(i, copy):
        copy.wait()
        for chip in range(4):
            sib[i, chip] = sib[i, chip] + part[i % 2, chip, core]
        way, near = (to_right, to_left) if i % 2 == 0 else (to_left, to_right)
        near_chip = left if i % 2 == 0 else right
        far_src[i] = sib[i, far].astype(BF16)
        transit = send(far_src.at[i], far_dst.at[i], far_s.at[i], far_r.at[i], way)
        out_src[i, 0] = sib[i, near_chip].astype(BF16)
        direct = send(out_src.at[i, 0], out_dst.at[i, 0], out_s.at[i, 0], out_r.at[i, 0], near)
        return transit, direct

    def through(i, transit):
        transit.wait()
        way, chip = (to_right, right) if i % 2 == 0 else (to_left, left)
        out_src[i, 1] = (sib[i, chip] + far_dst[i].astype(F32)).astype(BF16)
        return send(out_src.at[i, 1], out_dst.at[i, 1], out_s.at[i, 1], out_r.at[i, 1], way)

    def pass_on(i, slot, chip, to):
        ref = probe.at[i, pl.ds(pl.multiple_of(chip * 256 + core * 128, 128), 128), :]
        return send(ref, ref, ag_s.at[i, slot], ag_r.at[i, slot], to)

    def own(i, direct, joined):
        direct.wait()
        joined.wait()
        rows = pl.ds(pl.multiple_of(mine * 256 + core * 128, 128), 128)
        res = sib[i, mine] + out_dst[i, 0].astype(F32) + out_dst[i, 1].astype(F32)
        probe[i, rows, :] = res.astype(BF16)
        go_right = pass_on(i, 0, mine, to_right)
        go_left = pass_on(i, 1, mine, to_left)
        return go_right, go_left, pass_on(i, 2, mine, to_sib)

    def forward(i, go_right, go_left):
        if i % 2 == 0:
            go_right.wait()
            onward = pass_on(i, 3, left, to_right)
            go_left.wait()
        else:
            go_left.wait()
            onward = pass_on(i, 3, right, to_left)
            go_right.wait()
        return onward, pass_on(i, 4, left, to_sib), pass_on(i, 5, right, to_sib)

    def last_hop(i, onward):
        onward.wait()
        return pass_on(i, 6, far, to_sib)

    def back_block(i, waits):
        for copy in waits:
            copy.wait()
        at = columns(i)
        gnw[i] = lax.dot_general(
            probe[i], both[:, width:], (((0,), (0,)), ((), ())), preferred_element_type=F32
        ).reshape(4, blk // 4, width)
        half = blk // 8
        sent = []
        for k in (2, 1, 3):
            z = lax.rem(my_z + k, 4)
            sent.append(
                send(
                    gnw.at[i, z, 0:half, :], got_z.at[i, k - 1],
                    az_s.at[i, k], az_r.at[i, k], z_peers[k - 1],
                )
            )
        if i < 3:
            sent.append(
                send(
                    gnw.at[i, :, half : 2 * half, :], got_y.at[i],
                    ay_s.at[i], ay_r.at[i], y_peers[i],
                )
            )

        res = nt(probe[i], w[:, at])
        back[...] = res if i == 0 else back[...] + res
        return sent

    sib0 = compute(0)
    sib1 = compute(1)
    far0, dir0 = pairs(0, sib0)
    sib2 = compute(2)
    far1, dir1 = pairs(1, sib1)
    join0 = through(0, far0)
    sib3 = compute(3)
    far2, dir2 = pairs(2, sib2)
    join1 = through(1, far1)
    ag0 = own(0, dir0, join0)
    far3, dir3 = pairs(3, sib3)
    join2 = through(2, far2)
    ag1 = own(1, dir1, join1)
    fwd0 = forward(0, ag0[0], ag0[1])
    join3 = through(3, far3)
    ag2 = own(2, dir2, join2)
    fwd1 = forward(1, ag1[0], ag1[1])
    end0 = last_hop(0, fwd0[0])
    ag3 = own(3, dir3, join3)
    fwd2 = forward(2, ag2[0], ag2[1])
    end1 = last_hop(1, fwd1[0])
    sent = back_block(0, [ag0[2], fwd0[1], fwd0[2], end0])
    fwd3 = forward(3, ag3[0], ag3[1])
    end2 = last_hop(2, fwd2[0])
    sent = sent + back_block(1, [ag1[2], fwd1[1], fwd1[2], end1])
    end3 = last_hop(3, fwd3[0])
    sent = sent + back_block(2, [ag2[2], fwd2[1], fwd2[2], end2])
    sent = sent + back_block(3, [ag3[2], fwd3[1], fwd3[2], end3])

    def mixing(i, carry):
        start = pl.multiple_of(i * 128, 128)
        rows = pl.ds(start, 128)
        inv_c = column(0, start)
        mixed = jnp.zeros((128, 128), F32)
        for g in range(groups):
            at = slice(128 * g, 128 * g + 128)
            prod = back[rows, at] * gated[rows, at]
            gain_o[:, at] = gain_o[:, at] + fold(prod * inv_c)
            mixed = mixed + prod * gain[:, at]
        mix[pl.ds(i, 1), :] = jnp.sum(mixed.T, axis=0, keepdims=True)
        return carry

    lax.fori_loop(0, length // 128, mixing, 0)
    copies = []
    for k, to in enumerate(peers):
        copies.append(send(mix, mix_got.at[head], mix_s.at[k], mix_r.at[k], {"head": to}))
    mix_got[head] = mix[...]
    for copy in copies:
        copy.wait()
    total = mix_got[0]
    for i in range(1, 8):
        total = total + mix_got[i]
    mix[...] = total / channels

    def finish(i, carry):
        start = pl.multiple_of(i * 128, 128)
        rows = pl.ds(start, 128)
        inv_c = column(0, start)
        mixed_c = jnp.broadcast_to(mix[pl.ds(i, 1), :], (128, 128)).T * (inv_c * inv_c * inv_c)
        for g in range(groups):
            at = slice(128 * g, 128 * g + 128)
            gz = gate_z[rows, at].astype(F32)
            gate = gz * jax.nn.sigmoid(gz)
            by_o[rows, at] = (
                back[rows, at] * gain[:, at] * inv_c - gated[rows, at] * mixed_c
            ) * gate
        return carry

    lax.fori_loop(0, length // 128, finish, 0)
    for copy in sent:
        copy.wait()
    half = blk // 8
    for i in range(blocks):
        j = lax.rem(my_y + 1 + i, 4)
        sum_z_o[j] = gnw[i, my_z, 0:half, :] + got_z[i, 0] + got_z[i, 1] + got_z[i, 2]
    sum_y_o[...] = gnw[3, :, half : 2 * half, :] + got_y[0] + got_y[1] + got_y[2]


def middle_call(gated, dgated, sums, gate_z, w, tw, gain, tgain):
    length, width = gated.shape
    cols = w.shape[1]
    blk = cols // 4
    half = blk // 8
    out = lambda *s: jax.ShapeDtypeStruct(s, F32)
    dma = pltpu.SemaphoreType.DMA
    return pl.pallas_call(
        middle_kernel,
        in_specs=[VMEM] * 8,
        out_specs=[VMEM] * 4,
        out_shape=[out(length, width), out(8, width), out(4, half, width), out(4, half, width)],
        scratch_shapes=[
            pltpu.VMEM((8, 2, length), F32),
            pltpu.VMEM((8, length), F32),
            pltpu.VMEM((length, 2 * width), BF16),
            pltpu.VMEM((2, 4, 2, 128, blk), F32),
            pltpu.VMEM((4, 4, 128, blk), F32),
            pltpu.VMEM((4, 128, blk), BF16),
            pltpu.VMEM((4, 128, blk), BF16),
            pltpu.VMEM((4, 2, 128, blk), BF16),
            pltpu.VMEM((4, 2, 128, blk), BF16),
            pltpu.VMEM((4, length, blk), BF16),
            pltpu.VMEM((length, width), F32),
            pltpu.VMEM((4, 4, blk // 4, width), F32),
            pltpu.VMEM((4, 3, half, width), F32),
            pltpu.VMEM((3, 4, half, width), F32),
            pltpu.VMEM((8, 128), F32),
            pltpu.VMEM((8, 8, 128), F32),
            dma((8,)), dma((8,)), dma((4,)), dma((4,)), dma((4,)), dma((4,)),
            dma((4, 2)), dma((4, 2)), dma((4, 7)), dma((4, 7)), dma((8,)), dma((8,)),
            dma((4, 4)), dma((4, 4)), dma((3,)), dma((3,)),
        ],
        compiler_params=pltpu.CompilerParams(
            collective_id=3, has_side_effects=True, vmem_limit_bytes=61 * 1024 * 1024
        ),
        name="probe_and_back",
    )(gated, dgated, sums, gate_z, w, tw, gain, tgain)


def second_kernel(
    x, dx, bc, dbc, rowv, colv, st, dst, log, start, gate_z, dexp,
    gated_o, dgated_o, s0_o, sums_o,
):
    nst = bc.shape[1] // 2
    heads = x.shape[1] // HW
    b_mat, c_mat = bc[:, :nst], bc[:, nst:]
    db_mat, dc_mat = dbc[:, :nst], dbc[:, nst:]
    at_j = lax.broadcasted_iota(jnp.int32, (QB, QB), 1)
    at_i = lax.broadcasted_iota(jnp.int32, (QB, QB), 0)
    keep = at_i >= at_j
    inner = jnp.where(keep, nt3(c_mat, b_mat), 0.0)
    d_inner = jnp.where(
        keep,
        nt3(
            jnp.concatenate([dc_mat, c_mat], axis=1),
            jnp.concatenate([b_mat, db_mat], axis=1),
        ),
        0.0,
    )
    cols = colv[...]
    rows = rowv[...]
    mask = lane_mask()
    squares = jnp.zeros((QB, 128), F32)
    crossed = jnp.zeros((QB, 128), F32)
    for p in range(heads // 2):
        at = slice(128 * p, 128 * p + 128)
        reach = jnp.exp(log[0, 0:1, at])
        s_in = start[:, 0:8, at].reshape(nst, 128)
        ds_in = start[:, 8:16, at].reshape(nst, 128)
        s0 = st[0, :, at] + reach * s_in
        ds0 = dst[0, :, at] + reach * (ds_in + log[0, 1:2, at] * s_in)
        s0_o[0, :, at] = s0
        xp, dxp = x[:, at], dx[:, at]
        size, d_size = expand(cols, S_, p), expand(cols, DS_, p)
        u = size * xp
        du = size * dxp + d_size * xp
        z_h, z_l = split(jnp.concatenate([u, s0], axis=0))
        dz_h, dz_l = split(jnp.concatenate([du, ds0], axis=0))
        mats, d_mats = [], []
        for h in (2 * p, 2 * p + 1):
            c_col = bcast(cols, C_ + h)
            dc_col = bcast(cols, DC_ + h)
            c_row = rows[C_ + h : C_ + h + 1, :]
            dc_row = rows[DC_ + h : DC_ + h + 1, :]
            level = jnp.exp(jnp.minimum(c_col - c_row, 0.0))
            m = inner * level
            dm = d_inner * level + m * (dc_col - dc_row)
            lift = jnp.exp(c_col)
            e = lift * c_mat
            de = lift * dc_mat + dc_col * e
            mats.append(jnp.concatenate([m, e], axis=1))
            d_mats.append(jnp.concatenate([dm, de], axis=1))
        a_h, a_l = split(jnp.concatenate(mats, axis=0))
        da_h, da_l = split(jnp.concatenate(d_mats, axis=0))
        big = nn(a_h, jnp.concatenate([z_h, dz_h], axis=1))
        big = big + nn(a_h, jnp.concatenate([z_l, dz_l], axis=1))
        big = big + nn(a_l, jnp.concatenate([z_h, dz_h], axis=1))
        small = nn(da_h, jnp.concatenate([z_h, z_l], axis=1))
        low = nn(da_l, z_h)
        y2 = big[:, :128]
        dy2 = big[:, 128:] + small[:, :128] + small[:, 128:] + low
        skip, d_skip = dexp[0:1, at], dexp[1:2, at]
        y = jnp.where(mask, y2[:QB], y2[QB:]) + skip * xp
        dy = jnp.where(mask, dy2[:QB], dy2[QB:]) + skip * dxp + d_skip * xp
        gz = gate_z[:, at].astype(F32)
        gate = gz * jax.nn.sigmoid(gz)
        gated = y * gate
        dgated = dy * gate
        gated_o[:, at] = gated
        dgated_o[:, at] = dgated
        squares = squares + gated * gated
        crossed = crossed + 2.0 * gated * dgated
    sums_o[0:1, :] = jnp.sum(squares.T, axis=0, keepdims=True)
    sums_o[1:2, :] = jnp.sum(crossed.T, axis=0, keepdims=True)


def second_call(x, dx, bc, dbc, rowv, colv, st, dst, logs, start, gate_z, dexp):
    length, width = x.shape
    wide = bc.shape[1]
    nst = wide // 2
    count = length // QB
    whole = lambda a: pl.BlockSpec(a.shape, lambda i: (0,) * a.ndim)
    rows = lambda w: pl.BlockSpec((QB, w), lambda i: (i, 0))
    cube = lambda r: pl.BlockSpec((1, r, width), lambda i: (i, 0, 0))
    out = lambda *s: jax.ShapeDtypeStruct(s, F32)
    return pl.pallas_call(
        second_kernel,
        grid=(count,),
        in_specs=[
            rows(width), rows(width), rows(wide), rows(wide),
            pl.BlockSpec((128, QB), lambda i: (0, i)),
            rows(128), cube(nst), cube(nst), cube(8), whole(start), rows(width), whole(dexp),
        ],
        out_specs=[rows(width), rows(width), cube(nst), pl.BlockSpec((2, QB), lambda i: (0, i))],
        out_shape=[out(length, width), out(length, width), out(count, nst, width), out(2, length)],
        compiler_params=pltpu.CompilerParams(vmem_limit_bytes=LIMIT),
        name="outputs_and_tangents",
    )(x, dx, bc, dbc, rowv, colv, st, dst, logs, start, gate_z, dexp)


def fold(a):
    return jnp.sum(a.reshape(a.shape[0] // 8, 8, a.shape[1]), axis=0)


def adjoint_kernel(
    by, x, gx, pre_x, halo_x, bc, gbc, pre_bc, halo_bc, rowv, colv, s0_b, log, last_log,
    dexp, gain, decays, hp, own_z, own_y,
    piece_o, gcx_o, gcbc_o, heads_o, gain_o,
    wx, wbc, head_o, pack_o, lam, state, msg, landed, answer, s_end,
    end_z, end_y, pack_z, landed_z, landed_y, part, landed_q,
    bz_s, bz_r, by_s, by_r,
    s1_s, s1_r, s2_s, s2_r, f1_s, f1_r, f3_s, f3_r, f2_s, f2_r,
):
    step = pl.program_id(0)
    half = lam.shape[0]
    nst = bc.shape[1] // 2
    width = by.shape[1]
    heads = width // HW
    count, n_head = landed.shape[0], landed_q.shape[0]
    me, head = lax.axis_index("seq"), lax.axis_index("head")
    my_y, my_z = me // 4, lax.rem(me, 4)
    seq_peers, head_peers = others("seq", count), others("head", n_head)
    rows_half = own_z.shape[1]
    mask = lane_mask()

    y_peers = [{"seq": lax.rem(my_y + k, 4) * 4 + my_z} for k in range(1, 4)]
    z_peers = [{"seq": my_y * 4 + lax.rem(my_z + k, 4)} for k in range(1, 4)]

    def last_copies():
        copies = []
        for k in (2, 1, 3):
            z, y = lax.rem(my_z + k, 4), lax.rem(my_y + k, 4)
            copies.append(
                link(own_z.at[y], end_z.at[k - 1], bz_s.at[k], bz_r.at[k], {"seq": y * 4 + my_z})
            )
            copies.append(
                link(own_y.at[z], end_y.at[k - 1], by_s.at[k], by_r.at[k], {"seq": my_y * 4 + z})
            )
        return copies

    @pl.when(step == 0)
    def _():
        greet([{"seq": to} for to in seq_peers] + [{"head": to} for to in head_peers])
        for copy in last_copies():
            copy.start()
        state[...] = jnp.zeros_like(state)
        head_o[...] = jnp.zeros_like(head_o)
        pack_o[...] = jnp.zeros_like(pack_o)
        pack_o[8:9, :] = jnp.sum(gain[...], axis=0, keepdims=True)

    @pl.when(step < half)
    def _():
        lam[half - 1 - step] = state[...]
        cols = colv[...]
        ct_h, ct_l = split(bc[:, nst:].T)
        for p in range(heads // 2):
            at = slice(128 * p, 128 * p + 128)
            lifted = jnp.exp(expand(cols, C_, p)) * by[:, at]
            l_h, l_l = split(lifted)
            add = nn(ct_h, l_h) + nn(ct_h, l_l) + nn(ct_l, l_h)
            state[:, at] = jnp.exp(log[0, 2:3, at]) * state[:, at] + add

    @pl.when(step == half - 1)
    def _():
        msg[...] = state[...].reshape(count, 8, width)
        copies = []
        for k, to in enumerate(seq_peers):
            copies.append(send(msg.at[to], landed.at[me], s1_s.at[k], s1_r.at[k], {"seq": to}))
        landed[me] = msg[me]
        for copy in copies:
            copy.wait()
        adjoint = jnp.zeros((8, width), F32)
        for i in range(count - 1, -1, -1):
            answer[i] = adjoint
            adjoint = decays[i : i + 1, :] * adjoint + landed[i]
        copies = []
        for k, to in enumerate(seq_peers):
            copies.append(send(answer.at[to], s_end.at[me], s2_s.at[k], s2_r.at[k], {"seq": to}))
        s_end[me] = answer[me]
        for copy in copies:
            copy.wait()

    @pl.when(step >= half)
    def _():
        load_window(wx, halo_x, pre_x, step == half)
        load_window(wbc, halo_bc, pre_bc, step == half)
        b_mat, c_mat = bc[:, :nst], bc[:, nst:]
        at_i = lax.broadcasted_iota(jnp.int32, (QB, QB), 1)
        at_j = lax.broadcasted_iota(jnp.int32, (QB, QB), 0)
        keep = at_i >= at_j
        inner_t = jnp.where(keep, nt3(b_mat, c_mat), 0.0)
        cols = colv[...]
        rows = rowv[...]
        back_inner_t = jnp.zeros((QB, QB), F32)
        back_b = jnp.zeros((QB, nst), F32)
        back_c = jnp.zeros((QB, nst), F32)
        for p in range(heads // 2):
            at = slice(128 * p, 128 * p + 128)
            own, sig_own = log[0, 2:3, at], log[0, 4:5, at]
            reach = jnp.exp(last_log[0, 0:1, at] + last_log[0, 2:3, at] - log[0, 0:1, at] - own)
            s1 = lam[step - half, :, at] + reach * s_end[:, :, at].reshape(nst, 128)
            s0 = s0_b[0, :, at]
            byp, xp = by[:, at], x[:, at]
            size = expand(cols, S_, p)
            u = size * xp
            rhs_h, rhs_l = split(jnp.concatenate([byp, s1], axis=0))
            u_h, u_l = split(
                jnp.concatenate([jnp.where(mask, u, 0.0), jnp.where(mask, 0.0, u)], axis=0)
            )
            y_h, y_l = split(
                jnp.concatenate([jnp.where(mask, byp, 0.0), jnp.where(mask, 0.0, byp)], axis=0)
            )
            s0_h, s0_l = split(s0)
            mt_tt = nt(u_h, rhs_h) + nt(u_h, rhs_l) + nt(u_l, rhs_h)
            v_all = nt(y_h, s0_h) + nt(y_h, s0_l) + nt(y_l, s0_h)
            mats = []
            for s in range(2):
                h = 2 * p + s
                c_col, cs_col = bcast(cols, C_ + h), bcast(cols, CS_ + h)
                c_row = rows[C_ + h : C_ + h + 1, :]
                cs_row = rows[CS_ + h : CS_ + h + 1, :]
                c_end, cs_end = c_row[:, QB - 1 : QB], cs_row[:, QB - 1 : QB]
                back_mt = mt_tt[s * QB : s * QB + QB, :QB]
                tt = mt_tt[s * QB : s * QB + QB, QB:]
                v = v_all[s * QB : s * QB + QB]
                diff = jnp.minimum(c_row - c_col, 0.0)
                level = jnp.exp(diff)
                back_inner_t = back_inner_t + level * back_mt
                m_t = inner_t * level
                prod = m_t * back_mt
                lifted = jnp.exp(c_col) * v
                back_c = back_c + lifted
                lc = lifted * c_mat
                left = c_end - c_col
                to_end = jnp.exp(left)
                tb = to_end * tt
                back_b = back_b + tb
                tbb = tb * b_mat
                head_o[h, 0] = head_o[h, 0] + fold(prod * diff + lc * c_col + tbb * left)
                head_o[h, 1] = head_o[h, 1] + fold(
                    prod * (cs_row - cs_col) + lc * cs_col + tbb * (cs_end - cs_col)
                )
                mats.append(jnp.concatenate([m_t, to_end * b_mat], axis=1))
            a_h, a_l = split(jnp.concatenate(mats, axis=0))
            wide = nn(a_h, jnp.concatenate([rhs_h, rhs_l], axis=1))
            back_u2 = wide[:, :128] + wide[:, 128:] + nn(a_l, rhs_h)
            back_u = jnp.where(mask, back_u2[:QB], back_u2[QB:])
            back_x = back_u * size + dexp[0:1, at] * byp
            carried = jnp.sum(s1 * s0, axis=0, keepdims=True) * jnp.exp(own)
            through = jnp.sum(expand(cols, SG_, p) * (back_u * xp), axis=0, keepdims=True)
            pack_o[4:5, at] = pack_o[4:5, at] + through
            pack_o[5:6, at] = pack_o[5:6, at] + carried * own
            pack_o[6:7, at] = pack_o[6:7, at] + carried * sig_own
            pack_o[7:8, at] = pack_o[7:8, at] + jnp.sum(byp * xp, axis=0, keepdims=True)
            back_z = back_x * gx[:, at]
            for k in range(4):
                pack_o[k : k + 1, at] = pack_o[k : k + 1, at] + jnp.sum(
                    back_z * wx[5 + k : 5 + k + QB, at], axis=0, keepdims=True
                )
        back_inner_t = jnp.where(keep, back_inner_t, 0.0)
        back_b = back_b + nn3(back_inner_t, c_mat)
        back_c = back_c + nn3(back_inner_t.T, b_mat)
        back_zbc = jnp.concatenate([back_b, back_c], axis=1) * gbc[...]
        for k in range(4):
            pack_o[9 + k : 10 + k, 0 : 2 * nst] = pack_o[9 + k : 10 + k, 0 : 2 * nst] + jnp.sum(
                back_zbc * wbc[5 + k : 5 + k + QB, :], axis=0, keepdims=True
            )


    @pl.when(step == 2 * half - 1)
    def _():
        for p in range(heads // 2):
            at = slice(128 * p, 128 * p + 128)
            for kind in range(2):
                even, odd = head_o[2 * p, kind], head_o[2 * p + 1, kind]
                even = even + pltpu.roll(even, HW, 1)
                odd = odd + pltpu.roll(odd, HW, 1)
                both = jnp.sum(jnp.where(mask, even, odd), axis=0, keepdims=True)
                pack_o[5 + kind : 6 + kind, at] = pack_o[5 + kind : 6 + kind, at] + both
        for slots, group, sems, mine in (
            (landed_z, z_peers, (f1_s, f1_r), pack_o),
            (landed_y, y_peers, (f3_s, f3_r), pack_z),
        ):
            copies = []
            for k, to in enumerate(group):
                copies.append(send(mine, slots.at[k], sems[0].at[k], sems[1].at[k], to))
            for copy in copies:
                copy.wait()
            if slots is landed_z:
                for z in range(4):
                    k = lax.rem(my_z + 3 - z, 4)
                    term = jnp.where(z == my_z, pack_o[...], slots[jnp.minimum(k, 2)])
                    total = term if z == 0 else total + term
                pack_z[...] = total
            else:
                for y in range(4):
                    k = lax.rem(my_y + 3 - y, 4)
                    term = jnp.where(y == my_y, pack_z[...], slots[jnp.minimum(k, 2)])
                    total = term if y == 0 else total + term
        part[...] = total[8:16, 0 : 2 * nst]
        copies = []
        for k, to in enumerate(head_peers):
            copies.append(send(part, landed_q.at[head], f2_s.at[k], f2_r.at[k], {"head": to}))
        landed_q[head] = part[...]
        gcx_o[...] = total[0:4]
        gain_o[...] = total[8:9]
        at = lax.broadcasted_iota(jnp.int32, (width, 128), 0)
        to = lax.broadcasted_iota(jnp.int32, (width, 128), 1) * HW
        pick = jnp.where((at >= to) & (at < to + HW), 1.0, 0.0).astype(F32)
        sums = jnp.dot(
            total, pick, precision=lax.Precision.HIGHEST, preferred_element_type=F32
        )[:, :heads]
        heads_o[0:1] = sums[4:5] - jnp.exp(hp[1:2]) * sums[6:7]
        heads_o[1:2] = sums[5:6]
        heads_o[2:3] = sums[7:8]
        for copy in last_copies():
            copy.wait()
        piece_o[0:rows_half] = own_z[my_y] + end_z[0] + end_z[1] + end_z[2]
        piece_o[rows_half : 2 * rows_half] = own_y[my_z] + end_y[0] + end_y[1] + end_y[2]
        for copy in copies:
            copy.wait()
        total2 = landed_q[0]
        for i in range(1, n_head):
            total2 = total2 + landed_q[i]
        gcbc_o[...] = total2[1:5]


def adjoint_call(
    by, x, gx, pre_x, halo_x, bc, gbc, pre_bc, halo_bc, rowv, colv, s0, logs, dexp, gain, decays,
    hp, sum_z, sum_y, count, n_head,
):
    length, width = by.shape
    wide = bc.shape[1]
    nst = wide // 2
    heads = width // HW
    half = length // QB
    rows_half = sum_z.shape[1]
    piece = 2 * rows_half
    both = lambda i: jnp.maximum(half - 1 - i, i - half)
    late = lambda i: jnp.maximum(i - half, 0)
    whole = lambda a: pl.BlockSpec(a.shape, lambda i: (0,) * a.ndim)
    rows = lambda w, f: pl.BlockSpec((QB, w), lambda i: (f(i), 0))
    cube = lambda r, f: pl.BlockSpec((1, r, width), lambda i: (f(i), 0, 0))
    out = lambda *s: jax.ShapeDtypeStruct(s, F32)
    fixed = lambda *s: pl.BlockSpec(s, lambda i: (0,) * len(s))
    dma = pltpu.SemaphoreType.DMA
    return pl.pallas_call(
        adjoint_kernel,
        grid=(2 * half,),
        in_specs=[
            rows(width, both), rows(width, late), rows(width, late), rows(width, late),
            whole(halo_x), rows(wide, both), rows(wide, late), rows(wide, late), whole(halo_bc),
            pl.BlockSpec((128, QB), lambda i: (0, late(i))), rows(128, both),
            cube(nst, late), cube(8, both),
            pl.BlockSpec((1, 8, width), lambda i: (half - 1, 0, 0)),
            whole(dexp), whole(gain), whole(decays), whole(hp),
            whole(sum_z), whole(sum_y),
        ],
        out_specs=[
            fixed(piece, width), fixed(4, width), fixed(4, wide), fixed(3, heads), fixed(1, width),
        ],
        out_shape=[out(piece, width), out(4, width), out(4, wide), out(3, heads), out(1, width)],
        scratch_shapes=[
            pltpu.VMEM((QB + 8, width), F32), pltpu.VMEM((QB + 8, wide), F32),
            pltpu.VMEM((heads, 2, 8, 128), F32), pltpu.VMEM((16, width), F32),
            pltpu.VMEM((half, nst, width), F32), pltpu.VMEM((nst, width), F32),
            pltpu.VMEM((count, 8, width), F32), pltpu.VMEM((count, 8, width), F32),
            pltpu.VMEM((count, 8, width), F32), pltpu.VMEM((count, 8, width), F32),
            pltpu.VMEM((3, rows_half, width), F32), pltpu.VMEM((3, rows_half, width), F32),
            pltpu.VMEM((16, width), F32), pltpu.VMEM((3, 16, width), F32),
            pltpu.VMEM((3, 16, width), F32), pltpu.VMEM((8, wide), F32),
            pltpu.VMEM((n_head, 8, wide), F32),
            dma((4,)), dma((4,)), dma((4,)), dma((4,)),
            dma((count,)), dma((count,)), dma((count,)), dma((count,)),
            dma((3,)), dma((3,)), dma((3,)), dma((3,)), dma((n_head,)), dma((n_head,)),
        ],
        compiler_params=pltpu.CompilerParams(
            collective_id=2, has_side_effects=True, vmem_limit_bytes=LIMIT
        ),
        name="adjoint",
    )(
        by, x, gx, pre_x, halo_x, bc, gbc, pre_bc, halo_bc, rowv, colv, s0, logs, logs,
        dexp, gain, decays, hp, sum_z, sum_y,
    )


def on_device(
    pre_x, pre_bc, gate_z, dt_raw, conv_x, conv_bc, head_params, norm_gain, w_out,
    t_conv_x, t_conv_bc, t_heads, t_gain, t_wout,
):
    count = lax.axis_size("seq")
    width = pre_x.shape[1]
    heads = dt_raw.shape[0]
    channels = width * lax.axis_size("head") * 1.0
    tails = jnp.concatenate([pre_x[-8:], pre_bc[-8:]], axis=1)
    tails = lax.ppermute(tails, "seq", [(i, i + 1) for i in range(count - 1)]).astype(F32)
    halo_x, halo_bc = tails[:, :width], tails[:, width:]
    t_wout_all = lax.all_gather(t_wout.T, "seq", axis=0, tiled=True)
    hpc = jnp.concatenate([head_params, t_heads], axis=0).T
    dexp = jnp.repeat(jnp.stack([head_params[2], t_heads[2]]), HW, axis=1)
    x, dx, gx, bc, dbc, gbc, rowv, colv, st, dst, logs, msg, tile = first_call(
        pre_x, halo_x, pre_bc, halo_bc, dt_raw, conv_x, t_conv_x, conv_bc, t_conv_bc, hpc, count
    )
    start, decays = scan_forward(msg, tile)
    gated, d_gated, s0, sums = second_call(
        x, dx, bc, dbc, rowv, colv, st, dst, logs, start, gate_z, dexp
    )
    back_y, gain_part, sum_z, sum_y = middle_call(
        gated, d_gated, sums, gate_z, w_out, t_wout_all, norm_gain[None], t_gain[None]
    )
    gn_wout, gn_conv_x, gn_conv_bc, gn_heads, gn_gain = adjoint_call(
        back_y, x, gx, pre_x, halo_x, bc, gbc, pre_bc, halo_bc, rowv, colv, s0, logs, dexp,
        gain_part, decays, head_params, sum_z, sum_y, count, lax.axis_size("head"),
    )
    return (gn_conv_x, gn_conv_bc, gn_heads, gn_gain[0], gn_wout.T)


def solution(mesh):
    in_specs = (
        P("seq", "head"), P("seq", None), P("seq", "head"), P("head", "seq"), P(None, "head"),
        P(), P(None, "head"), P("head"), P("head", None), P(None, "head"), P(), P(None, "head"),
        P("head"), P("head", "seq"),
    )
    out_specs = (P(None, "head"), P(), P(None, "head"), P("head"), P("head", "seq"))
    return jax.shard_map(
        on_device, mesh=mesh, in_specs=in_specs, out_specs=out_specs, check_vma=False
    )
```

time: 293 us -> 275 us (0.939)
  waiting for transfers between devices: 22.4 us -> 0.69 us
  Pallas kernels: 222 us -> 235 us
  local copies, waits for them, and re-layouts: 29 us -> 19 us
    unnamed x3 -> x1, waiting for transfers between devices: 22.4 us -> 0.68 us
    pallas_call x5 -> x2, Pallas kernels: 154 us -> 167 us  [the longest x1 104 us: middle_call(): pl.pallas_call(middle_kernel, in_specs=[VMEM] * 8, out_specs=[VMEM] * 4,...]
    all_gather x1 -> x0, local copies, waits for them, and re-layouts: 5.6 us -> none  [on_device(): t_wout_all = lax.all_gather(t_wout, 'seq', axis=1, tiled=True)]
    unnamed x28 -> x34, local copies, waits for them, and re-layouts: 18 us -> 13.5 us
  transfers between devices with their start and end apart: 3 -> 2, of which waited for: 1 -> 0; matrix products, arithmetic and copies ran while one was open for 3% -> 3% of each run, Pallas kernels for 47% -> 25%
where the time goes in v3:
time: 275 us; the launch traced here: 273 us
  Pallas kernels  235 us (85%)
  local copies, waits for them, and re-layouts  19 us (7%)
  between operations  14.1 us (5%)
  starting transfers between devices  3.93 us (1%)
    pallas_call x1, Pallas kernels, middle_call(): pl.pallas_call(middle_kernel, in_specs=[VMEM] * 8, out_specs=[VMEM] * 4,...  104 us
    pallas_call x1, Pallas kernels, adjoint_call(): pl.pallas_call(adjoint_kernel, grid=(2 * half,), in_specs=[rows(width, bo...  62.7 us
    pallas_call x1, Pallas kernels, scan_forward(): pl.pallas_call(scan_forward_kernel, in_specs=[VMEM] * 2, out_specs=[VMEM]...  35.9 us
    pallas_call x1, Pallas kernels, second_call(): pl.pallas_call(second_kernel, grid=(count,), in_specs=[rows(width), rows(...  16.2 us
    pallas_call x1, Pallas kernels, first_call(): pl.pallas_call(first_kernel, grid=(count,), in_specs=[rows(width), whole(...  15.9 us
    unnamed x34, local copies, waits for them, and re-layouts  13.5 us
  transfers between devices with their start and end apart: 2, of which 0 were waited for; matrix products, arithmetic and copies ran while one was open for 3% of the time, Pallas kernels for 25%

profile of v3, /device:TPU:0, one launch (start us, length us, event | category | flops | bytes accessed | tf_op | source)
XLA Modules:
  0.0 273.2 jit_solution(17924625207771782254)
XLA Ops:
  7.2 0.0 all-gather.2.cloned.1.call-start
  7.2 0.7 all-gather.2.cloned.1.call-update
  7.9 0.7 slice.18
  8.6 0.7 slice.19
  9.3 3.9 %collective-permute-start = (bf16[8,896]{1,0:T(8,128)(2,1)S(1)}, bf16[8,896]{1,0:T(8,128)(2,1)S(1)}, u32[]{:S(2)}, u32[]{:S(2)}) collective-permute-start(bf16[8,896]{1,0:T(8,128)(2,1)S(1)} %pad_maximum_fusion), channel_id=1, source_target_pairs={{0,8},{8,16},{16,24},{24,32},{32,40},{40,48},{48,56},{56,64},{64,7... | collective-permute-start | bytes 43016 | tf_op jit(solution)/shard_map/ppermute | solution.py:970
  13.2 0.8 copy.21
  14.0 0.7 slice.22
  14.7 0.8 copy.22
  15.4 0.7 slice.23
  16.1 0.1 maximum_bitcast_fusion.hpc
  16.2 0.1 broadcast_in_dim.9
  16.3 0.1 reshape.13.dexp
  16.4 1.3 broadcast_in_dim.10.gain
  17.6 1.3 broadcast_in_dim.11.tgain
  18.9 0.0 collective-permute-done
  18.9 0.0 copy-start.1
  18.9 1.0 copy-done.1
  19.9 0.0 copy-start.6
  19.9 0.8 copy-done.6
  20.8 0.0 copy-start.8
  20.8 0.7 copy-done.8
  21.5 0.0 copy-start.9
  21.5 0.7 copy-done.9
  22.2 0.0 copy-start.12
  22.2 0.7 copy-done.12
  22.9 0.0 copy-start.13
  22.9 0.7 copy-done.13
  23.6 15.9 %conv_and_states.1 = (f32[1024,640]{1,0:T(8,128)}, f32[1024,640]{1,0:T(8,128)}, f32[1024,640]{1,0:T(8,128)}, f32[1024,256]{1,0:T(8,128)S(1)}, f32[1024,256]{1,0:...) custom-call(bf16[1024,640]{1,0:T(8,128)(2,1)} %pre_x.3, ...), custom_call_target="tpu_custom_call" | custom-call | tf_op jit(solution)/shard_map/conv_and_states/pallas_call | solution.py:191
  39.5 0.0 copy-start
  39.5 35.9 %state_scan_forward.1 = (f32[16,16,640]{2,1,0:T(8,128)S(1)}, f32[16,640]{1,0:T(8,128)S(1)}) custom-call(f32[16,16,640]{2,1,0:T(8,128)S(1)} %get-tuple-element.42.msg, f32[8,128]{1,0:T(8,128)S(1)} %get-tuple-element.43.tile), custom_call_target="tpu_custom_call" | custom-call | tf_op jit(solution)/shard_map/state_scan_forward/pallas_call | solution.py:290
  75.4 0.0 copy-start.3
  75.4 1.2 copy-done.3
  76.6 16.2 %outputs_and_tangents.1 = (f32[1024,640]{1,0:T(8,128)}, f32[1024,640]{1,0:T(8,128)}, f32[8,128,640]{2,1,0:T(8,128)}, f32[2,1024]{1,0:T(2,128)S(1)}) custom-call(f32[1024,640]{1,0:T(8,128)} %get-tuple-element.33.x, f32[1024,640]{1,0:T(8,128)} %get-tuple-element.34.dx, f32[1024,256]{1,0:T(8,128)S(1)} %get-tuple-element.35.bc, f32[1024,256]{1,0:T(8,128)S(1)} %copy-done.3, ...), custom_call_target="tpu_custom_call" | custom-call | tf_op jit(solution)/shard_map/outputs_and_tangents/pallas_call | solution.py:660
  92.8 0.0 copy-done
  92.8 0.0 copy-start.11
  92.8 0.6 copy-done.11
  93.4 0.0 all-gather.2.cloned.1.call-done.tw
  93.4 0.0 copy-start.2
  93.4 0.0 copy-start.10
  93.4 104.1 %probe_and_back.1 = (f32[1024,640]{1,0:T(8,128)}, f32[8,640]{1,0:T(8,128)}, f32[4,80,640]{2,1,0:T(8,128)}, f32[4,80,640]{2,1,0:T(8,128)}) custom-call(f32[1024,640]{1,0:T(8,128)} %get-tuple-element.45.gated, f32[1024,640]{1,0:T(8,128)} %get-tuple-element.46.dgated, f32[2,1024]{1,0:T(2,128)} %copy-done.11, bf16[1024,640]{1,0:T(8,128)(2,1)} %gate_z.3, ...), custom_call_target="tpu_custom_call" | custom-call | tf_op jit(solution)/shard_map/probe_and_back/pallas_call | solution.py:541
  197.5 0.0 copy-done.2
  197.5 0.0 copy-done.10
  197.5 0.0 copy-start.4
  197.5 1.1 copy-done.4
  198.7 0.0 copy-start.5
  198.7 1.1 copy-done.5
  199.8 0.0 copy-start.7
  199.8 0.7 copy-done.7
  200.5 62.7 %adjoint.1 = (f32[160,640]{1,0:T(8,128)S(1)}, f32[4,640]{1,0:T(4,128)S(1)}, f32[4,256]{1,0:T(4,128)S(1)}, f32[3,10]{1,0:T(4,128)S(1)}, f32[1,640]{1,0:T(1,128)S(1)}) custom-call(f32[1024,640]{1,0:T(8,128)} %get-tuple-element.48.by, f32[1024,640]{1,0:T(8,128)} %get-tuple-element.33.x, f32[1024,640]{1,0:T(8,128)} %get-tuple-element.49.gx, ...), custom_call_target="tpu_custom_call" | custom-call | tf_op jit(solution)/shard_map/adjoint/pallas_call | solution.py:921
  263.3 0.6 reduce
  263.9 0.6 copy.27
  264.5 0.6 copy.28
  265.1 0.6 copy.29
  265.6 0.8 copy.30
  (4 shorter events, 0.0 us)
Async XLA Ops:
  7.2 86.3 %all-gather.2.cloned.1.call-start = ((), (), s32[]{:S(2)}) async-start(), calls=%async_computation | async-start | bytes 3481600 | tf_op jit(solution)/shard_map/all_gather | solution.py:972
  9.3 9.6 %collective-permute-start = (bf16[8,896]{1,0:T(8,128)(2,1)S(1)}, bf16[8,896]{1,0:T(8,128)(2,1)S(1)}, u32[]{:S(2)}, u32[]{:S(2)}) collective-permute-start(bf16[8,896]{1,0:T(8,128)(2,1)S(1)} %pad_maximum_fusion), channel_id=1, source_target_pairs={{0,8},{8,16},{16,24},{24,32},{32,40},{40,48},{48,56},{56,64},{64,7... | collective-permute-start | bytes 43016 | tf_op jit(solution)/shard_map/ppermute | solution.py:970
  18.9 1.0 copy-start.1
  19.9 0.8 copy-start.6
  20.8 0.7 copy-start.8
  21.5 0.7 copy-start.9
  22.2 0.7 copy-start.12
  22.9 0.7 copy-start.13
  39.5 53.4 %copy-start = (f32[1024,256]{1,0:T(8,128)}, f32[1024,256]{1,0:T(8,128)S(1)}, u32[]{:S(2)}) copy-start(f32[1024,256]{1,0:T(8,128)S(1)} %get-tuple-element.35.bc) | copy-start | bytes 3145732
  75.4 1.2 copy-start.3
  92.8 0.6 copy-start.11
  93.4 104.1 %copy-start.2 = (bf16[1024,256]{1,0:T(8,128)(2,1)S(1)}, bf16[1024,256]{1,0:T(8,128)(2,1)}, u32[]{:S(2)}) copy-start(bf16[1024,256]{1,0:T(8,128)(2,1)} %pre_bc.3) | copy-start | bytes 1572868
  93.4 104.1 %copy-start.10 = (f32[3,10]{1,0:T(4,128)S(1)}, f32[3,10]{1,0:T(4,128)}, u32[]{:S(2)}) copy-start(f32[3,10]{1,0:T(4,128)} %hp.1) | copy-start | bytes 364
  197.5 1.1 copy-start.4
  198.7 1.1 copy-start.5
  199.8 0.7 copy-start.7
Sparse Core Ops, SparseCore 0:
  10.2 66.0 all-gather.1

commit v4 on v3

v4 whole, which is shorter than its diff:
```python
import jax
import jax.numpy as jnp
from jax import lax
from jax.experimental import pallas as pl
from jax.experimental.pallas import tpu as pltpu
from jax.sharding import PartitionSpec as P

QB = 128
HW = 64
F32 = jnp.float32
BF16 = jnp.bfloat16
MESH = pl.DeviceIdType.MESH
S_, DS_, C_, DC_, CS_, SG_, K_, DK_ = (16 * i for i in range(8))
LIMIT = 56 * 1024 * 1024
SCAN_AT = 4
TURN = (1, 3, 2, 4)


def split(a):
    high = a.astype(BF16)
    return high, (a - high.astype(F32)).astype(BF16)


def nn(a, b):
    return jnp.dot(a, b, preferred_element_type=F32)


def nt(a, b):
    return lax.dot_general(a, b, (((1,), (1,)), ((), ())), preferred_element_type=F32)


def nn3(a, b):
    (ah, al), (bh, bl) = split(a), split(b)
    return nn(ah, bh) + nn(ah, bl) + nn(al, bh)


def nt3(a, b):
    (ah, al), (bh, bl) = split(a), split(b)
    return nt(ah, bh) + nt(ah, bl) + nt(al, bh)


def lane_mask():
    return lax.broadcasted_iota(jnp.int32, (1, 128), 1) < HW


def bcast(cols, at):
    return jnp.broadcast_to(cols[:, at : at + 1], (cols.shape[0], 128))


def expand(cols, base, pair):
    return jnp.where(
        lane_mask(), bcast(cols, base + 2 * pair), bcast(cols, base + 2 * pair + 1)
    )


def expand_all(cols, base, heads):
    return jnp.concatenate([expand(cols, base, p) for p in range(heads // 2)], axis=1)


def load_window(window, halo, block, first):
    @pl.when(first)
    def _():
        window[0:8] = halo[...]

    @pl.when(jnp.logical_not(first))
    def _():
        window[0:8] = window[QB : QB + 8]

    window[8 : QB + 8] = block[...].astype(F32)


def conv_pair(window, weight, t_weight):
    z = jnp.zeros((QB, window.shape[1]), F32)
    dz = jnp.zeros((QB, window.shape[1]), F32)
    for k in range(4):
        rows = window[5 + k : 5 + k + QB, :]
        z = z + weight[k : k + 1, :] * rows
        dz = dz + t_weight[k : k + 1, :] * rows
    sig = jax.nn.sigmoid(z)
    slope = sig * (1.0 + z * (1.0 - sig))
    return z * sig, slope * dz, slope


def greet(peers):
    barrier = pltpu.get_barrier_semaphore()
    for peer in peers:
        pl.semaphore_signal(barrier, inc=1, device_id=peer, device_id_type=MESH)
    pl.semaphore_wait(barrier, len(peers))


def others(axis, count):
    me = lax.axis_index(axis)
    return [lax.rem(me + k, count) for k in range(1, count)]


def link(src, dst, send_sem, recv_sem, device):
    return pltpu.make_async_remote_copy(
        src_ref=src, dst_ref=dst, send_sem=send_sem, recv_sem=recv_sem,
        device_id=device, device_id_type=MESH,
    )


def send(*what):
    copy = link(*what)
    copy.start()
    return copy


VMEM = pl.BlockSpec(memory_space=pltpu.VMEM)


def column_of(row):
    heads = row.shape[1]
    at_i = lax.broadcasted_iota(jnp.int32, (heads, heads), 0)
    at_j = lax.broadcasted_iota(jnp.int32, (heads, heads), 1)
    return jnp.sum(jnp.where(at_i == at_j, row, 0.0), axis=1, keepdims=True)


def forward_kernel(
    pre_x, tail_x, pre_bc, tail_bc, dt, gate_z, cx, tcx, cbc, tcbc, hp, th,
    x_o, gx_o, bc_o, gbc_o, row_o, col_o, log_o, s0_o, gated_o, dgated_o, sums_o, decay_o,
    halo_x_o, halo_bc_o,
    wx, wbc, feat, state, d_state, logs, x_a, dx_a, bc_a, dbc_a, row_a, col_a, st_a, dst_a,
    log_a, y_a, dy_a, tile, got_x, got_bc, msg, landed, tiles, answer, start,
    halo_s, halo_r, tile_s, tile_r, s1_s, s1_r, s2_s, s2_r,
):
    step = pl.program_id(0)
    blocks = st_a.shape[0]
    heads = dt.shape[0]
    width = pre_x.shape[1]
    nst = cbc.shape[1] // 2
    count = landed.shape[0]
    me = lax.axis_index("seq")
    peers = others("seq", count)
    mask = lane_mask()

    def place(block):
        return pl.ds(pl.multiple_of(block * QB, QB), QB)

    def scan_copies():
        copies = []
        for k, to in enumerate(peers):
            at = {"seq": to}
            copies.append(link(tile, tiles.at[me], tile_s.at[k], tile_r.at[k], at))
            copies.append(link(msg.at[to], landed.at[me], s1_s.at[k], s1_r.at[k], at))
        return copies

    def back_copies():
        return [
            link(answer.at[to], start.at[me], s2_s.at[k], s2_r.at[k], {"seq": to})
            for k, to in enumerate(peers)
        ]

    @pl.when(step == 0)
    def _():
        greet([{"seq": to} for to in peers])
        after = {"seq": lax.rem(me + 1, count)}
        tails = [
            send(tail_x, got_x, halo_s.at[0], halo_r.at[0], after),
            send(tail_bc, got_bc, halo_s.at[1], halo_r.at[1], after),
        ]
        state[...] = jnp.zeros_like(state)
        d_state[...] = jnp.zeros_like(d_state)
        logs[...] = jnp.zeros_like(logs)
        feat[...] = jnp.zeros_like(feat)
        tile[...] = jnp.zeros_like(tile)
        for copy in tails:
            copy.wait()
        halo_x_o[...] = jnp.where(me == 0, 0.0, got_x[...].astype(F32)[8:16])
        halo_bc_o[...] = jnp.where(me == 0, 0.0, got_bc[...].astype(F32)[8:16])

    @pl.when(step < blocks)
    def _():
        load_window(wx, halo_x_o, pre_x, step == 0)
        load_window(wbc, halo_bc_o, pre_bc, step == 0)
        z = dt[...] + column_of(hp[0:1, :])
        rate = jnp.exp(column_of(hp[1:2, :]))
        t_bias, t_lrate = column_of(th[0:1, :]), column_of(th[1:2, :])
        size = jnp.maximum(z, 0.0) + jnp.log1p(jnp.exp(-jnp.abs(z)))
        sig = jax.nn.sigmoid(z)
        log_decay = -size * rate
        at_i = lax.broadcasted_iota(jnp.int32, (QB, QB), 1)
        at_j = lax.broadcasted_iota(jnp.int32, (QB, QB), 0)
        upper = jnp.where(at_j <= at_i, 1.0, 0.0).astype(F32)
        exact = dict(precision=lax.Precision.HIGHEST, preferred_element_type=F32)
        cumul = jnp.dot(log_decay, upper, **exact)
        sig_sum = jnp.dot(sig, upper, **exact)
        d_size = sig * t_bias
        d_cumul = cumul * t_lrate - rate * t_bias * sig_sum
        to_end = jnp.exp(cumul[:, QB - 1 : QB] - cumul)
        feat[S_ : S_ + heads] = size
        feat[DS_ : DS_ + heads] = d_size
        feat[C_ : C_ + heads] = cumul
        feat[DC_ : DC_ + heads] = d_cumul
        feat[CS_ : CS_ + heads] = sig_sum
        feat[SG_ : SG_ + heads] = sig
        feat[K_ : K_ + heads] = to_end * size
        feat[DK_ : DK_ + heads] = to_end * (
            d_size + size * (d_cumul[:, QB - 1 : QB] - d_cumul)
        )
        rows = feat[...]
        cols = rows.T
        row_o[...] = rows
        col_o[...] = cols
        row_a[step] = rows
        col_a[step] = cols

        bc, dbc, gbc = conv_pair(wbc, cbc, tcbc)
        bc_o[...] = bc
        gbc_o[...] = gbc
        bc_a[step] = bc
        dbc_a[step] = dbc
        x, dx, gx = conv_pair(wx, cx, tcx)
        x_o[...] = x
        gx_o[...] = gx
        x_a[step] = x
        dx_a[step] = dx

        last = cols[QB - 1 : QB, :]
        tile[0:1, :] = tile[0:1, :] + last
        own = expand_all(last, C_, heads)
        d_own = expand_all(last, DC_, heads)
        log = jnp.concatenate(
            [logs[0:1, :], logs[1:2, :], own, d_own, expand_all(last, CS_, heads)]
            + [jnp.zeros((3, width), F32)],
            axis=0,
        )
        log_o[0] = log
        log_a[step] = log
        logs[0:1, :] = logs[0:1, :] + own
        logs[1:2, :] = logs[1:2, :] + d_own

        st_a[step] = state[...]
        dst_a[step] = d_state[...]
        bt = bc[:, :nst].T
        dbt = dbc[:, :nst].T
        both_h, both_l = split(jnp.concatenate([bt, dbt], axis=1))
        for p in range(heads // 2):
            at = slice(128 * p, 128 * p + 128)
            k_x, dk_x = expand(cols, K_, p), expand(cols, DK_, p)
            ux = k_x * x[:, at]
            dux = k_x * dx[:, at] + dk_x * x[:, at]
            z_h, z_l = split(jnp.concatenate([dux, ux], axis=0))
            d_add = nn(both_h, z_h) + nn(both_h, z_l) + nn(both_l, z_h)
            b_h, b_l, u_h, u_l = both_h[:, :QB], both_l[:, :QB], z_h[QB:], z_l[QB:]
            add = nn(b_h, u_h) + nn(b_h, u_l) + nn(b_l, u_h)
            decay = jnp.exp(own[:, at])
            before = state[:, at]
            d_state[:, at] = decay * (d_state[:, at] + d_own[:, at] * before) + d_add
            state[:, at] = decay * before + add

    @pl.when(step == blocks - 1)
    def _():
        msg[:, 0:8, :] = state[...].reshape(count, 8, width)
        msg[:, 8:16, :] = d_state[...].reshape(count, 8, width)
        for copy in scan_copies():
            copy.start()

    @pl.when(step == blocks + SCAN_AT)
    def _():
        landed[me] = msg[me]
        tiles[me] = tile[...]
        for copy in scan_copies():
            copy.wait()
        total = jnp.zeros((8, width), F32)
        d_total = jnp.zeros((8, width), F32)
        for i in range(count):
            answer[i, 0:8] = total
            answer[i, 8:16] = d_total
            features = tiles[i, 0:1, :]
            decay = jnp.exp(expand_all(features, C_, heads))
            decay_o[i : i + 1, :] = decay
            d_total = decay * (d_total + expand_all(features, DC_, heads) * total)
            d_total = d_total + landed[i, 8:16]
            total = decay * total + landed[i, 0:8]
        for copy in back_copies():
            copy.start()

    @pl.when((step >= blocks) & (step < 2 * blocks))
    def _():
        block = step - blocks
        bc, dbc = bc_a[block], dbc_a[block]
        b_mat, c_mat = bc[:, :nst], bc[:, nst:]
        db_mat, dc_mat = dbc[:, :nst], dbc[:, nst:]
        at_j = lax.broadcasted_iota(jnp.int32, (QB, QB), 1)
        at_i = lax.broadcasted_iota(jnp.int32, (QB, QB), 0)
        keep = at_i >= at_j
        inner = jnp.where(keep, nt3(c_mat, b_mat), 0.0)
        d_inner = jnp.where(
            keep,
            nt3(
                jnp.concatenate([dc_mat, c_mat], axis=1),
                jnp.concatenate([b_mat, db_mat], axis=1),
            ),
            0.0,
        )
        cols = col_a[block]
        rows = row_a[block]
        for p in range(heads // 2):
            at = slice(128 * p, 128 * p + 128)
            xp, dxp = x_a[block, :, at], dx_a[block, :, at]
            size, d_size = expand(cols, S_, p), expand(cols, DS_, p)
            z_h, z_l = split(size * xp)
            dz_h, dz_l = split(size * dxp + d_size * xp)
            mats, d_mats = [], []
            for h in (2 * p, 2 * p + 1):
                c_row = rows[C_ + h : C_ + h + 1, :]
                dc_row = rows[DC_ + h : DC_ + h + 1, :]
                level = jnp.exp(jnp.minimum(bcast(cols, C_ + h) - c_row, 0.0))
                m = inner * level
                mats.append(m)
                d_mats.append(d_inner * level + m * (bcast(cols, DC_ + h) - dc_row))
            a_h, a_l = split(jnp.concatenate(mats, axis=0))
            da_h, da_l = split(jnp.concatenate(d_mats, axis=0))
            zz_h = jnp.concatenate([z_h, dz_h], axis=1)
            big = nn(
                jnp.concatenate([a_h, a_l], axis=1), jnp.concatenate([zz_h, zz_h], axis=0)
            ) + nn(a_h, jnp.concatenate([z_l, dz_l], axis=1))
            small = nn(
                jnp.concatenate([da_h, da_l], axis=1), jnp.concatenate([z_h, z_h], axis=0)
            ) + nn(da_h, z_l)
            y2 = big[:, :128]
            dy2 = big[:, 128:] + small
            skip, d_skip = expand(hp[2:3, :], 0, p), expand(th[2:3, :], 0, p)
            y_a[block, :, at] = jnp.where(mask, y2[:QB], y2[QB:]) + skip * xp
            dy_a[block, :, at] = (
                jnp.where(mask, dy2[:QB], dy2[QB:]) + skip * dxp + d_skip * xp
            )

    @pl.when(step == 2 * blocks)
    def _():
        start[me] = answer[me]
        for copy in back_copies():
            copy.wait()

    @pl.when(step >= 2 * blocks)
    def _():
        block = step - 2 * blocks
        cols = col_a[block]
        c_h, c_l = split(bc_a[block][:, nst:])
        dc_h, dc_l = split(dbc_a[block][:, nst:])
        squares = jnp.zeros((QB, 128), F32)
        crossed = jnp.zeros((QB, 128), F32)
        for p in range(heads // 2):
            at = slice(128 * p, 128 * p + 128)
            reach = jnp.exp(log_a[block, 0:1, at])
            s_in = start[:, 0:8, at].reshape(nst, 128)
            ds_in = start[:, 8:16, at].reshape(nst, 128)
            s0 = st_a[block, :, at] + reach * s_in
            ds0 = dst_a[block, :, at] + reach * (ds_in + log_a[block, 1:2, at] * s_in)
            s0_o[0, :, at] = s0
            s_h, s_l = split(s0)
            ds_h, ds_l = split(ds0)
            big = (
                nn(c_h, jnp.concatenate([s_h, ds_h], axis=1))
                + nn(c_h, jnp.concatenate([s_l, ds_l], axis=1))
                + nn(c_l, jnp.concatenate([s_h, ds_h], axis=1))
            )
            low = nn(dc_h, s_h) + nn(dc_h, s_l) + nn(dc_l, s_h)
            lift = jnp.exp(expand(cols, C_, p))
            add = lift * big[:, :128]
            y = y_a[block, :, at] + add
            dy = (
                dy_a[block, :, at]
                + lift * (big[:, 128:] + low)
                + expand(cols, DC_, p) * add
            )
            gz = gate_z[:, at].astype(F32)
            gate = gz * jax.nn.sigmoid(gz)
            gated = y * gate
            dgated = dy * gate
            gated_o[:, at] = gated
            dgated_o[:, at] = dgated
            squares = squares + gated * gated
            crossed = crossed + 2.0 * gated * dgated
        sums_o[0:1, :] = jnp.sum(squares.T, axis=0, keepdims=True)
        sums_o[1:2, :] = jnp.sum(crossed.T, axis=0, keepdims=True)


def forward_call(pre_x, pre_bc, dt, gate_z, cx, tcx, cbc, tcbc, hp, th, parts):
    length, width = pre_x.shape
    wide = pre_bc.shape[1]
    nst = wide // 2
    heads = dt.shape[0]
    count = length // QB
    first = lambda i: jnp.minimum(i, count - 1)
    last = lambda i: jnp.maximum(i - 2 * count, 0)
    whole = lambda a: pl.BlockSpec(a.shape, lambda i: (0,) * a.ndim)
    fixed = lambda *s: pl.BlockSpec(s, lambda i: (0,) * len(s))
    rows = lambda w, f: pl.BlockSpec((QB, w), lambda i: (f(i), 0))
    cube = lambda r, f: pl.BlockSpec((1, r, width), lambda i: (f(i), 0, 0))
    tail = lambda w: pl.BlockSpec((16, w), lambda i: (length // 16 - 1, 0))
    lanes = lambda r, f: pl.BlockSpec((r, QB), lambda i: (0, f(i)))
    out = lambda *s: jax.ShapeDtypeStruct(s, F32)
    vmem = lambda *s: pltpu.VMEM(s, F32)
    dma = pltpu.SemaphoreType.DMA
    return pl.pallas_call(
        forward_kernel,
        grid=(3 * count,),
        in_specs=[
            rows(width, first), tail(width), rows(wide, first), tail(wide), lanes(heads, first),
            rows(width, last), whole(cx), whole(tcx), whole(cbc), whole(tcbc), whole(hp),
            whole(th),
        ],
        out_specs=[
            rows(width, first), rows(width, first), rows(wide, first), rows(wide, first),
            lanes(128, first), rows(128, first), cube(8, first), cube(nst, last),
            rows(width, last), rows(width, last), lanes(2, last), fixed(parts, width),
            fixed(8, width), fixed(8, wide),
        ],
        out_shape=[
            out(length, width), out(length, width), out(length, wide), out(length, wide),
            out(128, length), out(length, 128), out(count, 8, width), out(count, nst, width),
            out(length, width), out(length, width), out(2, length), out(parts, width),
            out(8, width), out(8, wide),
        ],
        scratch_shapes=[
            vmem(QB + 8, width), vmem(QB + 8, wide), vmem(128, QB), vmem(nst, width),
            vmem(nst, width), vmem(8, width), vmem(count, QB, width), vmem(count, QB, width),
            vmem(count, QB, wide), vmem(count, QB, wide), vmem(count, 128, QB),
            vmem(count, QB, 128), vmem(count, nst, width), vmem(count, nst, width),
            vmem(count, 8, width), vmem(count, QB, width), vmem(count, QB, width),
            vmem(8, 128), pltpu.VMEM((16, width), BF16), pltpu.VMEM((16, wide), BF16),
            vmem(parts, 16, width), vmem(parts, 16, width), vmem(parts, 8, 128),
            vmem(parts, 16, width), vmem(parts, 16, width),
            dma((2,)), dma((2,)), dma((parts,)), dma((parts,)), dma((parts,)), dma((parts,)),
            dma((parts,)), dma((parts,)),
        ],
        compiler_params=pltpu.CompilerParams(
            collective_id=1, has_side_effects=True, vmem_limit_bytes=LIMIT
        ),
        name="forward",
    )(pre_x, pre_x, pre_bc, pre_bc, dt, gate_z, cx, tcx, cbc, tcbc, hp, th)


def middle_kernel(
    gated, dgated, sums, gate_z, w, tw, gain_in, tgain_in,
    by_o, gain_o, sum_z_o, sum_y_o, late_o,
    got, scal, both, part, sib, far_src, far_dst, out_src, out_dst, probe, back, gnw, got_z, got_y,
    mix, mix_got, gains,
    sums_s, sums_r, sib_s, sib_r, far_s, far_r, out_s, out_r, ag_s, ag_r, mix_s, mix_r,
    az_s, az_r, ay_s, ay_r,
):
    length, width = gated.shape
    blocks, _, blk = probe.shape
    groups = width // 128
    channels = width * 8.0
    head = lax.axis_index("head")
    me = lax.axis_index("seq")
    my_y, my_z = me // 4, lax.rem(me, 4)
    mine = head // 2
    core = lax.rem(head, 2)
    right, left, far = (lax.rem(mine + k, 4) for k in (1, 3, 2))
    device = lambda chip, c: {"head": chip * 2 + c}
    to_right, to_left, to_sib = device(right, core), device(left, core), device(mine, 1 - core)
    y_peers = [{"seq": lax.rem(my_y + k, 4) * 4 + my_z} for k in range(1, 4)]
    z_peers = [{"seq": my_y * 4 + lax.rem(my_z + k, 4)} for k in range(1, 4)]
    peers = others("head", 8)
    greet([{"head": to} for to in peers] + y_peers + z_peers)
    copies = []
    for k, to in enumerate(peers):
        copies.append(send(sums, got.at[head], sums_s.at[k], sums_r.at[k], {"head": to}))
    got[head] = sums[...]
    gain_o[...] = jnp.zeros_like(gain_o)
    gains[0:1] = gain_in[...].reshape(1, width)
    gains[1:2] = tgain_in[...].reshape(1, width)
    gain, tgain = gains.at[0:1], gains.at[1:2]
    for copy in copies:
        copy.wait()
    total = got[0]
    for i in range(1, 8):
        total = total + got[i]
    inv = lax.rsqrt(total[0:1] / channels + 1e-05)
    scal[0:1] = inv
    scal[1:2] = -0.5 * inv * inv * inv * total[1:2] / channels

    def column(row, start):
        at = pl.ds(pl.multiple_of(start, 128), 128)
        return jnp.broadcast_to(scal[row : row + 1, at], (128, 128)).T

    def norm(i, carry):
        start = pl.multiple_of(i * 128, 128)
        rows = pl.ds(start, 128)
        inv_c, d_inv_c = column(0, start), column(1, start)
        for g in range(groups):
            at = slice(128 * g, 128 * g + 128)
            gt, dgt = gated[rows, at], dgated[rows, at]
            ga = gain[:, at]
            scaled = gt * inv_c
            normed = scaled * ga
            d_normed = (dgt * inv_c + gt * d_inv_c) * ga + scaled * tgain[:, at]
            both[rows, at] = d_normed.astype(BF16)
            both[rows, width + 128 * g : width + 128 * g + 128] = normed.astype(BF16)
        return carry

    lax.fori_loop(0, length // 128, norm, 0)

    def columns(i):
        return pl.ds(pl.multiple_of(lax.rem(my_y + TURN[i], 4) * blk, 128), blk)

    def compute(i):
        slot, at = i % 2, columns(i)

        res = nn(both[:, 0:width], w[:, at]) + nt(both[:, width:], tw[at, :])
        part[slot] = res.reshape(4, 2, 128, blk)
        return send(part.at[slot, :, 1 - core], sib.at[i], sib_s.at[i], sib_r.at[i], to_sib)

    def pairs(i, copy):
        copy.wait()
        for chip in range(4):
            sib[i, chip] = sib[i, chip] + part[i % 2, chip, core]
        way, near = (to_right, to_left) if i % 2 == 0 else (to_left, to_right)
        near_chip = left if i % 2 == 0 else right
        far_src[i] = sib[i, far].astype(BF16)
        transit = send(far_src.at[i], far_dst.at[i], far_s.at[i], far_r.at[i], way)
        out_src[i, 0] = sib[i, near_chip].astype(BF16)
        direct = send(out_src.at[i, 0], out_dst.at[i, 0], out_s.at[i, 0], out_r.at[i, 0], near)
        return transit, direct

    def through(i, transit):
        transit.wait()
        way, chip = (to_right, right) if i % 2 == 0 else (to_left, left)
        out_src[i, 1] = (sib[i, chip] + far_dst[i].astype(F32)).astype(BF16)
        return send(out_src.at[i, 1], out_dst.at[i, 1], out_s.at[i, 1], out_r.at[i, 1], way)

    def pass_on(i, slot, chip, to):
        ref = probe.at[i, pl.ds(pl.multiple_of(chip * 256 + core * 128, 128), 128), :]
        return send(ref, ref, ag_s.at[i, slot], ag_r.at[i, slot], to)

    def own(i, direct, joined):
        direct.wait()
        joined.wait()
        rows = pl.ds(pl.multiple_of(mine * 256 + core * 128, 128), 128)
        res = sib[i, mine] + out_dst[i, 0].astype(F32) + out_dst[i, 1].astype(F32)
        probe[i, rows, :] = res.astype(BF16)
        go_right = pass_on(i, 0, mine, to_right)
        go_left = pass_on(i, 1, mine, to_left)
        return go_right, go_left, pass_on(i, 2, mine, to_sib)

    def forward(i, go_right, go_left):
        if i % 2 == 0:
            go_right.wait()
            onward = pass_on(i, 3, left, to_right)
            go_left.wait()
        else:
            go_left.wait()
            onward = pass_on(i, 3, right, to_left)
            go_right.wait()
        return onward, pass_on(i, 4, left, to_sib), pass_on(i, 5, right, to_sib)

    def last_hop(i, onward):
        onward.wait()
        return pass_on(i, 6, far, to_sib)

    def back_block(i, waits):
        for copy in waits:
            copy.wait()
        at = columns(i)
        summed = lax.dot_general(
            probe[i], both[:, width:], (((0,), (0,)), ((), ())), preferred_element_type=F32
        ).reshape(4, blk // 4, width)
        half = blk // 8
        sent = []
        if i < 2:
            gnw[i] = summed
        else:
            late_o[i - 2] = summed
        for k in (2, 1, 3) if i < 2 else ():
            z = lax.rem(my_z + k, 4)
            sent.append(
                send(
                    gnw.at[i, z, 0:half, :], got_z.at[i, k - 1],
                    az_s.at[i, k], az_r.at[i, k], z_peers[k - 1],
                )
            )
        if i < 2:
            sent.append(
                send(
                    gnw.at[i, :, half : 2 * half, :], got_y.at[i],
                    ay_s.at[i], ay_r.at[i], y_peers[TURN[i] - 1],
                )
            )

        res = nt(probe[i], w[:, at])
        back[...] = res if i == 0 else back[...] + res
        return sent

    sib0 = compute(0)
    sib1 = compute(1)
    far0, dir0 = pairs(0, sib0)
    sib2 = compute(2)
    far1, dir1 = pairs(1, sib1)
    join0 = through(0, far0)
    sib3 = compute(3)
    far2, dir2 = pairs(2, sib2)
    join1 = through(1, far1)
    ag0 = own(0, dir0, join0)
    far3, dir3 = pairs(3, sib3)
    join2 = through(2, far2)
    ag1 = own(1, dir1, join1)
    fwd0 = forward(0, ag0[0], ag0[1])
    join3 = through(3, far3)
    ag2 = own(2, dir2, join2)
    fwd1 = forward(1, ag1[0], ag1[1])
    end0 = last_hop(0, fwd0[0])
    ag3 = own(3, dir3, join3)
    fwd2 = forward(2, ag2[0], ag2[1])
    end1 = last_hop(1, fwd1[0])
    sent = back_block(0, [ag0[2], fwd0[1], fwd0[2], end0])
    fwd3 = forward(3, ag3[0], ag3[1])
    end2 = last_hop(2, fwd2[0])
    sent = sent + back_block(1, [ag1[2], fwd1[1], fwd1[2], end1])
    end3 = last_hop(3, fwd3[0])
    sent = sent + back_block(2, [ag2[2], fwd2[1], fwd2[2], end2])
    sent = sent + back_block(3, [ag3[2], fwd3[1], fwd3[2], end3])

    def mixing(i, carry):
        start = pl.multiple_of(i * 128, 128)
        rows = pl.ds(start, 128)
        inv_c = column(0, start)
        mixed = jnp.zeros((128, 128), F32)
        for g in range(groups):
            at = slice(128 * g, 128 * g + 128)
            prod = back[rows, at] * gated[rows, at]
            gain_o[:, at] = gain_o[:, at] + fold(prod * inv_c)
            mixed = mixed + prod * gain[:, at]
        mix[pl.ds(i, 1), :] = jnp.sum(mixed.T, axis=0, keepdims=True)
        return carry

    lax.fori_loop(0, length // 128, mixing, 0)
    copies = []
    for k, to in enumerate(peers):
        copies.append(send(mix, mix_got.at[head], mix_s.at[k], mix_r.at[k], {"head": to}))
    mix_got[head] = mix[...]
    for copy in copies:
        copy.wait()
    total = mix_got[0]
    for i in range(1, 8):
        total = total + mix_got[i]
    mix[...] = total / channels

    def finish(i, carry):
        start = pl.multiple_of(i * 128, 128)
        rows = pl.ds(start, 128)
        inv_c = column(0, start)
        mixed_c = jnp.broadcast_to(mix[pl.ds(i, 1), :], (128, 128)).T * (inv_c * inv_c * inv_c)
        for g in range(groups):
            at = slice(128 * g, 128 * g + 128)
            gz = gate_z[rows, at].astype(F32)
            gate = gz * jax.nn.sigmoid(gz)
            by_o[rows, at] = (
                back[rows, at] * gain[:, at] * inv_c - gated[rows, at] * mixed_c
            ) * gate
        return carry

    lax.fori_loop(0, length // 128, finish, 0)
    for copy in sent:
        copy.wait()
    half = blk // 8
    for i in range(2):
        sum_z_o[i] = gnw[i, my_z, 0:half, :] + got_z[i, 0] + got_z[i, 1] + got_z[i, 2]
    sum_y_o[...] = late_o[1, :, half : 2 * half, :] + got_y[0] + got_y[1]


def middle_call(gated, dgated, sums, gate_z, w, tw, gain, tgain):
    length, width = gated.shape
    cols = w.shape[1]
    blk = cols // 4
    half = blk // 8
    out = lambda *s: jax.ShapeDtypeStruct(s, F32)
    dma = pltpu.SemaphoreType.DMA
    return pl.pallas_call(
        middle_kernel,
        in_specs=[VMEM] * 8,
        out_specs=[VMEM] * 5,
        out_shape=[
            out(length, width), out(8, width), out(2, half, width), out(4, half, width),
            out(2, 4, blk // 4, width),
        ],
        scratch_shapes=[
            pltpu.VMEM((8, 2, length), F32),
            pltpu.VMEM((8, length), F32),
            pltpu.VMEM((length, 2 * width), BF16),
            pltpu.VMEM((2, 4, 2, 128, blk), F32),
            pltpu.VMEM((4, 4, 128, blk), F32),
            pltpu.VMEM((4, 128, blk), BF16),
            pltpu.VMEM((4, 128, blk), BF16),
            pltpu.VMEM((4, 2, 128, blk), BF16),
            pltpu.VMEM((4, 2, 128, blk), BF16),
            pltpu.VMEM((4, length, blk), BF16),
            pltpu.VMEM((length, width), F32),
            pltpu.VMEM((2, 4, blk // 4, width), F32),
            pltpu.VMEM((2, 3, half, width), F32),
            pltpu.VMEM((2, 4, half, width), F32),
            pltpu.VMEM((8, 128), F32),
            pltpu.VMEM((8, 8, 128), F32),
            pltpu.VMEM((8, width), F32),
            dma((8,)), dma((8,)), dma((4,)), dma((4,)), dma((4,)), dma((4,)),
            dma((4, 2)), dma((4, 2)), dma((4, 7)), dma((4, 7)), dma((8,)), dma((8,)),
            dma((2, 4)), dma((2, 4)), dma((2,)), dma((2,)),
        ],
        compiler_params=pltpu.CompilerParams(
            collective_id=3, has_side_effects=True, vmem_limit_bytes=61 * 1024 * 1024
        ),
        name="probe_and_back",
    )(gated, dgated, sums, gate_z, w, tw, gain, tgain)


def fold(a):
    return jnp.sum(a.reshape(a.shape[0] // 8, 8, a.shape[1]), axis=0)


def adjoint_kernel(
    by, x, gx, pre_x, halo_x, bc, gbc, pre_bc, halo_bc, rowv, colv, s0_b, log, last_log,
    gain, decays, hp, sum_z, sum_y, late,
    result_o,
    wx, wbc, head_o, pack_o, lam, back_u_a, back_bc_a, state, msg, landed, answer, s_end,
    own_z, own_y, got_z, got_y, end_z, end_y, pack_z, landed_z, landed_y, part, landed_q,
    az_s, az_r, ay_s, ay_r, bz_s, bz_r, by_s, by_r,
    s1_s, s1_r, s2_s, s2_r, f1_s, f1_r, f3_s, f3_r, f2_s, f2_r,
):
    step = pl.program_id(0)
    half = lam.shape[0]
    nst = bc.shape[1] // 2
    width = by.shape[1]
    heads = width // HW
    count, n_head = landed.shape[0], landed_q.shape[0]
    me, head = lax.axis_index("seq"), lax.axis_index("head")
    my_y, my_z = me // 4, lax.rem(me, 4)
    seq_peers, head_peers = others("seq", count), others("head", n_head)
    rows_half = sum_z.shape[1]
    mask = lane_mask()

    y_peers = [{"seq": lax.rem(my_y + k, 4) * 4 + my_z} for k in range(1, 4)]
    z_peers = [{"seq": my_y * 4 + lax.rem(my_z + k, 4)} for k in range(1, 4)]

    def late_copies(part_at):
        copies = []
        for i, k in ((0, 1), (0, 3)) if part_at % 2 == 0 else ((0, 2),):
            i = i + part_at // 2
            copies.append(
                link(
                    late.at[i, lax.rem(my_z + k, 4), 0:rows_half, :], got_z.at[i, k - 1],
                    az_s.at[i, k], az_r.at[i, k], z_peers[k - 1],
                )
            )
        copies.append(
            link(
                late.at[0, part_at, rows_half : 2 * rows_half, :], got_y.at[part_at],
                ay_s.at[part_at], ay_r.at[part_at], y_peers[TURN[2] - 1],
            )
        )
        return copies

    def early_last():
        return [
            link(sum_z.at[i], end_z.at[i], bz_s.at[i], bz_r.at[i], y_peers[TURN[i] - 1])
            for i in range(2)
        ]

    def last_copies():
        copies = [link(own_z, end_z.at[2], bz_s.at[2], bz_r.at[2], y_peers[TURN[2] - 1])]
        for k in (2, 1, 3):
            z = lax.rem(my_z + k, 4)
            copies.append(
                link(own_y.at[z], end_y.at[k - 1], by_s.at[k], by_r.at[k], z_peers[k - 1])
            )
        return copies

    for part_at, when in enumerate((0, 3, half + SCAN_AT + 1, half + SCAN_AT + 2)):

        @pl.when(step == when)
        def _(part_at=part_at):
            if part_at == 0:
                greet([{"seq": to} for to in seq_peers] + [{"head": to} for to in head_peers])
            for copy in late_copies(part_at) + (early_last() if part_at == 3 else []):
                copy.start()

    @pl.when(step == 0)
    def _():
        state[...] = jnp.zeros_like(state)
        head_o[...] = jnp.zeros_like(head_o)
        pack_o[...] = jnp.zeros_like(pack_o)
        pack_o[8:9, :] = jnp.sum(gain[...], axis=0, keepdims=True)

    @pl.when(step < half)
    def _():
        lam[half - 1 - step] = state[...]
        cols = colv[...]
        ct_h, ct_l = split(bc[:, nst:].T)
        for p in range(heads // 2):
            at = slice(128 * p, 128 * p + 128)
            lifted = jnp.exp(expand(cols, C_, p)) * by[:, at]
            l_h, l_l = split(lifted)
            add = nn(ct_h, l_h) + nn(ct_h, l_l) + nn(ct_l, l_h)
            state[:, at] = jnp.exp(log[0, 2:3, at]) * state[:, at] + add

    def scan_copies():
        return [
            link(msg.at[to], landed.at[me], s1_s.at[k], s1_r.at[k], {"seq": to})
            for k, to in enumerate(seq_peers)
        ]

    def back_copies():
        return [
            link(answer.at[to], s_end.at[me], s2_s.at[k], s2_r.at[k], {"seq": to})
            for k, to in enumerate(seq_peers)
        ]

    @pl.when(step == half - 1)
    def _():
        msg[...] = state[...].reshape(count, 8, width)
        for copy in scan_copies():
            copy.start()

    @pl.when(step == half + SCAN_AT)
    def _():
        landed[me] = msg[me]
        for copy in scan_copies():
            copy.wait()
        adjoint = jnp.zeros((8, width), F32)
        for i in range(count - 1, -1, -1):
            answer[i] = adjoint
            adjoint = decays[i : i + 1, :] * adjoint + landed[i]
        for copy in back_copies():
            copy.start()

    @pl.when((step >= half) & (step < 2 * half))
    def _():
        block = step - half
        b_mat, c_mat = bc[:, :nst], bc[:, nst:]
        at_i = lax.broadcasted_iota(jnp.int32, (QB, QB), 1)
        at_j = lax.broadcasted_iota(jnp.int32, (QB, QB), 0)
        keep = at_i >= at_j
        inner_t = jnp.where(keep, nt3(b_mat, c_mat), 0.0)
        cols = colv[...]
        rows = rowv[...]
        back_inner_t = jnp.zeros((QB, QB), F32)
        for p in range(heads // 2):
            at = slice(128 * p, 128 * p + 128)
            byp = by[:, at]
            u = expand(cols, S_, p) * x[:, at]
            y_h, y_l = split(byp)
            u_h, u_l = split(
                jnp.concatenate([jnp.where(mask, u, 0.0), jnp.where(mask, 0.0, u)], axis=0)
            )
            back_mts = nt(
                jnp.concatenate([u_h, u_l], axis=1), jnp.concatenate([y_h, y_h], axis=1)
            ) + nt(u_h, y_l)
            mats = []
            for s in range(2):
                h = 2 * p + s
                c_row = rows[C_ + h : C_ + h + 1, :]
                cs_row = rows[CS_ + h : CS_ + h + 1, :]
                back_mt = back_mts[s * QB : s * QB + QB]
                diff = jnp.minimum(c_row - bcast(cols, C_ + h), 0.0)
                level = jnp.exp(diff)
                back_inner_t = back_inner_t + level * back_mt
                m_t = inner_t * level
                prod = m_t * back_mt
                head_o[h, 0] = head_o[h, 0] + fold(prod * diff)
                head_o[h, 1] = head_o[h, 1] + fold(prod * (cs_row - bcast(cols, CS_ + h)))
                mats.append(m_t)
            a_h, a_l = split(jnp.concatenate(mats, axis=0))
            back_u2 = nn(
                jnp.concatenate([a_h, a_l], axis=1), jnp.concatenate([y_h, y_h], axis=0)
            ) + nn(a_h, y_l)
            back_u_a[block, :, at] = jnp.where(mask, back_u2[:QB], back_u2[QB:])
        back_inner_t = jnp.where(keep, back_inner_t, 0.0)
        back_bc_a[block, :, 0:nst] = nn3(back_inner_t, c_mat)
        back_bc_a[block, :, nst:] = nn3(back_inner_t.T, b_mat)

    @pl.when(step == 2 * half)
    def _():
        s_end[me] = answer[me]
        for copy in back_copies():
            copy.wait()

    @pl.when(step >= 2 * half)
    def _():
        block = step - 2 * half
        load_window(wx, halo_x, pre_x, step == 2 * half)
        load_window(wbc, halo_bc, pre_bc, step == 2 * half)
        b_h, b_l = split(bc[:, :nst])
        c_h, c_l = split(bc[:, nst:])
        cols = colv[...]
        back_b = back_bc_a[block, :, 0:nst]
        back_c = back_bc_a[block, :, nst:]
        for p in range(heads // 2):
            at = slice(128 * p, 128 * p + 128)
            own, sig_own = log[0, 2:3, at], log[0, 4:5, at]
            reach = jnp.exp(last_log[0, 0:1, at] + last_log[0, 2:3, at] - log[0, 0:1, at] - own)
            s1 = lam[block, :, at] + reach * s_end[:, :, at].reshape(nst, 128)
            s0 = s0_b[0, :, at]
            byp, xp = by[:, at], x[:, at]
            size = expand(cols, S_, p)
            c_cols, cs_cols = expand(cols, C_, p), expand(cols, CS_, p)
            left = own - c_cols
            to_end = jnp.exp(left)
            u = size * xp
            lifted = jnp.exp(c_cols) * byp
            s0_h, s0_l = split(s0)
            s1_h, s1_l = split(s1)
            l_h, l_l = split(lifted)
            e_h, e_l = split(to_end * u)
            back_c = back_c + nt(
                jnp.concatenate([l_h, l_l], axis=1), jnp.concatenate([s0_h, s0_h], axis=1)
            ) + nt(l_h, s0_l)
            back_b = back_b + nt(
                jnp.concatenate([e_h, e_l], axis=1), jnp.concatenate([s1_h, s1_h], axis=1)
            ) + nt(e_h, s1_l)
            through_c = lifted * (nn(c_h, s0_h) + nn(c_h, s0_l) + nn(c_l, s0_h))
            from_end = to_end * (nn(b_h, s1_h) + nn(b_h, s1_l) + nn(b_l, s1_h))
            through_b = u * from_end
            back_u = back_u_a[block, :, at] + from_end
            back_x = back_u * size + expand(hp[2:3, :], 0, p) * byp
            carried = jnp.sum(s1 * s0, axis=0, keepdims=True) * jnp.exp(own)
            total = lambda a: jnp.sum(a, axis=0, keepdims=True)
            pack_o[4:5, at] = pack_o[4:5, at] + total(expand(cols, SG_, p) * (back_u * xp))
            pack_o[5:6, at] = (
                pack_o[5:6, at] + carried * own + total(through_c * c_cols + through_b * left)
            )
            pack_o[6:7, at] = (
                pack_o[6:7, at]
                + carried * sig_own
                + total(through_c * cs_cols + through_b * (sig_own - cs_cols))
            )
            pack_o[7:8, at] = pack_o[7:8, at] + total(byp * xp)
            back_z = back_x * gx[:, at]
            for k in range(4):
                pack_o[k : k + 1, at] = pack_o[k : k + 1, at] + total(
                    back_z * wx[5 + k : 5 + k + QB, at]
                )
        back_zbc = jnp.concatenate([back_b, back_c], axis=1) * gbc[...]
        for k in range(4):
            pack_o[9 + k : 10 + k, 0 : 2 * nst] = pack_o[
                9 + k : 10 + k, 0 : 2 * nst
            ] + jnp.sum(back_zbc * wbc[5 + k : 5 + k + QB, :], axis=0, keepdims=True)

    @pl.when(step == 3 * half - 5)
    def _():
        for part_at in range(4):
            for copy in late_copies(part_at):
                copy.wait()
        own_z[...] = late[0, my_z, 0:rows_half, :] + got_z[0, 0] + got_z[0, 1] + got_z[0, 2]
        own_y[...] = sum_y[...] + got_y[...]
        for copy in last_copies():
            copy.start()

    @pl.when(step == 3 * half - 1)
    def _():
        for p in range(heads // 2):
            at = slice(128 * p, 128 * p + 128)
            for kind in range(2):
                even, odd = head_o[2 * p, kind], head_o[2 * p + 1, kind]
                even = even + pltpu.roll(even, HW, 1)
                odd = odd + pltpu.roll(odd, HW, 1)
                both = jnp.sum(jnp.where(mask, even, odd), axis=0, keepdims=True)
                pack_o[5 + kind : 6 + kind, at] = pack_o[5 + kind : 6 + kind, at] + both
        for slots, group, sems, mine in (
            (landed_z, z_peers, (f1_s, f1_r), pack_o),
            (landed_y, y_peers, (f3_s, f3_r), pack_z),
        ):
            copies = []
            for k, to in enumerate(group):
                copies.append(send(mine, slots.at[k], sems[0].at[k], sems[1].at[k], to))
            for copy in copies:
                copy.wait()
            if slots is landed_z:
                for z in range(4):
                    k = lax.rem(my_z + 3 - z, 4)
                    term = jnp.where(z == my_z, pack_o[...], slots[jnp.minimum(k, 2)])
                    total = term if z == 0 else total + term
                pack_z[...] = total
            else:
                for y in range(4):
                    k = lax.rem(my_y + 3 - y, 4)
                    term = jnp.where(y == my_y, pack_z[...], slots[jnp.minimum(k, 2)])
                    total = term if y == 0 else total + term
        part[...] = total[8:16, 0 : 2 * nst]
        copies = []
        for k, to in enumerate(head_peers):
            copies.append(send(part, landed_q.at[head], f2_s.at[k], f2_r.at[k], {"head": to}))
        landed_q[head] = part[...]
        result_o[2 * rows_half : 2 * rows_half + 16] = total
        at = lax.broadcasted_iota(jnp.int32, (width, 128), 0)
        to = lax.broadcasted_iota(jnp.int32, (width, 128), 1) * HW
        pick = jnp.where((at >= to) & (at < to + HW), 1.0, 0.0).astype(F32)
        sums = jnp.dot(
            total, pick, precision=lax.Precision.HIGHEST, preferred_element_type=F32
        )[:, :heads]
        at = 2 * rows_half + 24
        result_o[at : at + 1, 0:heads] = sums[4:5] - jnp.exp(hp[1:2]) * sums[6:7]
        result_o[at + 1 : at + 2, 0:heads] = sums[5:6]
        result_o[at + 2 : at + 3, 0:heads] = sums[7:8]
        for copy in early_last() + last_copies():
            copy.wait()
        total = late[1, my_z, 0:rows_half, :] + got_z[1, 0] + got_z[1, 1] + got_z[1, 2]
        result_o[0:rows_half] = total + end_z[0] + end_z[1] + end_z[2]
        result_o[rows_half : 2 * rows_half] = own_y[my_z] + end_y[0] + end_y[1] + end_y[2]
        for copy in copies:
            copy.wait()
        total2 = landed_q[0]
        for i in range(1, n_head):
            total2 = total2 + landed_q[i]
        result_o[2 * rows_half + 16 : 2 * rows_half + 24, 0 : 2 * nst] = total2


def adjoint_call(
    by, x, gx, pre_x, halo_x, bc, gbc, pre_bc, halo_bc, rowv, colv, s0, logs, gain, decays,
    hp, sum_z, sum_y, late_sums, count, n_head,
):
    length, width = by.shape
    wide = bc.shape[1]
    nst = wide // 2
    heads = width // HW
    half = length // QB
    rows_half = sum_z.shape[1]
    piece = 2 * rows_half
    every = lambda i: jnp.where(i < half, half - 1 - i, lax.rem(i, half))
    mid = lambda i: jnp.where(i < half, 0, lax.rem(i, half))
    late = lambda i: jnp.maximum(i - 2 * half, 0)
    whole = lambda a: pl.BlockSpec(a.shape, lambda i: (0,) * a.ndim)
    rows = lambda w, f: pl.BlockSpec((QB, w), lambda i: (f(i), 0))
    cube = lambda r, f: pl.BlockSpec((1, r, width), lambda i: (f(i), 0, 0))
    out = lambda *s: jax.ShapeDtypeStruct(s, F32)
    fixed = lambda *s: pl.BlockSpec(s, lambda i: (0,) * len(s))
    dma = pltpu.SemaphoreType.DMA
    return pl.pallas_call(
        adjoint_kernel,
        grid=(3 * half,),
        in_specs=[
            rows(width, every), rows(width, mid), rows(width, late), rows(width, late),
            whole(halo_x), rows(wide, every), rows(wide, late), rows(wide, late), whole(halo_bc),
            pl.BlockSpec((128, QB), lambda i: (0, mid(i))), rows(128, every),
            cube(nst, late), cube(8, every),
            pl.BlockSpec((1, 8, width), lambda i: (half - 1, 0, 0)),
            whole(gain), whole(decays), whole(hp),
            whole(sum_z), whole(sum_y), VMEM,
        ],
        out_specs=fixed(256, width),
        out_shape=out(256, width),
        scratch_shapes=[
            pltpu.VMEM((QB + 8, width), F32), pltpu.VMEM((QB + 8, wide), F32),
            pltpu.VMEM((heads, 2, 8, 128), F32), pltpu.VMEM((16, width), F32),
            pltpu.VMEM((half, nst, width), F32), pltpu.VMEM((half, QB, width), F32),
            pltpu.VMEM((half, QB, wide), F32), pltpu.VMEM((nst, width), F32),
            pltpu.VMEM((count, 8, width), F32), pltpu.VMEM((count, 8, width), F32),
            pltpu.VMEM((count, 8, width), F32), pltpu.VMEM((count, 8, width), F32),
            pltpu.VMEM((rows_half, width), F32), pltpu.VMEM((4, rows_half, width), F32),
            pltpu.VMEM((2, 3, rows_half, width), F32), pltpu.VMEM((4, rows_half, width), F32),
            pltpu.VMEM((3, rows_half, width), F32), pltpu.VMEM((3, rows_half, width), F32),
            pltpu.VMEM((16, width), F32), pltpu.VMEM((3, 16, width), F32),
            pltpu.VMEM((3, 16, width), F32), pltpu.VMEM((8, wide), F32),
            pltpu.VMEM((n_head, 8, wide), F32),
            dma((2, 4)), dma((2, 4)), dma((4,)), dma((4,)),
            dma((4,)), dma((4,)), dma((4,)), dma((4,)),
            dma((count,)), dma((count,)), dma((count,)), dma((count,)),
            dma((3,)), dma((3,)), dma((3,)), dma((3,)), dma((n_head,)), dma((n_head,)),
        ],
        compiler_params=pltpu.CompilerParams(
            collective_id=2, has_side_effects=True, vmem_limit_bytes=LIMIT
        ),
        name="adjoint",
    )(
        by, x, gx, pre_x, halo_x, bc, gbc, pre_bc, halo_bc, rowv, colv, s0, logs, logs,
        gain, decays, hp, sum_z, sum_y, late_sums,
    )


def outputs_kernel(result, gcx_o, gcbc_o, heads_o, gain_o, gnw_o):
    piece, heads, wide = gnw_o.shape[0], heads_o.shape[1], gcbc_o.shape[1]
    width = result.shape[1]
    gcx_o[...] = result[piece : piece + 4]
    gain_o[...] = result[piece + 8 : piece + 9].reshape(width)
    gcbc_o[...] = result[piece + 17 : piece + 21, 0:wide]
    heads_o[...] = result[piece + 24 : piece + 27, 0:heads]
    gnw_o[...] = result[0:piece]


def outputs_call(result, piece, bc_shape, heads_shape):
    width = result.shape[1]
    out = lambda *s: jax.ShapeDtypeStruct(s, F32)
    return pl.pallas_call(
        outputs_kernel,
        in_specs=[VMEM],
        out_specs=[VMEM] * 5,
        out_shape=[
            out(4, width), out(*bc_shape), out(*heads_shape), out(width), out(piece, width),
        ],
        name="outputs",
    )(result)


def on_device(
    pre_x, pre_bc, gate_z, dt_raw, conv_x, conv_bc, head_params, norm_gain, w_out,
    t_conv_x, t_conv_bc, t_heads, t_gain, t_wout,
):
    count = lax.axis_size("seq")
    t_wout_all = lax.all_gather(t_wout.T, "seq", axis=0, tiled=True)
    x, gx, bc, gbc, rowv, colv, logs, s0, gated, d_gated, sums, decays, halo_x, halo_bc = forward_call(
        pre_x, pre_bc, dt_raw, gate_z, conv_x, t_conv_x, conv_bc, t_conv_bc, head_params, t_heads,
        count,
    )
    back_y, gain_part, sum_z, sum_y, late_sums = middle_call(
        gated, d_gated, sums, gate_z, w_out, t_wout_all, norm_gain, t_gain
    )
    result = adjoint_call(
        back_y, x, gx, pre_x, halo_x, bc, gbc, pre_bc, halo_bc, rowv, colv, s0, logs,
        gain_part, decays, head_params, sum_z, sum_y, late_sums, count, lax.axis_size("head"),
    )
    gn_conv_x, gn_conv_bc, gn_heads, gn_gain, gn_wout = outputs_call(
        result, t_wout.shape[1], conv_bc.shape, head_params.shape
    )
    return gn_conv_x, gn_conv_bc, gn_heads, gn_gain, gn_wout.T


def solution(mesh):
    in_specs = (
        P("seq", "head"), P("seq", None), P("seq", "head"), P("head", "seq"), P(None, "head"),
        P(), P(None, "head"), P("head"), P("head", None), P(None, "head"), P(), P(None, "head"),
        P("head"), P("head", "seq"),
    )
    out_specs = (P(None, "head"), P(), P(None, "head"), P("head"), P("head", "seq"))
    return jax.shard_map(
        on_device, mesh=mesh, in_specs=in_specs, out_specs=out_specs, check_vma=False
    )
```

time: 275 us -> 231 us (0.84)
  Pallas kernels: 235 us -> 212 us
  local copies, waits for them, and re-layouts: 19 us -> 0 us
  starting transfers between devices: 3.93 us -> 0.04 us
  waiting for transfers between devices: 0.69 us -> 3.94 us
    pallas_call x5 -> x4, Pallas kernels: 235 us -> 212 us  [the longest x1 87.5 us: middle_call(): pl.pallas_call(middle_kernel, in_specs=[VMEM] * 8, out_specs=[VMEM] * 5,...]
    unnamed x34 -> x0, local copies, waits for them, and re-layouts: 13.5 us -> none
    ppermute x1 -> x0, starting transfers between devices: 3.89 us -> none  [on_device(): lax.ppermute(tails, 'seq', [(i, i + 1) for i in range(count - 1)])]
    all_gather x1, waiting for transfers between devices: 0.01 us -> 3.26 us  [on_device(): t_wout_all = lax.all_gather(t_wout.T, 'seq', axis=0, tiled=True)]
    slice x6 -> x0, local copies, waits for them, and re-layouts: 2.77 us -> none  [the longest x2 1.39 us: on_device(): tails = jnp.concatenate([pre_x[-8:], pre_bc[-8:]], axis=1)]
  transfers between devices with their start and end apart: 2 -> 1, of which waited for: 0 -> 1; matrix products, arithmetic and copies ran while one was open for 3% -> 0% of each run, Pallas kernels for 25% -> 25%
where the time goes in v4:
time: 231 us; the launch traced here: 230 us
  Pallas kernels  212 us (92%)
  between operations  14.1 us (6%)
  waiting for transfers between devices  3.94 us (2%)
    pallas_call x1, Pallas kernels, middle_call(): pl.pallas_call(middle_kernel, in_specs=[VMEM] * 8, out_specs=[VMEM] * 5,...  87.5 us
    pallas_call x1, Pallas kernels, adjoint_call(): pl.pallas_call(adjoint_kernel, grid=(3 * half,), in_specs=[rows(width, ev...  65.8 us
    pallas_call x1, Pallas kernels, forward_call(): pl.pallas_call(forward_kernel, grid=(3 * count,), in_specs=[rows(width, f...  56.7 us
  transfers between devices with their start and end apart: 1, of which 1 were waited for; matrix products, arithmetic and copies ran while one was open for 0% of the time, Pallas kernels for 25%

profile of v4, /device:TPU:0, one launch (start us, length us, event | category | flops | bytes accessed | tf_op | source)
XLA Modules:
  0.0 230.0 jit_solution(5350865290903965345)
XLA Ops:
  7.2 0.0 all-gather.2.cloned.1.call-start
  7.2 0.7 all-gather.2.cloned.1.call-update
  7.9 56.7 %forward.1 = (f32[1024,640]{1,0:T(8,128)}, f32[1024,640]{1,0:T(8,128)}, f32[1024,256]{1,0:T(8,128)}, f32[1024,256]{1,0:T(8,128)}, f32[128,1024]{1,0:T(8,128)}, /...) custom-call(bf16[1024,640]{1,0:T(8,128)(2,1)} %pre_x.3, ...), custom_call_target="tpu_custom_call" | custom-call | tf_op jit(solution)/shard_map/forward/pallas_call | solution.py:397
  64.7 3.3 %all-gather.2.cloned.1.call-done.tw = bf16[2560,640]{1,0:T(8,128)(2,1)} async-done(((bf16[160,640]{1,0:T(8,128)(2,1)}), bf16[2560,640]{1,0:T(8,128)(2,1)}) %all-gather.2.cloned.1.call-update) | async-done | bytes 3276816 | tf_op jit(solution)/shard_map/all_gather | solution.py:1100
  67.9 87.5 %probe_and_back.1 = (f32[1024,640]{1,0:T(8,128)}, f32[8,640]{1,0:T(8,128)}, f32[2,80,640]{2,1,0:T(8,128)}, f32[4,80,640]{2,1,0:T(8,128)}, f32[2,4,160,640]{3,2,1,0:T(8,128)}) custom-call(f32[1024,640]{1,0:T(8,128)} %get-tuple-element.29.gated, f32[1024,640]{1,0:T(8,128)} %get-tuple-element.30.dgated, f32[2,1024]{1,0:T(2,128)} %get-tuple-element.31.sums, ...), custom_call_target="tpu_custom_call" | custom-call | tf_op jit(solution)/shard_map/probe_and_back/pallas_call | solution.py:672
  155.5 65.8 %adjoint.1.result = f32[256,640]{1,0:T(8,128)} custom-call(f32[1024,640]{1,0:T(8,128)} %get-tuple-element.32.by, f32[1024,640]{1,0:T(8,128)} %get-tuple-element.33.x, f32[1024,640]{1,0:T(8,128)} %get-tuple-element.34.gx, bf16[1024,640]{1,0:T(8,128)(2,1)} %pre_x.3, f32[8,640]{1,0:T(8,128)} %get-tuple-element.35.halo_x, f32[1024,256]{1,0:T(8,128)} %get-tuple-element.36.bc, ...), custom_call_target="tpu_custom_call" | custom-call | tf_op jit(solution)/shard_map/adjoint/pallas_call | solution.py:1029
  221.3 1.9 outputs.1
Async XLA Ops:
  7.2 60.7 %all-gather.2.cloned.1.call-start = ((), (), s32[]{:S(2)}) async-start(), calls=%async_computation | async-start | bytes 3481600 | tf_op jit(solution)/shard_map/all_gather | solution.py:1100
Sparse Core Ops, SparseCore 0:
  10.2 57.6 all-gather.1

commit v5 on v4

--- a/solution.py
+++ b/solution.py
@@ -117,12 +117,13 @@
 
 
 def forward_kernel(
-    pre_x, tail_x, pre_bc, tail_bc, dt, gate_z, cx, tcx, cbc, tcbc, hp, th,
+    pre_x, tail_x, pre_bc, tail_bc, dt, gate_z, cx, tcx, cbc, tcbc, hp, th, tw_in,
     x_o, gx_o, bc_o, gbc_o, row_o, col_o, log_o, s0_o, gated_o, dgated_o, sums_o, decay_o,
-    halo_x_o, halo_bc_o,
+    halo_x_o, halo_bc_o, tw_o,
     wx, wbc, feat, state, d_state, logs, x_a, dx_a, bc_a, dbc_a, row_a, col_a, st_a, dst_a,
     log_a, y_a, dy_a, tile, got_x, got_bc, msg, landed, tiles, answer, start,
     halo_s, halo_r, tile_s, tile_r, s1_s, s1_r, s2_s, s2_r,
+    own_m, gz_s, gz_r, gy_s, gy_r, hz_s, hz_r, hy_s, hy_r,
 ):
     step = pl.program_id(0)
     blocks = st_a.shape[0]
@@ -134,8 +135,39 @@
     peers = others("seq", count)
     mask = lane_mask()
 
-    def place(block):
-        return pl.ds(pl.multiple_of(block * QB, QB), QB)
+    my_y, my_z = me // 4, lax.rem(me, 4)
+    y_peers = [{"seq": lax.rem(my_y + k, 4) * 4 + my_z} for k in range(1, 4)]
+    z_peers = [{"seq": my_y * 4 + lax.rem(my_z + k, 4)} for k in range(1, 4)]
+    piece = tw_in.shape[0]
+    upper_rows, lower_rows = slice(0, piece // 2), slice(piece // 2, piece)
+
+    def own_copy():
+        return pltpu.make_async_copy(tw_in, tw_o.at[my_y, my_z], own_m.at[0])
+
+    def gather_first():
+        copies = []
+        for k in (2, 1, 3):
+            copies.append(
+                link(
+                    tw_in.at[upper_rows, :], tw_o.at[my_y, my_z, upper_rows, :],
+                    gz_s.at[k], gz_r.at[k], z_peers[k - 1],
+                )
+            )
+            copies.append(
+                link(
+                    tw_in.at[lower_rows, :], tw_o.at[my_y, my_z, lower_rows, :],
+                    gy_s.at[k], gy_r.at[k], y_peers[k - 1],
+                )
+            )
+        return copies
+
+    def gather_second(k):
+        along_y = tw_o.at[my_y, :, upper_rows, :]
+        along_z = tw_o.at[:, my_z, lower_rows, :]
+        return [
+            link(along_y, along_y, hz_s.at[k], hz_r.at[k], y_peers[k - 1]),
+            link(along_z, along_z, hy_s.at[k], hy_r.at[k], z_peers[k - 1]),
+        ]
 
     def scan_copies():
         copies = []
@@ -168,6 +200,28 @@
             copy.wait()
         halo_x_o[...] = jnp.where(me == 0, 0.0, got_x[...].astype(F32)[8:16])
         halo_bc_o[...] = jnp.where(me == 0, 0.0, got_bc[...].astype(F32)[8:16])
+        own_copy().start()
+        for copy in gather_first():
+            copy.start()
+
+    @pl.when(step == 3)
+    def _():
+        own_copy().wait()
+        for copy in gather_first():
+            copy.wait()
+        for copy in gather_second(1) + gather_second(3):
+            copy.start()
+
+    @pl.when(step == blocks + SCAN_AT + 1)
+    def _():
+        for copy in gather_second(2):
+            copy.start()
+
+    @pl.when(step == 3 * blocks - 1)
+    def _():
+        for k in (1, 3, 2):
+            for copy in gather_second(k):
+                copy.wait()
 
     @pl.when(step < blocks)
     def _():
@@ -264,13 +318,15 @@
             copy.wait()
         total = jnp.zeros((8, width), F32)
         d_total = jnp.zeros((8, width), F32)
+        features = tiles[...][:, 0, :]
+        decays = jnp.exp(expand_all(features, C_, heads))
+        d_logs = expand_all(features, DC_, heads)
+        decay_o[...] = decays
         for i in range(count):
             answer[i, 0:8] = total
             answer[i, 8:16] = d_total
-            features = tiles[i, 0:1, :]
-            decay = jnp.exp(expand_all(features, C_, heads))
-            decay_o[i : i + 1, :] = decay
-            d_total = decay * (d_total + expand_all(features, DC_, heads) * total)
+            decay = decays[i : i + 1]
+            d_total = decay * (d_total + d_logs[i : i + 1] * total)
             d_total = d_total + landed[i, 8:16]
             total = decay * total + landed[i, 0:8]
         for copy in back_copies():
@@ -377,7 +433,7 @@
         sums_o[1:2, :] = jnp.sum(crossed.T, axis=0, keepdims=True)
 
 
-def forward_call(pre_x, pre_bc, dt, gate_z, cx, tcx, cbc, tcbc, hp, th, parts):
+def forward_call(pre_x, pre_bc, dt, gate_z, cx, tcx, cbc, tcbc, hp, th, tw, parts):
     length, width = pre_x.shape
     wide = pre_bc.shape[1]
     nst = wide // 2
@@ -400,19 +456,20 @@
         in_specs=[
             rows(width, first), tail(width), rows(wide, first), tail(wide), lanes(heads, first),
             rows(width, last), whole(cx), whole(tcx), whole(cbc), whole(tcbc), whole(hp),
-            whole(th),
+            whole(th), pl.BlockSpec(memory_space=pl.ANY),
         ],
         out_specs=[
             rows(width, first), rows(width, first), rows(wide, first), rows(wide, first),
             lanes(128, first), rows(128, first), cube(8, first), cube(nst, last),
             rows(width, last), rows(width, last), lanes(2, last), fixed(parts, width),
-            fixed(8, width), fixed(8, wide),
+            fixed(8, width), fixed(8, wide), pl.BlockSpec(memory_space=pl.ANY),
         ],
         out_shape=[
             out(length, width), out(length, width), out(length, wide), out(length, wide),
             out(128, length), out(length, 128), out(count, 8, width), out(count, nst, width),
             out(length, width), out(length, width), out(2, length), out(parts, width),
             out(8, width), out(8, wide),
+            jax.ShapeDtypeStruct((4, 4, *tw.shape), BF16),
         ],
         scratch_shapes=[
             vmem(QB + 8, width), vmem(QB + 8, wide), vmem(128, QB), vmem(nst, width),
@@ -424,25 +481,32 @@
             vmem(parts, 16, width), vmem(parts, 16, width), vmem(parts, 8, 128),
             vmem(parts, 16, width), vmem(parts, 16, width),
             dma((2,)), dma((2,)), dma((parts,)), dma((parts,)), dma((parts,)), dma((parts,)),
-            dma((parts,)), dma((parts,)),
+            dma((parts,)), dma((parts,)), dma((1,)), dma((4,)), dma((4,)), dma((4,)), dma((4,)),
+            dma((4,)), dma((4,)), dma((4,)), dma((4,)),
         ],
         compiler_params=pltpu.CompilerParams(
             collective_id=1, has_side_effects=True, vmem_limit_bytes=LIMIT
         ),
         name="forward",
-    )(pre_x, pre_x, pre_bc, pre_bc, dt, gate_z, cx, tcx, cbc, tcbc, hp, th)
+    )(pre_x, pre_x, pre_bc, pre_bc, dt, gate_z, cx, tcx, cbc, tcbc, hp, th, tw)
 
 
 def middle_kernel(
-    gated, dgated, sums, gate_z, w, tw, gain_in, tgain_in,
+    gated, dgated, sums, gate_in, w_in, tw_in, gain_in, tgain_in,
     by_o, gain_o, sum_z_o, sum_y_o, late_o,
     got, scal, both, part, sib, far_src, far_dst, out_src, out_dst, probe, back, gnw, got_z, got_y,
-    mix, mix_got, gains,
+    mix, mix_got, gains, gate_z, w, tw, fetch_m,
     sums_s, sums_r, sib_s, sib_r, far_s, far_r, out_s, out_r, ag_s, ag_r, mix_s, mix_r,
     az_s, az_r, ay_s, ay_r,
 ):
     length, width = gated.shape
     blocks, _, blk = probe.shape
+    fetches = [
+        pltpu.make_async_copy(src, dst, fetch_m.at[i])
+        for i, (src, dst) in enumerate(((w_in, w), (tw_in, tw), (gate_in, gate_z)))
+    ]
+    for copy in fetches:
+        copy.start()
     groups = width // 128
     channels = width * 8.0
     head = lax.axis_index("head")
@@ -585,31 +649,33 @@
         back[...] = res if i == 0 else back[...] + res
         return sent
 
+    fetches[0].wait()
+    fetches[1].wait()
     sib0 = compute(0)
     sib1 = compute(1)
     far0, dir0 = pairs(0, sib0)
     sib2 = compute(2)
     far1, dir1 = pairs(1, sib1)
     join0 = through(0, far0)
-    sib3 = compute(3)
     far2, dir2 = pairs(2, sib2)
     join1 = through(1, far1)
+    sib3 = compute(3)
     ag0 = own(0, dir0, join0)
-    far3, dir3 = pairs(3, sib3)
-    join2 = through(2, far2)
     ag1 = own(1, dir1, join1)
     fwd0 = forward(0, ag0[0], ag0[1])
-    join3 = through(3, far3)
-    ag2 = own(2, dir2, join2)
+    join2 = through(2, far2)
+    far3, dir3 = pairs(3, sib3)
     fwd1 = forward(1, ag1[0], ag1[1])
     end0 = last_hop(0, fwd0[0])
+    join3 = through(3, far3)
+    sent = back_block(0, [ag0[2], fwd0[1], fwd0[2], end0])
+    end1 = last_hop(1, fwd1[0])
+    ag2 = own(2, dir2, join2)
     ag3 = own(3, dir3, join3)
     fwd2 = forward(2, ag2[0], ag2[1])
-    end1 = last_hop(1, fwd1[0])
-    sent = back_block(0, [ag0[2], fwd0[1], fwd0[2], end0])
+    sent = sent + back_block(1, [ag1[2], fwd1[1], fwd1[2], end1])
     fwd3 = forward(3, ag3[0], ag3[1])
     end2 = last_hop(2, fwd2[0])
-    sent = sent + back_block(1, [ag1[2], fwd1[1], fwd1[2], end1])
     end3 = last_hop(3, fwd3[0])
     sent = sent + back_block(2, [ag2[2], fwd2[1], fwd2[2], end2])
     sent = sent + back_block(3, [ag3[2], fwd3[1], fwd3[2], end3])
@@ -653,6 +719,7 @@
             ) * gate
         return carry
 
+    fetches[2].wait()
     lax.fori_loop(0, length // 128, finish, 0)
     for copy in sent:
         copy.wait()
@@ -671,7 +738,7 @@
     dma = pltpu.SemaphoreType.DMA
     return pl.pallas_call(
         middle_kernel,
-        in_specs=[VMEM] * 8,
+        in_specs=[VMEM] * 3 + [pl.BlockSpec(memory_space=pl.ANY)] * 3 + [VMEM] * 2,
         out_specs=[VMEM] * 5,
         out_shape=[
             out(length, width), out(8, width), out(2, half, width), out(4, half, width),
@@ -695,6 +762,8 @@
             pltpu.VMEM((8, 128), F32),
             pltpu.VMEM((8, 8, 128), F32),
             pltpu.VMEM((8, width), F32),
+            pltpu.VMEM(gate_z.shape, BF16), pltpu.VMEM(w.shape, BF16), pltpu.VMEM(tw.shape, BF16),
+            dma((3,)),
             dma((8,)), dma((8,)), dma((4,)), dma((4,)), dma((4,)), dma((4,)),
             dma((4, 2)), dma((4, 2)), dma((4, 7)), dma((4, 7)), dma((8,)), dma((8,)),
             dma((2, 4)), dma((2, 4)), dma((2,)), dma((2,)),
@@ -1097,13 +1166,12 @@
     t_conv_x, t_conv_bc, t_heads, t_gain, t_wout,
 ):
     count = lax.axis_size("seq")
-    t_wout_all = lax.all_gather(t_wout.T, "seq", axis=0, tiled=True)
-    x, gx, bc, gbc, rowv, colv, logs, s0, gated, d_gated, sums, decays, halo_x, halo_bc = forward_call(
+    x, gx, bc, gbc, rowv, colv, logs, s0, gated, d_gated, sums, decays, halo_x, halo_bc, tw = forward_call(
         pre_x, pre_bc, dt_raw, gate_z, conv_x, t_conv_x, conv_bc, t_conv_bc, head_params, t_heads,
-        count,
+        t_wout.T, count,
     )
     back_y, gain_part, sum_z, sum_y, late_sums = middle_call(
-        gated, d_gated, sums, gate_z, w_out, t_wout_all, norm_gain, t_gain
+        gated, d_gated, sums, gate_z, w_out, tw.reshape(-1, w_out.shape[0]), norm_gain, t_gain
     )
     result = adjoint_call(
         back_y, x, gx, pre_x, halo_x, bc, gbc, pre_bc, halo_bc, rowv, colv, s0, logs,

time: 231 us -> 216 us (0.935)
  between operations: 14.1 us -> 0.66 us
  waiting for transfers between devices: 3.94 us -> 0 us
    pallas_call x1, Pallas kernels: 56.7 us -> 66.4 us  [forward_call(): pl.pallas_call(forward_kernel, grid=(3 * count,), in_specs=[rows(width, f...]
    pallas_call x1, Pallas kernels: 87.5 us -> 80.1 us  [middle_call(): pl.pallas_call(middle_kernel, in_specs=[VMEM] * 3 + [pl.BlockSpec(memory_...]
    all_gather x1 -> x0, waiting for transfers between devices: 3.26 us -> none  [on_device(): t_wout_all = lax.all_gather(t_wout.T, 'seq', axis=0, tiled=True)]
  transfers between devices with their start and end apart: 1 -> 0, of which waited for: 1 -> 0; matrix products, arithmetic and copies ran while one was open for 0% -> 0% of each run, Pallas kernels for 25% -> 0%
where the time goes in v5:
time: 216 us; the launch traced here: 214 us
  Pallas kernels  213 us (99%)
    pallas_call x1, Pallas kernels, middle_call(): pl.pallas_call(middle_kernel, in_specs=[VMEM] * 3 + [pl.BlockSpec(memory_...  80.1 us
    pallas_call x1, Pallas kernels, forward_call(): pl.pallas_call(forward_kernel, grid=(3 * count,), in_specs=[rows(width, f...  66.4 us
    pallas_call x1, Pallas kernels, adjoint_call(): pl.pallas_call(adjoint_kernel, grid=(3 * half,), in_specs=[rows(width, ev...  65 us

profile of v5, /device:TPU:0, one launch (start us, length us, event | category | flops | bytes accessed | tf_op | source)
XLA Modules:
  0.0 214.0 jit_solution(9224756592639931197)
XLA Ops:
  0.6 66.4 %forward.1 = (f32[1024,640]{1,0:T(8,128)}, f32[1024,640]{1,0:T(8,128)}, f32[1024,256]{1,0:T(8,128)}, f32[1024,256]{1,0:T(8,128)}, f32[128,1024]{1,0:T(8,128)}, /...) custom-call(bf16[1024,640]{1,0:T(8,128)(2,1)} %pre_x.3, ...), custom_call_target="tpu_custom_call" | custom-call | tf_op jit(solution)/shard_map/forward/pallas_call | solution.py:453
  67.1 80.1 %probe_and_back.1 = (f32[1024,640]{1,0:T(8,128)}, f32[8,640]{1,0:T(8,128)}, f32[2,80,640]{2,1,0:T(8,128)}, f32[4,80,640]{2,1,0:T(8,128)}, f32[2,4,160,640]{3,2,1,0:T(8,128)}) custom-call(f32[1024,640]{1,0:T(8,128)} %get-tuple-element.30.gated, f32[1024,640]{1,0:T(8,128)} %get-tuple-element.31.dgated, f32[2,1024]{1,0:T(2,128)} %get-tuple-element.32.sums, ...), custom_call_target="tpu_custom_call" | custom-call | tf_op jit(solution)/shard_map/probe_and_back/pallas_call | solution.py:739
  147.2 65.0 %adjoint.1.result = f32[256,640]{1,0:T(8,128)} custom-call(f32[1024,640]{1,0:T(8,128)} %get-tuple-element.34.by, f32[1024,640]{1,0:T(8,128)} %get-tuple-element.35.x, f32[1024,640]{1,0:T(8,128)} %get-tuple-element.36.gx, bf16[1024,640]{1,0:T(8,128)(2,1)} %pre_x.3, f32[8,640]{1,0:T(8,128)} %get-tuple-element.37.halo_x, f32[1024,256]{1,0:T(8,128)} %get-tuple-element.38.bc, ...), custom_call_target="tpu_custom_call" | custom-call | tf_op jit(solution)/shard_map/adjoint/pallas_call | solution.py:1098
  212.2 1.9 outputs.1

commit v6 on v5

--- a/solution.py
+++ b/solution.py
@@ -173,8 +173,9 @@
         copies = []
         for k, to in enumerate(peers):
             at = {"seq": to}
-            copies.append(link(tile, tiles.at[me], tile_s.at[k], tile_r.at[k], at))
             copies.append(link(msg.at[to], landed.at[me], s1_s.at[k], s1_r.at[k], at))
+        for k, to in enumerate(peers):
+            copies.append(link(tile, tiles.at[me], tile_s.at[k], tile_r.at[k], {"seq": to}))
         return copies
 
     def back_copies():
@@ -497,7 +498,7 @@
     got, scal, both, part, sib, far_src, far_dst, out_src, out_dst, probe, back, gnw, got_z, got_y,
     mix, mix_got, gains, gate_z, w, tw, fetch_m,
     sums_s, sums_r, sib_s, sib_r, far_s, far_r, out_s, out_r, ag_s, ag_r, mix_s, mix_r,
-    az_s, az_r, ay_s, ay_r,
+    az_s, az_r, ay_s, ay_r, one_s, one_r,
 ):
     length, width = gated.shape
     blocks, _, blk = probe.shape
@@ -569,6 +570,33 @@
         part[slot] = res.reshape(4, 2, 128, blk)
         return send(part.at[slot, :, 1 - core], sib.at[i], sib_s.at[i], sib_r.at[i], to_sib)
 
+    def compute_first():
+        copies = []
+        for n, chip in enumerate((far, left, right, mine)):
+            rows, at = pl.ds(pl.multiple_of(chip * 256, 256), 256), columns(0)
+            res = nn(both[rows, 0:width], w[:, at]) + nt(both[rows, width:], tw[at, :])
+            part[0, chip] = res.reshape(2, 128, blk)
+            copies.append(
+                send(
+                    part.at[0, chip, 1 - core], sib.at[0, chip], one_s.at[n], one_r.at[n], to_sib
+                )
+            )
+        return copies
+
+    def pairs_first(copies):
+        for n, (chip, copy) in enumerate(zip((far, left, right, mine), copies)):
+            copy.wait()
+            sib[0, chip] = sib[0, chip] + part[0, chip, core]
+            if n == 0:
+                far_src[0] = sib[0, far].astype(BF16)
+                transit = send(far_src.at[0], far_dst.at[0], far_s.at[0], far_r.at[0], to_right)
+            elif n == 1:
+                out_src[0, 0] = sib[0, left].astype(BF16)
+                direct = send(
+                    out_src.at[0, 0], out_dst.at[0, 0], out_s.at[0, 0], out_r.at[0, 0], to_left
+                )
+        return transit, direct
+
     def pairs(i, copy):
         copy.wait()
         for chip in range(4):
@@ -616,19 +644,19 @@
         onward.wait()
         return pass_on(i, 6, far, to_sib)
 
+    def weight_part(i):
+        return lax.dot_general(
+            probe[i], both[:, width:], (((0,), (0,)), ((), ())), preferred_element_type=F32
+        ).reshape(4, blk // 4, width)
+
     def back_block(i, waits):
         for copy in waits:
             copy.wait()
         at = columns(i)
-        summed = lax.dot_general(
-            probe[i], both[:, width:], (((0,), (0,)), ((), ())), preferred_element_type=F32
-        ).reshape(4, blk // 4, width)
         half = blk // 8
         sent = []
         if i < 2:
-            gnw[i] = summed
-        else:
-            late_o[i - 2] = summed
+            gnw[i] = weight_part(i)
         for k in (2, 1, 3) if i < 2 else ():
             z = lax.rem(my_z + k, 4)
             sent.append(
@@ -651,9 +679,8 @@
 
     fetches[0].wait()
     fetches[1].wait()
-    sib0 = compute(0)
+    far0, dir0 = pairs_first(compute_first())
     sib1 = compute(1)
-    far0, dir0 = pairs(0, sib0)
     sib2 = compute(2)
     far1, dir1 = pairs(1, sib1)
     join0 = through(0, far0)
@@ -698,6 +725,8 @@
     for k, to in enumerate(peers):
         copies.append(send(mix, mix_got.at[head], mix_s.at[k], mix_r.at[k], {"head": to}))
     mix_got[head] = mix[...]
+    for i in range(2):
+        late_o[i] = weight_part(2 + i)
     for copy in copies:
         copy.wait()
     total = mix_got[0]
@@ -766,7 +795,7 @@
             dma((3,)),
             dma((8,)), dma((8,)), dma((4,)), dma((4,)), dma((4,)), dma((4,)),
             dma((4, 2)), dma((4, 2)), dma((4, 7)), dma((4, 7)), dma((8,)), dma((8,)),
-            dma((2, 4)), dma((2, 4)), dma((2,)), dma((2,)),
+            dma((2, 4)), dma((2, 4)), dma((2,)), dma((2,)), dma((4,)), dma((4,)),
         ],
         compiler_params=pltpu.CompilerParams(
             collective_id=3, has_side_effects=True, vmem_limit_bytes=61 * 1024 * 1024

time: 216 us -> 217 us (level)
  no operation moved by 1% of the time
where the time goes in v6:
time: 217 us; the launch traced here: 216 us
  Pallas kernels  215 us (99%)
    pallas_call x1, Pallas kernels, middle_call(): pl.pallas_call(middle_kernel, in_specs=[VMEM] * 3 + [pl.BlockSpec(memory_...  79.8 us
    pallas_call x1, Pallas kernels, forward_call(): pl.pallas_call(forward_kernel, grid=(3 * count,), in_specs=[rows(width, f...  66.7 us
    pallas_call x1, Pallas kernels, adjoint_call(): pl.pallas_call(adjoint_kernel, grid=(3 * half,), in_specs=[rows(width, ev...  66.6 us

profile of v6, /device:TPU:0, one launch (start us, length us, event | category | flops | bytes accessed | tf_op | source)
XLA Modules:
  0.0 215.5 jit_solution(3080961847528756348)
XLA Ops:
  0.6 66.7 %forward.1 = (f32[1024,640]{1,0:T(8,128)}, f32[1024,640]{1,0:T(8,128)}, f32[1024,256]{1,0:T(8,128)}, f32[1024,256]{1,0:T(8,128)}, f32[128,1024]{1,0:T(8,128)}, /...) custom-call(bf16[1024,640]{1,0:T(8,128)(2,1)} %pre_x.3, ...), custom_call_target="tpu_custom_call" | custom-call | tf_op jit(solution)/shard_map/forward/pallas_call | solution.py:454
  67.3 79.8 %probe_and_back.1 = (f32[1024,640]{1,0:T(8,128)}, f32[8,640]{1,0:T(8,128)}, f32[2,80,640]{2,1,0:T(8,128)}, f32[4,80,640]{2,1,0:T(8,128)}, f32[2,4,160,640]{3,2,1,0:T(8,128)}) custom-call(f32[1024,640]{1,0:T(8,128)} %get-tuple-element.30.gated, f32[1024,640]{1,0:T(8,128)} %get-tuple-element.31.dgated, f32[2,1024]{1,0:T(2,128)} %get-tuple-element.32.sums, ...), custom_call_target="tpu_custom_call" | custom-call | tf_op jit(solution)/shard_map/probe_and_back/pallas_call | solution.py:768
  147.1 66.6 %adjoint.1.result = f32[256,640]{1,0:T(8,128)} custom-call(f32[1024,640]{1,0:T(8,128)} %get-tuple-element.34.by, f32[1024,640]{1,0:T(8,128)} %get-tuple-element.35.x, f32[1024,640]{1,0:T(8,128)} %get-tuple-element.36.gx, bf16[1024,640]{1,0:T(8,128)(2,1)} %pre_x.3, f32[8,640]{1,0:T(8,128)} %get-tuple-element.37.halo_x, f32[1024,256]{1,0:T(8,128)} %get-tuple-element.38.bc, ...), custom_call_target="tpu_custom_call" | custom-call | tf_op jit(solution)/shard_map/adjoint/pallas_call | solution.py:1127
  213.7 1.9 outputs.1

commit v7 on v5

--- a/solution.py
+++ b/solution.py
@@ -210,11 +210,6 @@
         for copy in gather_first():
             copy.wait()
         for copy in gather_second(1) + gather_second(3):
-            copy.start()
-
-    @pl.when(step == blocks + SCAN_AT + 1)
-    def _():
-        for copy in gather_second(2):
             copy.start()
 
     @pl.when(step == 3 * blocks - 1)
@@ -388,6 +383,8 @@
         start[me] = answer[me]
         for copy in back_copies():
             copy.wait()
+        for copy in gather_second(2):
+            copy.start()
 
     @pl.when(step >= 2 * blocks)
     def _():

time: 216 us -> 212 us (0.981)
  Pallas kernels: 213 us -> 210 us
    pallas_call x1, Pallas kernels: 66.4 us -> 64.1 us  [forward_call(): pl.pallas_call(forward_kernel, grid=(3 * count,), in_specs=[rows(width, f...]
where the time goes in v7:
time: 212 us; the launch traced here: 210 us
  Pallas kernels  210 us (99%)
    pallas_call x1, Pallas kernels, middle_call(): pl.pallas_call(middle_kernel, in_specs=[VMEM] * 3 + [pl.BlockSpec(memory_...  78 us
    pallas_call x1, Pallas kernels, adjoint_call(): pl.pallas_call(adjoint_kernel, grid=(3 * half,), in_specs=[rows(width, ev...  65.7 us
    pallas_call x1, Pallas kernels, forward_call(): pl.pallas_call(forward_kernel, grid=(3 * count,), in_specs=[rows(width, f...  64.1 us

profile of v7, /device:TPU:0, one launch (start us, length us, event | category | flops | bytes accessed | tf_op | source)
XLA Modules:
  0.0 210.3 jit_solution(11831029010219111185)
XLA Ops:
  0.6 64.1 %forward.1 = (f32[1024,640]{1,0:T(8,128)}, f32[1024,640]{1,0:T(8,128)}, f32[1024,256]{1,0:T(8,128)}, f32[1024,256]{1,0:T(8,128)}, f32[128,1024]{1,0:T(8,128)}, /...) custom-call(bf16[1024,640]{1,0:T(8,128)(2,1)} %pre_x.3, ...), custom_call_target="tpu_custom_call" | custom-call | tf_op jit(solution)/shard_map/forward/pallas_call | solution.py:450
  64.7 78.0 %probe_and_back.1 = (f32[1024,640]{1,0:T(8,128)}, f32[8,640]{1,0:T(8,128)}, f32[2,80,640]{2,1,0:T(8,128)}, f32[4,80,640]{2,1,0:T(8,128)}, f32[2,4,160,640]{3,2,1,0:T(8,128)}) custom-call(f32[1024,640]{1,0:T(8,128)} %get-tuple-element.30.gated, f32[1024,640]{1,0:T(8,128)} %get-tuple-element.31.dgated, f32[2,1024]{1,0:T(2,128)} %get-tuple-element.32.sums, ...), custom_call_target="tpu_custom_call" | custom-call | tf_op jit(solution)/shard_map/probe_and_back/pallas_call | solution.py:736
  142.7 65.7 %adjoint.1.result = f32[256,640]{1,0:T(8,128)} custom-call(f32[1024,640]{1,0:T(8,128)} %get-tuple-element.34.by, f32[1024,640]{1,0:T(8,128)} %get-tuple-element.35.x, f32[1024,640]{1,0:T(8,128)} %get-tuple-element.36.gx, bf16[1024,640]{1,0:T(8,128)(2,1)} %pre_x.3, f32[8,640]{1,0:T(8,128)} %get-tuple-element.37.halo_x, f32[1024,256]{1,0:T(8,128)} %get-tuple-element.38.bc, ...), custom_call_target="tpu_custom_call" | custom-call | tf_op jit(solution)/shard_map/adjoint/pallas_call | solution.py:1095
  208.4 1.9 outputs.1
